TPU v7x, 32 devices: a whole 2x2x4 slice. The times are simulated.
32 devices in a mesh: dp: 2 (over x), seq: 4 (over z), mp: 4 (over y, core).
Axes of the slice: x: 2, y: 2, z: 4, core: 2. Of those that a mesh axis runs over, the one named last changes fastest.
Arguments:
- inputs: bfloat16 [8, 1024, 1536], P('dp', 'seq', 'mp'), may hold values from -6 to 6
- gain_mix: bfloat16 [1536], P('mp'), may hold values from 0.25 to 1.75
- w_in: bfloat16 [1536, 3, 1536], P(None, None, 'mp'), may hold values from -0.15625 to 0.15625
- kernel: bfloat16 [3, 1536], P(None, 'mp'), may hold values from -3.5 to 3.5
- w_out: bfloat16 [1536, 1536], P('mp'), may hold values from -0.15625 to 0.15625
- gain_ff: bfloat16 [1536], P('mp'), may hold values from 0.25 to 1.75
- w_gate: bfloat16 [1536, 6912], P(None, 'mp'), may hold values from -0.15625 to 0.15625
- w_up: bfloat16 [1536, 6912], P(None, 'mp'), may hold values from -0.15625 to 0.15625
- w_down: bfloat16 [6912, 1536], P('mp'), may hold values from -0.109375 to 0.109375
- cotangent: bfloat16 [8, 1024, 1536], P('dp', 'seq', 'mp'), may hold values from -6 to 6
Outputs:
- block_out: bfloat16 [8, 1024, 1536], P('dp', 'seq', 'mp')
- grad_input: bfloat16 [8, 1024, 1536], P('dp', 'seq', 'mp')
- grad_gain_mix: float32 [1536], P('mp')
- grad_w_in: float32 [1536, 3, 1536], P(('dp', 'seq'), None, 'mp')
- grad_kernel: float32 [3, 1536], P(None, 'mp')
- grad_w_out: float32 [1536, 1536], P('mp', ('dp', 'seq'))
- grad_gain_ff: float32 [1536], P('mp')
- grad_w_gate: float32 [1536, 6912], P(('dp', 'seq'), 'mp')
- grad_w_up: float32 [1536, 6912], P(('dp', 'seq'), 'mp')
- grad_w_down: float32 [6912, 1536], P('mp', ('dp', 'seq'))
All inputs are finite; a program needn't handle non-finite values.
Results may differ from a plain program's by a relative error of at most 0.011.
Values may be sent and summed in bfloat16 or wider, within the bound.
A program may use at most 192 MiB of HBM per device.

v0:
```python
import jax
import jax.numpy as jnp
from jax import lax
from jax.sharding import PartitionSpec as P

EPS = 1e-05


def shifted(array, axis, by):
    count = lax.axis_size(axis)
    pairs = [(i, i + by) for i in range(count) if 0 <= i + by < count]
    return lax.ppermute(array, axis, pairs)


def contract_rows(left, right):
    return lax.dot_general(
        left, right, (((0,), (0,)), ((), ())), preferred_element_type=jnp.float32
    )


def contract_cols(left, right):
    return lax.dot_general(
        left, right, (((1,), (1,)), ((), ())), preferred_element_type=jnp.float32
    )


def on_device(inputs, gain_mix, w_in, kernel, w_out, gain_ff, w_gate, w_up, w_down, cotangent):
    groups, seq_rows, local_width = inputs.shape
    full_width = local_width * lax.axis_size("mp")
    tokens = groups * seq_rows
    x_float = inputs.reshape(tokens, local_width).astype(jnp.float32)
    gain_one = gain_mix.astype(jnp.float32)
    gain_two = gain_ff.astype(jnp.float32)
    taps = kernel.astype(jnp.float32)

    def row_total(values):
        return lax.psum(jnp.sum(values, axis=-1, keepdims=True), "mp")

    def all_features(values):
        return lax.all_gather(values, "mp", axis=1, tiled=True)

    def share_sums(values):
        return lax.psum_scatter(values, "mp", scatter_dimension=1, tiled=True)

    def norm_scale(values):
        return lax.rsqrt(row_total(values * values) / full_width + EPS)

    def norm_back(values, scale, gain_vec, upstream):
        inner = row_total(gain_vec * upstream * values)
        grad_values = scale * gain_vec * upstream - values * scale**3 * inner / full_width
        return (grad_values, jnp.sum(upstream * values * scale, axis=0))

    scale_one = norm_scale(x_float)
    normed_in = all_features((x_float * scale_one * gain_one).astype(jnp.bfloat16))
    proj = jnp.einsum("td,dkc->tkc", normed_in, w_in, preferred_element_type=jnp.float32)
    b_gate = proj[:, 0]
    c_gate = proj[:, 1]
    values_v = proj[:, 2]
    b_times_x = (b_gate * values_v).astype(jnp.bfloat16).reshape(groups, seq_rows, local_width)
    before = shifted(b_times_x[:, seq_rows - 2 :], "seq", 1)
    padded = jnp.concatenate([before, b_times_x], 1).astype(jnp.float32)
    conv = taps[0] * padded[:, :-2] + taps[1] * padded[:, 1:-1] + taps[2] * padded[:, 2:]
    conv = conv.reshape(tokens, local_width)
    mixed = (c_gate * conv).astype(jnp.bfloat16)
    hidden_one = x_float + share_sums(jnp.dot(mixed, w_out, preferred_element_type=jnp.float32))
    scale_two = norm_scale(hidden_one)
    normed_ff = all_features((hidden_one * scale_two * gain_two).astype(jnp.bfloat16))
    gate = jnp.dot(normed_ff, w_gate, preferred_element_type=jnp.float32)
    up_proj = jnp.dot(normed_ff, w_up, preferred_element_type=jnp.float32)
    sigma = jax.nn.sigmoid(gate)
    active = gate * sigma
    hidden = (active * up_proj).astype(jnp.bfloat16)
    ffn_out = share_sums(jnp.dot(hidden, w_down, preferred_element_type=jnp.float32))
    block_out = (hidden_one + ffn_out).astype(jnp.bfloat16).reshape(groups, seq_rows, local_width)
    grad_flat = cotangent.reshape(tokens, local_width)
    grad_full = all_features(grad_flat)
    grad_down = contract_rows(hidden, grad_full)
    grad_hidden = contract_cols(grad_full, w_down)
    grad_gate_act = (grad_hidden * up_proj * sigma * (1.0 + gate * (1.0 - sigma))).astype(
        jnp.bfloat16
    )
    grad_up_act = (grad_hidden * active).astype(jnp.bfloat16)
    grad_gate = contract_rows(normed_ff, grad_gate_act)
    grad_up = contract_rows(normed_ff, grad_up_act)
    grad_normed_ff = share_sums(
        contract_cols(grad_gate_act, w_gate) + contract_cols(grad_up_act, w_up)
    )
    grad_norm_two, grad_gain_two = norm_back(hidden_one, scale_two, gain_two, grad_normed_ff)
    grad_hidden_one = grad_flat.astype(jnp.float32) + grad_norm_two
    grad_out_full = all_features(grad_hidden_one.astype(jnp.bfloat16))
    grad_out = contract_rows(mixed, grad_out_full)
    grad_mixed = contract_cols(grad_out_full, w_out)
    grad_c = grad_mixed * conv
    grad_conv = (grad_mixed * c_gate).astype(jnp.bfloat16).reshape(groups, seq_rows, local_width)
    after = shifted(grad_conv[:, :2], "seq", -1)
    extended = jnp.concatenate([grad_conv, after], 1).astype(jnp.float32)
    grad_bx = taps[2] * extended[:, :-2] + taps[1] * extended[:, 1:-1] + taps[0] * extended[:, 2:]
    grad_bx = grad_bx.reshape(tokens, local_width)
    conv_grad_float = extended[:, :-2]
    grad_taps = jnp.stack(
        [
            jnp.sum(conv_grad_float * padded[:, :-2], axis=(0, 1)),
            jnp.sum(conv_grad_float * padded[:, 1:-1], axis=(0, 1)),
            jnp.sum(conv_grad_float * padded[:, 2:], axis=(0, 1)),
        ]
    )
    grad_proj = jnp.stack([grad_bx * values_v, grad_c, grad_bx * b_gate], 1).astype(jnp.bfloat16)
    grad_in = jnp.einsum("td,tkc->dkc", normed_in, grad_proj, preferred_element_type=jnp.float32)
    grad_normed_in = share_sums(
        jnp.einsum("tkc,dkc->td", grad_proj, w_in, preferred_element_type=jnp.float32)
    )
    grad_norm_one, grad_gain_one = norm_back(x_float, scale_one, gain_one, grad_normed_in)
    grad_input = (
        (grad_hidden_one + grad_norm_one)
        .astype(jnp.bfloat16)
        .reshape(groups, seq_rows, local_width)
    )
    small_sums = lax.psum((grad_gain_one, grad_taps, grad_gain_two), ("dp", "seq"))
    by_row = (
        lax.psum_scatter(grad_in, ("dp", "seq"), scatter_dimension=0, tiled=True),
        lax.psum_scatter(grad_gate, ("dp", "seq"), scatter_dimension=0, tiled=True),
        lax.psum_scatter(grad_up, ("dp", "seq"), scatter_dimension=0, tiled=True),
    )
    by_col = (
        lax.psum_scatter(grad_out, ("dp", "seq"), scatter_dimension=1, tiled=True),
        lax.psum_scatter(grad_down, ("dp", "seq"), scatter_dimension=1, tiled=True),
    )
    return (
        block_out,
        grad_input,
        small_sums[0],
        by_row[0],
        small_sums[1],
        by_col[0],
        small_sums[2],
        by_row[1],
        by_row[2],
        by_col[1],
    )


def solution(mesh):
    placed = (
        P("dp", "seq", "mp"),
        P("mp"),
        P(None, None, "mp"),
        P(None, "mp"),
        P("mp", None),
        P("mp"),
        P(None, "mp"),
        P(None, "mp"),
        P("mp", None),
        P("dp", "seq", "mp"),
    )
    return jax.shard_map(
        on_device,
        mesh=mesh,
        in_specs=placed,
        out_specs=(
            P("dp", "seq", "mp"),
            P("dp", "seq", "mp"),
            P("mp"),
            P(("dp", "seq"), None, "mp"),
            P(None, "mp"),
            P("mp", ("dp", "seq")),
            P("mp"),
            P(("dp", "seq"), "mp"),
            P(("dp", "seq"), "mp"),
            P("mp", ("dp", "seq")),
        ),
        check_vma=False,
    )
```

profile of v0, /device:TPU:0, one launch (start us, length us, event | category | flops | bytes accessed | tf_op | source)
XLA Modules:
  0.0 1247.9 jit_solution(2513081856668947589)
XLA Ops:
  9.6 8.4 psum.49
  21.5 28.9 %all-gather.5.cloned.1.call-done = bf16[1024,1536]{1,0:T(8,128)(2,1)} async-done(((bf16[1024,384]{1,0:T(8,128)(2,1)}), bf16[1024,1536]{1,0:T(8,128)(2,1)}) %all-gather.5.cloned.1.call-update) | async-done | bytes 3145744 | tf_op jit(solution)/shard_map/all_gather | solution.py:40
  70.0 58.6 %reduce-scatter.10.cloned.1.call-done = f32[1024,384]{1,0:T(8,128)} async-done(((f32[1024,1536]{1,0:T(8,128)}), f32[1024,384]{1,0:T(8,128)}) %reduce-scatter.10.cloned.1.call-update) | async-done | bytes 1572880 | tf_op jit(solution)/shard_map/reduce_scatter | solution.py:43
  142.2 28.6 %all-gather.7.cloned.1.call-done = bf16[1024,1536]{1,0:T(8,128)(2,1)} async-done(((bf16[1024,384]{1,0:T(8,128)(2,1)}), bf16[1024,1536]{1,0:T(8,128)(2,1)}) %all-gather.7.cloned.1.call-update) | async-done | bytes 3145744 | tf_op jit(solution)/shard_map/all_gather | solution.py:40
  170.9 10.9 fusion.27
  181.8 10.3 fusion.26
  192.0 8.9 all-gather.9.cloned.1.call-done
  200.9 15.3 %multiply_convert_fusion = (bf16[1024,1728]{0,1:T(8,128)(2,1)S(1)}, bf16[1024,1728]{0,1:T(8,128)(2,1)S(1)}, bf16[1024,1728]{0,1:T(8,128)(2,1)}) fusion(f32[1024,1728]{0,1:T(8,128)} %fusion.26, f32[1024,1728]{0,1:T(8,128)} %fusion.27, bf16[1024,1536]{1,0:T(8,128)(2,1)} %all-gather.9.cloned.1.call-done, bf16[1728,1536]{1,0:T(8,128)(2,1)} %param.18), kind=kOutput, calls=%fused_computation | convolution fusion | flops 5462360064 | bytes 33226752 | tf_op jit(solution)/shard_map/dot_general | solution.py:22
  216.2 10.3 fusion.29
  226.5 10.3 convolution_add_fusion
  236.9 10.9 fusion.28
  247.8 47.5 %reduce-scatter.14.cloned.1.call-done = f32[1024,384]{1,0:T(8,128)} async-done(((f32[1024,1536]{1,0:T(8,128)}), f32[1024,384]{1,0:T(8,128)}) %reduce-scatter.14.cloned.1.call-update) | async-done | bytes 1572880 | tf_op jit(solution)/shard_map/reduce_scatter | solution.py:43
  304.8 51.4 %reduce-scatter.12.cloned.1.call-done = f32[1024,384]{1,0:T(8,128)} async-done(((f32[1024,1536]{1,0:T(8,128)}), f32[1024,384]{1,0:T(8,128)}) %reduce-scatter.12.cloned.1.call-update) | async-done | bytes 1572880 | tf_op jit(solution)/shard_map/reduce_scatter | solution.py:43
  360.5 28.6 %all-gather.11.cloned.1.call-done = bf16[1024,1536]{1,0:T(8,128)(2,1)} async-done(((bf16[1024,384]{1,0:T(8,128)(2,1)}), bf16[1024,1536]{1,0:T(8,128)(2,1)}) %all-gather.11.cloned.1.call-update) | async-done | bytes 3145744 | tf_op jit(solution)/shard_map/all_gather | solution.py:40
  413.3 10.7 fusion.33
  426.1 9.9 fusion.32
  437.9 10.5 fusion.31
  456.4 9.0 fusion.1
  471.2 39.1 %all-reduce = (f32[384]{0:T(512)}, f32[3,384]{1,0:T(4,128)}, f32[384]{0:T(512)}) all-reduce(f32[384]{0:T(512)S(1)} %get-tuple-element.15, f32[3,384]{1,0:T(4,128)S(1)} %pad_maximum_fusion.3, f32[384]{0:T(512)S(1)} %copy-done.27), channel_id=1, replica_groups=mesh['dp'=2,'seq'=4,'mp'=4] {'dp','seq'}, use_global_device_ids=true, to_apply=%region_13.0 | all-reduce | flops 1920 | bytes 15360 | tf_op jit(solution)/shard_map/psum | solution.py:118
  520.0 139.3 %reduce-scatter.26.cloned.1.call-done = f32[1728,192]{0,1:T(8,128)} async-done(((f32[1728,1536]{0,1:T(8,128)}), f32[1728,192]{0,1:T(8,128)}) %reduce-scatter.26.cloned.1.call-update) | async-done | bytes 1327120 | tf_op jit(solution)/shard_map/reduce_scatter | solution.py:126
  659.3 188.6 %reduce-scatter.24.cloned.1.call-done = f32[192,1728]{1,0:T(8,128)} async-done(((f32[1536,1728]{1,0:T(8,128)}), f32[192,1728]{1,0:T(8,128)}) %reduce-scatter.24.cloned.1.call-update) | async-done | bytes 1327120 | tf_op jit(solution)/shard_map/reduce_scatter | solution.py:122
  847.9 188.7 %reduce-scatter.22.cloned.1.call-done = f32[192,1728]{1,0:T(8,128)} async-done(((f32[1536,1728]{1,0:T(8,128)}), f32[192,1728]{1,0:T(8,128)}) %reduce-scatter.22.cloned.1.call-update) | async-done | bytes 1327120 | tf_op jit(solution)/shard_map/reduce_scatter | solution.py:121
  1036.6 72.0 %reduce-scatter.20.cloned.1.call-done = f32[384,192]{0,1:T(8,128)} async-done(((f32[384,1536]{0,1:T(8,128)}), f32[384,192]{0,1:T(8,128)}) %reduce-scatter.20.cloned.1.call-update) | async-done | bytes 294928 | tf_op jit(solution)/shard_map/reduce_scatter | solution.py:125
  1108.6 132.3 %reduce-scatter.18.cloned.1.call-done = f32[192,3,384]{2,0,1:T(8,128)} async-done(((f32[1536,3,384]{2,0,1:T(8,128)}), f32[192,3,384]{2,0,1:T(8,128)}) %reduce-scatter.18.cloned.1.call-update) | async-done | bytes 884752 | tf_op jit(solution)/shard_map/reduce_scatter | solution.py:120
  (141 shorter events, 104.2 us)
Async XLA Ops:
  7.2 43.2 %copy-start = (bf16[1536,3,384]{2,0,1:T(8,128)(2,1)S(1)}, bf16[1536,3,384]{2,0,1:T(8,128)(2,1)}, u32[]{:S(2)}) copy-start(bf16[1536,3,384]{2,0,1:T(8,128)(2,1)} %param.12) | copy-start | bytes 10616836
  7.2 14.3 %copy-start.31 = (bf16[3,384]{1,0:T(4,128)(2,1)S(1)}, bf16[3,384]{1,0:T(4,128)(2,1)}, u32[]{:S(2)}) copy-start(bf16[3,384]{1,0:T(4,128)(2,1)} %param.13) | copy-start | bytes 6916
  7.2 43.2 %all-gather.5.cloned.1.call-start = ((), (), s32[]{:S(2)}) async-start(), calls=%async_computation.9 | async-start | bytes 3932160 | tf_op jit(solution)/shard_map/all_gather | solution.py:40
  8.1 48.4 %copy-start.20 = (f32[384]{0:T(512)}, f32[384]{0:T(512)S(1)}, u32[]{:S(2)}) copy-start(f32[384]{0:T(512)S(1)} %convert_element_type.68) | copy-start | bytes 4612
  21.5 107.2 %reduce-scatter.10.cloned.1.call-start = ((), (), s32[]{:S(2)}) async-start(), calls=%async_computation.10 | async-start | bytes 7864320 | tf_op jit(solution)/shard_map/reduce_scatter | solution.py:43
  56.7 4.7 collective-permute-start
  69.3 101.5 %all-gather.7.cloned.1.call-start = ((), (), s32[]{:S(2)}) async-start(), calls=%async_computation.11 | async-start | bytes 3932160 | tf_op jit(solution)/shard_map/all_gather | solution.py:40
  141.1 59.8 %all-gather.9.cloned.1.call-start = ((), (), s32[]{:S(2)}) async-start(), calls=%async_computation.13 | async-start | bytes 3932160 | tf_op jit(solution)/shard_map/all_gather | solution.py:40
  141.7 153.6 %reduce-scatter.14.cloned.1.call-start = ((), (), s32[]{:S(2)}) async-start(), calls=%async_computation.14 | async-start | bytes 7864320 | tf_op jit(solution)/shard_map/reduce_scatter | solution.py:43
  170.9 10.9 copy-start.33
  216.2 10.3 copy-start.36
  216.2 10.3 copy-start.9
  236.8 119.3 %reduce-scatter.12.cloned.1.call-start = ((), (), s32[]{:S(2)}) async-start(), calls=%async_computation.12 | async-start | bytes 7864320 | tf_op jit(solution)/shard_map/reduce_scatter | solution.py:43
  247.8 141.3 %all-gather.11.cloned.1.call-start = ((), (), s32[]{:S(2)}) async-start(), calls=%async_computation.15 | async-start | bytes 3932160 | tf_op jit(solution)/shard_map/all_gather | solution.py:40
  360.4 108.7 %reduce-scatter.16.cloned.1.call-start = ((), (), s32[]{:S(2)}) async-start(), calls=%async_computation.16 | async-start | bytes 7864320 | tf_op jit(solution)/shard_map/reduce_scatter | solution.py:43
  394.1 9.8 copy-start.12
  394.1 5.7 collective-permute-start.1
  411.5 247.9 %reduce-scatter.26.cloned.1.call-start = ((), (), s32[]{:S(2)}) async-start(), calls=%async_computation.21 | async-start | bytes 12386304 | tf_op jit(solution)/shard_map/reduce_scatter | solution.py:126
  424.1 423.9 %reduce-scatter.24.cloned.1.call-start = ((), (), s32[]{:S(2)}) async-start(), calls=%async_computation.20 | async-start | bytes 12386304 | tf_op jit(solution)/shard_map/reduce_scatter | solution.py:122
  436.0 600.6 %reduce-scatter.22.cloned.1.call-start = ((), (), s32[]{:S(2)}) async-start(), calls=%async_computation.19 | async-start | bytes 12386304 | tf_op jit(solution)/shard_map/reduce_scatter | solution.py:121
  448.5 660.1 %reduce-scatter.20.cloned.1.call-start = ((), (), s32[]{:S(2)}) async-start(), calls=%async_computation.18 | async-start | bytes 2654208 | tf_op jit(solution)/shard_map/reduce_scatter | solution.py:125
  454.7 786.3 %reduce-scatter.18.cloned.1.call-start = ((), (), s32[]{:S(2)}) async-start(), calls=%async_computation.17 | async-start | bytes 7962624 | tf_op jit(solution)/shard_map/reduce_scatter | solution.py:120
  465.5 50.9 %copy-start.26 = (f32[1024,1]{0,1:T(1,128)S(1)}, f32[1024,1]{0,1:T(1,128)}, u32[]{:S(2)}) copy-start(f32[1024,1]{0,1:T(1,128)} %get-tuple-element.23) | copy-start | bytes 12292
  516.3 724.6 %copy-start.1 = (bf16[1536,3,384]{2,0,1:T(8,128)(2,1)S(1)}, bf16[1536,3,384]{2,0,1:T(8,128)(2,1)}, u32[]{:S(2)}) copy-start(bf16[1536,3,384]{2,0,1:T(8,128)(2,1)} %param.12) | copy-start | bytes 10616836
  (28 other events, 66.3 us)
Sparse Core Ops, SparseCore 0:
  21.6 28.7 all-gather.4
  69.5 59.1 reduce-scatter.9
  141.3 29.5 all-gather.6
  172.4 28.4 all-gather.8
  237.0 58.3 reduce-scatter.13
  297.7 58.3 reduce-scatter.11
  360.5 28.4 all-gather.10
  411.6 57.4 reduce-scatter.15
  473.3 186.0 reduce-scatter.25
  663.4 184.4 reduce-scatter.23
  852.1 184.4 reduce-scatter.21
  1040.6 67.9 reduce-scatter.19
  1112.8 128.0 reduce-scatter.17
where the time goes:
time: 1250 us
  waiting for transfers between devices  983 us (79%)
  matrix products  134 us (11%)
  blocking collectives  66.3 us (5%)
  other arithmetic  29.4 us (2%)
  between operations  14.7 us (1%)
  local copies, waits for them, and re-layouts  14.5 us (1%)
    reduce_scatter x1, waiting for transfers between devices, on_device(): lax.psum_scatter(grad_gate, ('dp', 'seq'), scatter_dimension=0, tiled=True)  189 us
    reduce_scatter x1, waiting for transfers between devices, on_device(): lax.psum_scatter(grad_up, ('dp', 'seq'), scatter_dimension=0, tiled=True)  189 us
    reduce_scatter x4, waiting for transfers between devices, share_sums(): return lax.psum_scatter(values, 'mp', scatter_dimension=1, tiled=True)  161 us
    reduce_scatter x1, waiting for transfers between devices, on_device(): lax.psum_scatter(grad_down, ('dp', 'seq'), scatter_dimension=1, tiled=True)  139 us
    reduce_scatter x1, waiting for transfers between devices, on_device(): lax.psum_scatter(grad_in, ('dp', 'seq'), scatter_dimension=0, tiled=True)  132 us
    all_gather x4, waiting for transfers between devices, all_features(): return lax.all_gather(values, 'mp', axis=1, tiled=True)  95 us
    reduce_scatter x1, waiting for transfers between devices, on_device(): lax.psum_scatter(grad_out, ('dp', 'seq'), scatter_dimension=1, tiled=True)  72 us
    dot_general x4, matrix products, contract_cols(): lax.dot_general(left, right, (((1,), (1,)), ((), ())), preferred_element_...  40.9 us
  transfers between devices with their start and end apart: 15, of which 15 were waited for; matrix products, arithmetic and copies ran while one was open for 7% of the time, Pallas kernels for 0%

commit v1 on v0

--- a/solution.py
+++ b/solution.py
@@ -40,7 +40,14 @@
         return lax.all_gather(values, "mp", axis=1, tiled=True)
 
     def share_sums(values):
-        return lax.psum_scatter(values, "mp", scatter_dimension=1, tiled=True)
+        return lax.psum_scatter(
+            values.astype(jnp.bfloat16), "mp", scatter_dimension=1, tiled=True
+        ).astype(jnp.float32)
+
+    def scattered(values, dim):
+        return lax.psum_scatter(
+            values.astype(jnp.bfloat16), ("dp", "seq"), scatter_dimension=dim, tiled=True
+        ).astype(jnp.float32)
 
     def norm_scale(values):
         return lax.rsqrt(row_total(values * values) / full_width + EPS)
@@ -117,13 +124,13 @@
     )
     small_sums = lax.psum((grad_gain_one, grad_taps, grad_gain_two), ("dp", "seq"))
     by_row = (
-        lax.psum_scatter(grad_in, ("dp", "seq"), scatter_dimension=0, tiled=True),
-        lax.psum_scatter(grad_gate, ("dp", "seq"), scatter_dimension=0, tiled=True),
-        lax.psum_scatter(grad_up, ("dp", "seq"), scatter_dimension=0, tiled=True),
+        scattered(grad_in, 0),
+        scattered(grad_gate, 0),
+        scattered(grad_up, 0),
     )
     by_col = (
-        lax.psum_scatter(grad_out, ("dp", "seq"), scatter_dimension=1, tiled=True),
-        lax.psum_scatter(grad_down, ("dp", "seq"), scatter_dimension=1, tiled=True),
+        scattered(grad_out, 1),
+        scattered(grad_down, 1),
     )
     return (
         block_out,

time: 1250 us -> 884 us (0.71)
  waiting for transfers between devices: 983 us -> 585 us
  local copies, waits for them, and re-layouts: 14.5 us -> 34.9 us
    reduce_scatter x9 -> x5, waiting for transfers between devices: 881 us -> 398 us  [scattered(): lax.psum_scatter(values.astype(jnp.bfloat16), ('dp', 'seq'), scatter_dime...]
    unnamed x13 -> x17, waiting for transfers between devices: 0.72 us -> 115 us
    all_gather x4, waiting for transfers between devices: 95 us -> 66.4 us  [all_features(): return lax.all_gather(values, 'mp', axis=1, tiled=True)]
    unnamed x75 -> x59, local copies, waits for them, and re-layouts: 14.4 us -> 32.8 us
  transfers between devices with their start and end apart: 15 -> 15, of which waited for: 15 -> 13; matrix products, arithmetic and copies ran while one was open for 7% -> 14% of each run, Pallas kernels for 0% -> 0%
where the time goes in v1:
time: 884 us; the launch traced here: 877 us
  waiting for transfers between devices  585 us (66%)
  matrix products  133 us (15%)
  blocking collectives  65.7 us (7%)
  other arithmetic  38.6 us (4%)
  local copies, waits for them, and re-layouts  34.9 us (4%)
  between operations  14.7 us (2%)
    reduce_scatter x5, waiting for transfers between devices, scattered(): lax.psum_scatter(values.astype(jnp.bfloat16), ('dp', 'seq'), scatter_dime...  398 us
    unnamed x17, waiting for transfers between devices  115 us
    all_gather x4, waiting for transfers between devices, all_features(): return lax.all_gather(values, 'mp', axis=1, tiled=True)  66.4 us
    dot_general x4, matrix products, contract_cols(): lax.dot_general(left, right, (((1,), (1,)), ((), ())), preferred_element_...  41 us
    psum x1, blocking collectives, on_device(): lax.psum((grad_gain_one, grad_taps, grad_gain_two), ('dp', 'seq'))  39 us
    dot_general x4, matrix products, contract_rows(): lax.dot_general(left, right, (((0,), (0,)), ((), ())), preferred_element_...  36.2 us
    unnamed x59, local copies, waits for them, and re-layouts  32.8 us
    psum x4, blocking collectives, row_total(): return lax.psum(jnp.sum(values, axis=-1, keepdims=True), 'mp')  26.7 us
  transfers between devices with their start and end apart: 15, of which 13 were waited for; matrix products, arithmetic and copies ran while one was open for 14% of the time, Pallas kernels for 0%

profile of v1, /device:TPU:0, one launch (start us, length us, event | category | flops | bytes accessed | tf_op | source)
XLA Modules:
  0.0 877.1 jit_solution(17644380780598046710)
XLA Ops:
  9.6 8.4 psum.49
  21.5 28.9 %all-gather.5.cloned.1.call-done = bf16[1024,1536]{1,0:T(8,128)(2,1)} async-done(((bf16[1024,384]{1,0:T(8,128)(2,1)}), bf16[1024,1536]{1,0:T(8,128)(2,1)}) %all-gather.5.cloned.1.call-update) | async-done | bytes 3145744 | tf_op jit(solution)/shard_map/all_gather | solution.py:40
  73.6 38.3 %reduce-scatter.28.cloned.1.call-done = bf16[384,1024]{1,0:T(8,128)(2,1)} async-done(((bf16[1536,1024]{1,0:T(8,128)(2,1)}), bf16[384,1024]{1,0:T(8,128)(2,1)}) %reduce-scatter.28.cloned.1.call-update) | async-done | bytes 786448
  125.4 28.6 %all-gather.7.cloned.1.call-done = bf16[1024,1536]{1,0:T(8,128)(2,1)} async-done(((bf16[1024,384]{1,0:T(8,128)(2,1)}), bf16[1024,1536]{1,0:T(8,128)(2,1)}) %all-gather.7.cloned.1.call-update) | async-done | bytes 3145744 | tf_op jit(solution)/shard_map/all_gather | solution.py:40
  154.0 10.9 %fusion.32 = f32[1024,1728]{0,1:T(8,128)} fusion(bf16[1024,1536]{1,0:T(8,128)(2,1)} %all-gather.7.cloned.1.call-done, bf16[1536,1728]{0,1:T(8,128)(2,1)} %param.17), kind=kOutput, calls=%fused_computation.82 | convolution fusion | flops 5435817984 | bytes 15532032 | tf_op jit(solution)/shard_map/dot_general | solution.py:76
  164.9 10.2 %fusion.31 = f32[1024,1728]{0,1:T(8,128)} fusion(bf16[1024,1536]{1,0:T(8,128)(2,1)S(1)} %copy-done.22, bf16[1536,1728]{0,1:T(8,128)(2,1)} %param.16), kind=kOutput, calls=%fused_computation.81 | convolution fusion | flops 5435817984 | bytes 15532032 | tf_op jit(solution)/shard_map/dot_general | solution.py:75
  175.1 8.9 %all-gather.9.cloned.1.call-done = bf16[1024,1536]{1,0:T(8,128)(2,1)} async-done(((bf16[1024,384]{1,0:T(8,128)(2,1)}), bf16[1024,1536]{1,0:T(8,128)(2,1)}) %all-gather.9.cloned.1.call-update) | async-done | bytes 3145744 | tf_op jit(solution)/shard_map/all_gather | solution.py:40
  184.0 15.5 %multiply_convert_fusion = (bf16[1024,1728]{0,1:T(8,128)(2,1)S(1)}, bf16[1024,1728]{0,1:T(8,128)(2,1)S(1)}, bf16[1024,1728]{0,1:T(8,128)(2,1)}) fusion(f32[1024,1728]{0,1:T(8,128)} %fusion.31, f32[1024,1728]{0,1:T(8,128)} %fusion.32, bf16[1024,1536]{1,0:T(8,128)(2,1)} %all-gather.9.cloned.1.call-done, bf16[1728,1536]{1,0:T(8,128)(2,1)} %param.18), kind=kOutput, calls=%fused_computation.3 | convolution fusion | flops 5462360064 | bytes 33226752 | tf_op jit(solution)/shard_map/dot_general | solution.py:22
  199.5 10.3 %fusion.33 = f32[1024,1536]{1,0:T(8,128)S(1)} fusion(bf16[1024,1728]{0,1:T(8,128)(2,1)S(1)} %get-tuple-element.28, bf16[1536,1728]{0,1:T(8,128)(2,1)} %param.16), kind=kOutput, calls=%fused_computation.83 | convolution fusion | flops 5435817984 | bytes 15138816 | tf_op jit(solution)/shard_map/dot_general | solution.py:22
  209.8 10.3 %add_convert_fusion = bf16[1024,1536]{1,0:T(8,128)(2,1)} fusion(f32[1024,1536]{1,0:T(8,128)S(1)} %fusion.33, bf16[1024,1728]{0,1:T(8,128)(2,1)S(1)} %get-tuple-element.27, bf16[1536,1728]{0,1:T(8,128)(2,1)} %param.17), kind=kOutput, calls=%fused_computation.9 | convolution fusion | flops 5438963712 | bytes 18284544 | tf_op jit(solution)/shard_map/dot_general | solution.py:22
  224.7 38.1 %reduce-scatter.32.cloned.1.call-done = bf16[384,1024]{1,0:T(8,128)(2,1)} async-done(((bf16[1536,1024]{1,0:T(8,128)(2,1)}), bf16[384,1024]{1,0:T(8,128)(2,1)}) %reduce-scatter.32.cloned.1.call-update) | async-done | bytes 786448
  277.3 10.2 %convolution_convert_fusion.4 = bf16[1024,1536]{1,0:T(8,128)(2,1)} fusion(bf16[1024,1728]{0,1:T(8,128)(2,1)} %get-tuple-element.29, bf16[1728,1536]{1,0:T(8,128)(2,1)} %param.18), kind=kOutput, calls=%fused_computation.11 | convolution fusion | flops 5437390848 | bytes 11993088 | tf_op jit(solution)/shard_map/dot_general | solution.py:80
  292.3 10.2 %convolution_convert_fusion = bf16[1728,1536]{0,1:T(8,128)(2,1)} fusion(bf16[1024,1728]{0,1:T(8,128)(2,1)} %get-tuple-element.29, bf16[1024,1536]{1,0:T(8,128)(2,1)} %all-gather.9.cloned.1.call-done), kind=kOutput, calls=%fused_computation | convolution fusion | flops 5438472192 | bytes 11993088 | tf_op jit(solution)/shard_map/dot_general | solution.py:16
  302.6 10.4 %convolution_convert_fusion.1 = bf16[1536,1728]{1,0:T(8,128)(2,1)} fusion(bf16[1024,1536]{1,0:T(8,128)(2,1)} %all-gather.7.cloned.1.call-done, bf16[1024,1728]{0,1:T(8,128)(2,1)} %copy-done.23), kind=kOutput, calls=%fused_computation.1 | convolution fusion | flops 5438472192 | bytes 11993088 | tf_op jit(solution)/shard_map/dot_general | solution.py:16
  313.0 10.6 %convolution_convert_fusion.2 = bf16[1536,1728]{1,0:T(8,128)(2,1)} fusion(bf16[1024,1536]{1,0:T(8,128)(2,1)} %all-gather.7.cloned.1.call-done, bf16[1024,1728]{0,1:T(8,128)(2,1)} %copy-done.24), kind=kOutput, calls=%fused_computation.2 | convolution fusion | flops 5438472192 | bytes 11993088 | tf_op jit(solution)/shard_map/dot_general | solution.py:16
  355.6 8.6 convolution_convert_fusion.3
  366.7 91.2 %reduce-scatter.26.cloned.1.call-done = bf16[1728,192]{0,1:T(8,128)(2,1)} async-done(((bf16[1728,1536]{0,1:T(8,128)(2,1)}), bf16[1728,192]{0,1:T(8,128)(2,1)}) %reduce-scatter.26.cloned.1.call-update) | async-done | bytes 663568 | tf_op jit(solution)/shard_map/reduce_scatter | solution.py:48
  460.1 107.4 %reduce-scatter.24.cloned.1.call-done = bf16[192,1728]{1,0:T(8,128)(2,1)} async-done(((bf16[1536,1728]{1,0:T(8,128)(2,1)}), bf16[192,1728]{1,0:T(8,128)(2,1)}) %reduce-scatter.24.cloned.1.call-update) | async-done | bytes 663568 | tf_op jit(solution)/shard_map/reduce_scatter | solution.py:48
  569.8 107.6 %reduce-scatter.22.cloned.1.call-done = bf16[192,1728]{1,0:T(8,128)(2,1)} async-done(((bf16[1536,1728]{1,0:T(8,128)(2,1)}), bf16[192,1728]{1,0:T(8,128)(2,1)}) %reduce-scatter.22.cloned.1.call-update) | async-done | bytes 663568 | tf_op jit(solution)/shard_map/reduce_scatter | solution.py:48
  682.3 62.2 %reduce-scatter.20.cloned.1.call-done = bf16[384,192]{0,1:T(8,128)(2,1)} async-done(((bf16[384,1536]{0,1:T(8,128)(2,1)}), bf16[384,192]{0,1:T(8,128)(2,1)}) %reduce-scatter.20.cloned.1.call-update) | async-done | bytes 147472 | tf_op jit(solution)/shard_map/reduce_scatter | solution.py:48
  746.2 37.8 %reduce-scatter.34.cloned.1.call-done = bf16[384,1024]{1,0:T(8,128)(2,1)} async-done(((bf16[1536,1024]{1,0:T(8,128)(2,1)}), bf16[384,1024]{1,0:T(8,128)(2,1)}) %reduce-scatter.34.cloned.1.call-update) | async-done | bytes 786448
  789.0 39.0 %all-reduce = (f32[384]{0:T(512)}, f32[3,384]{1,0:T(4,128)}, f32[384]{0:T(512)}) all-reduce(f32[384]{0:T(512)} %get-tuple-element.15, f32[3,384]{1,0:T(4,128)} %pad_maximum_fusion.3, f32[384]{0:T(512)} %get-tuple-element.13), channel_id=1, replica_groups=mesh['dp'=2,'seq'=4,'mp'=4] {'dp','seq'}, use_global_device_ids=true, to_apply=%region_13.0 | all-reduce | flops 1920 | bytes 15360 | tf_op jit(solution)/shard_map/psum | solution.py:125
  828.0 6.7 psum.52
  838.7 29.5 %reduce-scatter.18.cloned.1.call-done = bf16[192,3,384]{2,0,1:T(8,128)(2,1)} async-done(((bf16[1536,3,384]{2,0,1:T(8,128)(2,1)}), bf16[192,3,384]{2,0,1:T(8,128)(2,1)}) %reduce-scatter.18.cloned.1.call-update) | async-done | bytes 442384 | tf_op jit(solution)/shard_map/reduce_scatter | solution.py:48
  (130 shorter events, 122.8 us)
Async XLA Ops:
  7.2 43.2 %copy-start = (bf16[1536,3,384]{2,0,1:T(8,128)(2,1)S(1)}, bf16[1536,3,384]{2,0,1:T(8,128)(2,1)}, u32[]{:S(2)}) copy-start(bf16[1536,3,384]{2,0,1:T(8,128)(2,1)} %param.12) | copy-start | bytes 10616836
  7.2 14.3 %copy-start.20 = (bf16[3,384]{1,0:T(4,128)(2,1)S(1)}, bf16[3,384]{1,0:T(4,128)(2,1)}, u32[]{:S(2)}) copy-start(bf16[3,384]{1,0:T(4,128)(2,1)} %param.13) | copy-start | bytes 6916
  7.2 43.2 %all-gather.5.cloned.1.call-start = ((), (), s32[]{:S(2)}) async-start(), calls=%async_computation.9 | async-start | bytes 3932160 | tf_op jit(solution)/shard_map/all_gather | solution.py:40
  8.1 48.5 %copy-start.13 = (f32[384]{0:T(512)}, f32[384]{0:T(512)S(1)}, u32[]{:S(2)}) copy-start(f32[384]{0:T(512)S(1)} %convert_element_type.122) | copy-start | bytes 4612
  21.5 90.4 %reduce-scatter.28.cloned.1.call-start = ((), (), s32[]{:S(2)}) async-start(), calls=%async_computation.18 | async-start | bytes 3932160
  56.7 4.7 collective-permute-start
  73.0 81.0 %all-gather.7.cloned.1.call-start = ((), (), s32[]{:S(2)}) async-start(), calls=%async_computation.10 | async-start | bytes 3932160 | tf_op jit(solution)/shard_map/all_gather | solution.py:40
  124.3 59.7 %all-gather.9.cloned.1.call-start = ((), (), s32[]{:S(2)}) async-start(), calls=%async_computation.11 | async-start | bytes 3932160 | tf_op jit(solution)/shard_map/all_gather | solution.py:40
  124.8 138.0 %reduce-scatter.32.cloned.1.call-start = ((), (), s32[]{:S(2)}) async-start(), calls=%async_computation.20 | async-start | bytes 3932160
  154.0 10.9 %copy-start.22 = (bf16[1024,1536]{1,0:T(8,128)(2,1)S(1)}, bf16[1024,1536]{1,0:T(8,128)(2,1)}, u32[]{:S(2)}) copy-start(bf16[1024,1536]{1,0:T(8,128)(2,1)} %all-gather.7.cloned.1.call-done) | copy-start | bytes 9437188
  199.5 10.3 %copy-start.24 = (bf16[1024,1728]{0,1:T(8,128)(2,1)}, bf16[1024,1728]{0,1:T(8,128)(2,1)S(1)}, u32[]{:S(2)}) copy-start(bf16[1024,1728]{0,1:T(8,128)(2,1)S(1)} %get-tuple-element.28) | copy-start | bytes 10616836
  199.5 10.3 %copy-start.23 = (bf16[1024,1728]{0,1:T(8,128)(2,1)}, bf16[1024,1728]{0,1:T(8,128)(2,1)S(1)}, u32[]{:S(2)}) copy-start(bf16[1024,1728]{0,1:T(8,128)(2,1)S(1)} %get-tuple-element.27) | copy-start | bytes 10616836
  224.7 99.1 %all-gather.11.cloned.1.call-start = ((), (), s32[]{:S(2)}) async-start(), calls=%async_computation.12 | async-start | bytes 3932160 | tf_op jit(solution)/shard_map/all_gather | solution.py:40
  277.3 87.0 %reduce-scatter.30.cloned.1.call-start = ((), (), s32[]{:S(2)}) async-start(), calls=%async_computation.19 | async-start | bytes 3932160
  292.3 165.6 %reduce-scatter.26.cloned.1.call-start = ((), (), s32[]{:S(2)}) async-start(), calls=%async_computation.17 | async-start | bytes 6193152 | tf_op jit(solution)/shard_map/reduce_scatter | solution.py:48
  302.6 264.9 %reduce-scatter.24.cloned.1.call-start = ((), (), s32[]{:S(2)}) async-start(), calls=%async_computation.16 | async-start | bytes 6193152 | tf_op jit(solution)/shard_map/reduce_scatter | solution.py:48
  313.0 364.4 %reduce-scatter.22.cloned.1.call-start = ((), (), s32[]{:S(2)}) async-start(), calls=%async_computation.15 | async-start | bytes 6193152 | tf_op jit(solution)/shard_map/reduce_scatter | solution.py:48
  323.7 420.9 %reduce-scatter.20.cloned.1.call-start = ((), (), s32[]{:S(2)}) async-start(), calls=%async_computation.14 | async-start | bytes 1327104 | tf_op jit(solution)/shard_map/reduce_scatter | solution.py:48
  328.8 455.2 %reduce-scatter.34.cloned.1.call-start = ((), (), s32[]{:S(2)}) async-start(), calls=%async_computation.21 | async-start | bytes 3932160
  333.8 10.0 %copy-start.5 = (bf16[1024,384]{1,0:T(8,128)(2,1)}, bf16[1024,384]{1,0:T(8,128)(2,1)S(1)}, u32[]{:S(2)}) copy-start(bf16[1024,384]{1,0:T(8,128)(2,1)S(1)} %get-tuple-element.35) | copy-start | bytes 2359300
  333.8 6.0 copy-start.2
  333.9 5.8 collective-permute-start.1
  355.6 512.6 %reduce-scatter.18.cloned.1.call-start = ((), (), s32[]{:S(2)}) async-start(), calls=%async_computation.13 | async-start | bytes 3981312 | tf_op jit(solution)/shard_map/reduce_scatter | solution.py:48
  569.8 216.5 %copy-start.11 = (f32[1024,1]{0,1:T(1,128)S(1)}, f32[1024,1]{0,1:T(1,128)}, u32[]{:S(2)}) copy-start(f32[1024,1]{0,1:T(1,128)} %copy-done.10) | copy-start | bytes 12292
  (16 other events, 40.0 us)
Sparse Core Ops, SparseCore 0:
  21.6 28.7 all-gather.4
  73.1 38.7 reduce-scatter.27
  124.4 29.5 all-gather.6
  155.5 28.4 all-gather.8
  224.8 37.9 reduce-scatter.31
  277.4 29.5 all-gather.10
  309.6 37.9 reduce-scatter.29
  351.6 106.2 reduce-scatter.25
  461.5 105.9 reduce-scatter.23
  571.4 105.9 reduce-scatter.21
  680.8 63.7 reduce-scatter.19
  746.9 36.9 reduce-scatter.33
  788.0 80.1 reduce-scatter.17

commit v2 on v1

--- a/solution.py
+++ b/solution.py
@@ -1,9 +1,628 @@
+import functools
+
 import jax
 import jax.numpy as jnp
 from jax import lax
+from jax.experimental import pallas as pl
+from jax.experimental.pallas import tpu as pltpu
 from jax.sharding import PartitionSpec as P
 
 EPS = 1e-05
+MESH = pl.DeviceIdType.MESH
+BF = jnp.bfloat16
+F32 = jnp.float32
+ROWS = 32
+ANY = pl.BlockSpec(memory_space=pl.ANY)
+VMEM = pl.BlockSpec(memory_space=pltpu.VMEM)
+
+
+def nn(left, right):
+    return lax.dot_general(left, right, (((1,), (0,)), ((), ())), preferred_element_type=F32)
+
+
+def nt(left, right):
+    return lax.dot_general(left, right, (((1,), (1,)), ((), ())), preferred_element_type=F32)
+
+
+def backward_kernel(
+    dims,
+    hidden_h, gate_h, up_h, a1_h, a2_h, x_h, h1_h, cot_h, bcv_h, before_v,
+    wd_h, wg_h, wu_h, wo_h, wi_h, gains_v, taps_v,
+    gdown_h, ggate_h, gup_h, gout_h, gin_h, gx_h, small_v,
+    lt, r, w0, wg, wu, wo, cotc, h1c, xc, xo, bcv, bxp, dbuf, dcp, dhoc, dh1s, r1s,
+    xs, xr, s_buf, zs, zr, ob,
+    ck, cs, cr, ys, yr, da2f, ck2, cs2, cr2, ys2, yr2, qk2,
+    ins, inr, iys, iyr, gxb, halo_s, halo_r,
+    xs_sem, xr_sem, zs_sem, zr_sem, ob_sem, c_sem, y_sem, f_sem, c2_sem, y2_sem,
+    i_sem, iy_sem, halo_sem, w_sem, l_sem, gx_sem,
+):
+    tokens, chunk, width, ff, local, nseq = dims
+    chunks = tokens // chunk
+    block = width // (2 * nseq)
+    per = block // ROWS
+    units = 4 * per
+    depth = nseq + 1
+    p = lax.axis_index("dp")
+    z = lax.axis_index("seq")
+    me = lax.axis_index("mp")
+    y, c = me // 2, me % 2
+    x_dev = {"dp": 1 - p}
+    up_dev = {"seq": z + 1}
+    dn_dev = {"seq": z - 1}
+    y_dev = {"mp": (1 - y) * 2 + c}
+    c_dev = {"mp": y * 2 + 1 - c}
+    last = nseq - 1
+
+    def remote(src, dst, sems, where, at=None):
+        s_sem, r_sem = (sems.at[0], sems.at[1]) if at is None else (sems.at[0, at], sems.at[1, at])
+        return pltpu.make_async_remote_copy(
+            src_ref=src, dst_ref=dst, send_sem=s_sem, recv_sem=r_sem,
+            device_id=where, device_id_type=MESH,
+        )
+
+    def load(src, dst, sem):
+        return pltpu.make_async_copy(src, dst, sem)
+
+    first_loads = [
+        load(cot_h, r.at[2, :, pl.ds(0, width)], w_sem.at[0]),
+        load(hidden_h, r.at[0], w_sem.at[1]),
+    ]
+    gate_load = load(gate_h, r.at[1], w_sem.at[2])
+    up_load = load(up_h, r.at[2], w_sem.at[3])
+    wd_load = load(wd_h, w0, w_sem.at[4])
+    wg_load = load(wg_h, wg, w_sem.at[5])
+    wu_load = load(wu_h, wu, w_sem.at[6])
+    wo_load = load(wo_h, wo, w_sem.at[7])
+    wi_loads = [
+        load(wi_h.at[k], w0.at[pl.ds(0, width), pl.ds(k * local, local)], w_sem.at[8 + k])
+        for k in range(3)
+    ]
+    for one in first_loads:
+        one.start()
+    gate_load.start()
+    wd_load.start()
+    wg_load.start()
+    wu_load.start()
+    wo_load.start()
+
+    barrier = pltpu.get_barrier_semaphore()
+    for dev in (x_dev, y_dev, c_dev):
+        pl.semaphore_signal(barrier, inc=1, device_id=dev, device_id_type=MESH)
+
+    @pl.when(z < last)
+    def _():
+        pl.semaphore_signal(barrier, inc=1, device_id=up_dev, device_id_type=MESH)
+
+    @pl.when(z > 0)
+    def _():
+        pl.semaphore_signal(barrier, inc=1, device_id=dn_dev, device_id_type=MESH)
+
+    peers = 3 + jnp.where(z < last, 1, 0) + jnp.where(z > 0, 1, 0)
+    pl.semaphore_wait(barrier, peers)
+
+    small_v[...] = jnp.zeros_like(small_v)
+
+    def transpose_into(index, src, at):
+        for q in range(4):
+            lt[index, pl.ds(q * local, local), pl.ds(at, chunk)] = src(q).T
+
+    for one in first_loads:
+        one.wait()
+
+    def cot_t(i, _):
+        at = pl.multiple_of(i * chunk, chunk)
+        transpose_into(0, lambda q: r[2, pl.ds(at, chunk), pl.ds(q * local, local)], at)
+        return 0
+
+    lax.fori_loop(0, chunks, cot_t, 0)
+    up_load.start()
+
+    def x_copy(u):
+        return pltpu.make_async_remote_copy(
+            src_ref=xs.at[lax.rem(u, 2)], dst_ref=xr.at[lax.rem(u, 4)],
+            send_sem=xs_sem.at[lax.rem(u, 2)], recv_sem=xr_sem.at[lax.rem(u, 4)],
+            device_id=x_dev, device_id_type=MESH,
+        )
+
+    def zs_at(u, step):
+        first = sum(last - one for one in range(step))
+        return first + lax.rem(u, last - step)
+
+    def z_copy(u, way, step):
+        return pltpu.make_async_remote_copy(
+            src_ref=zs.at[way, zs_at(u, step)], dst_ref=zr.at[way, step, lax.rem(u, 3)],
+            send_sem=zs_sem.at[way, step, lax.rem(u, 3)], recv_sem=zr_sem.at[way, step, lax.rem(u, 3)],
+            device_id=dn_dev if way else up_dev, device_id_type=MESH,
+        )
+
+    def sends(way, step):
+        return z >= last - step if way else jnp.logical_and(z <= step, z < last)
+
+    def receives(way, step):
+        if way:
+            return jnp.logical_and(z < last, z >= last - 1 - step)
+        return jnp.logical_and(z > 0, z <= step + 1)
+
+    def can_send(way, step):
+        if way:
+            return jnp.logical_and(z > 0, z >= last - step)
+        return jnp.logical_and(z < last, z <= step)
+
+    def z_step(u, step):
+        sl, slot = lax.rem(u, 6), lax.rem(u, 3)
+        for way in (0, 1):
+            quarter = z - last + step if way else last - step + z
+            if step > 0:
+                @pl.when(jnp.logical_and(receives(way, step - 1), can_send(way, step)))
+                def _(way=way, quarter=quarter):
+                    z_copy(u, way, step - 1).wait_recv()
+                    value = s_buf[sl, pl.ds(quarter * ROWS, ROWS), :].astype(F32) + zr[
+                        way, step - 1, slot
+                    ].astype(F32)
+                    zs[way, zs_at(u, step)] = value.astype(BF)
+
+                fresh = jnp.logical_and(can_send(way, step), jnp.logical_not(receives(way, step - 1)))
+            else:
+                fresh = can_send(way, step)
+
+            @pl.when(fresh)
+            def _(way=way, quarter=quarter):
+                zs[way, zs_at(u, step)] = s_buf[sl, pl.ds(quarter * ROWS, ROWS), :]
+
+            @pl.when(can_send(way, step))
+            def _(way=way):
+                z_copy(u, way, step).start()
+
+    def compute(u, kind):
+        k = lax.rem(u, per)
+        at = k * ROWS
+
+        def rows_of(index, half):
+            return [
+                lt[index, pl.ds(pl.multiple_of((half * nseq + s) * block + at, ROWS), ROWS), :]
+                for s in range(nseq)
+            ]
+
+        m = ROWS * nseq
+        if kind == 3:
+            left = jnp.concatenate(rows_of(0, 1 - p) + rows_of(0, p), 0)
+            out = nn(left, r[0, :, pl.ds(0, local)])
+            xs[lax.rem(u, 2), :, pl.ds(0, local)] = out[:m].astype(BF)
+            s_buf[lax.rem(u, 6), :, pl.ds(0, local)] = out[m:].astype(BF)
+            left = jnp.concatenate(rows_of(1, 1 - p) + rows_of(1, p), 0)
+            out = nn(left, r[0, :, pl.ds(local, 3 * local)])
+            xs[lax.rem(u, 2), :, pl.ds(local, 3 * local)] = out[:m].astype(BF)
+            s_buf[lax.rem(u, 6), :, pl.ds(local, 3 * local)] = out[m:].astype(BF)
+        else:
+            if kind == 0:
+                li, ri = 0, 0
+            else:
+                li, ri = 1, u // per
+            left = jnp.concatenate(rows_of(li, 1 - p) + rows_of(li, p), 0)
+            cut = (ff // 2 + 127) // 128 * 128
+            for lo, n in ((0, cut), (cut, ff - cut)):
+                out = nn(left, r[ri, :, pl.ds(lo, n)])
+                xs[lax.rem(u, 2), :, pl.ds(lo, n)] = out[:m].astype(BF)
+                s_buf[lax.rem(u, 6), :, pl.ds(lo, n)] = out[m:].astype(BF)
+
+    def out_do(u, what):
+        slot = lax.rem(u, 2)
+        rows = pl.ds(pl.multiple_of(lax.rem(u, per) * ROWS, ROWS), ROWS)
+        for g, target in enumerate((gdown_h, ggate_h, gup_h)):
+            @pl.when(u // per == g)
+            def _(target=target):
+                getattr(load(ob.at[slot], target.at[rows, :], ob_sem.at[slot]), what)()
+
+        @pl.when(u // per == 3)
+        def _():
+            out = load(ob.at[slot, :, pl.ds(0, local)], gout_h.at[rows, :], ob_sem.at[slot])
+            getattr(out, what)()
+            for k in range(3):
+                part = ob.at[slot, :, pl.ds((k + 1) * local, local)]
+                one = load(part, gin_h.at[k, rows, :], ob_sem.at[slot + 2 + 2 * k])
+                getattr(one, what)()
+
+    def finish(u):
+        sl, slot = lax.rem(u, 6), lax.rem(u, 3)
+
+        @pl.when(u >= 2)
+        def _():
+            out_do(u - 2, "wait")
+
+        ob[lax.rem(u, 2)] = s_buf[sl, pl.ds(z * ROWS, ROWS), :].astype(F32)
+        for way in (0, 1):
+            @pl.when(receives(way, last - 1))
+            def _(way=way):
+                z_copy(u, way, last - 1).wait_recv()
+                ob[lax.rem(u, 2)] += zr[way, last - 1, slot].astype(F32)
+
+        for way in (0, 1):
+            for step in range(last):
+                @pl.when(can_send(way, step))
+                def _(way=way, step=step):
+                    z_copy(u, way, step).wait_send()
+
+        out_do(u, "start")
+
+    def tick(t, kind=None, guard=True):
+        def within(u, f):
+            if guard:
+                @pl.when(jnp.logical_and(u >= 0, u < units))
+                def _():
+                    f()
+            else:
+                f()
+
+        within(t - depth, lambda: finish(t - depth))
+        for step in range(last - 1, 0, -1):
+            within(t - 2 - step, lambda step=step: z_step(t - 2 - step, step))
+
+        def x_in():
+            u = t - 2
+            x_copy(u).wait()
+            sl = lax.rem(u, 6)
+            s_buf[sl] = (s_buf[sl].astype(F32) + xr[lax.rem(u, 4)].astype(F32)).astype(BF)
+            z_step(u, 0)
+
+        within(t - 2, x_in)
+        if kind is not None:
+            compute(t, kind)
+            x_copy(t).start()
+
+    def rows_at(i):
+        return pl.ds(pl.multiple_of(i * chunk, chunk), chunk)
+
+    def cot_load(i, slot, sem):
+        return load(cot_h.at[rows_at(i), :], cotc.at[slot], l_sem.at[sem, slot])
+
+    def h1_load(i):
+        return load(h1_h.at[rows_at(i), :], h1c, l_sem.at[1, 0])
+
+    def bcv_load(i):
+        return load(bcv_h.at[:, rows_at(i), :], bcv, l_sem.at[2, 0])
+
+    def x_load(i):
+        return load(x_h.at[rows_at(i), :], xc, l_sem.at[3, 0])
+
+    def hidden_back(i):
+        slot = lax.rem(i, 2)
+        cot_load(i, slot, 0).wait()
+
+        @pl.when(i + 1 < chunks)
+        def _():
+            cot_load(i + 1, 1 - slot, 0).start()
+
+        cut = (ff // 2 + 127) // 128 * 128
+        for lo, n in ((0, cut), (cut, ff - cut)):
+            cols = pl.ds(lo, n)
+            dbuf[:, pl.ds(0, n)] = nt(cotc[slot], w0[pl.ds(lo, n), :])
+
+            def by_rows(b, _, cols=cols, n=n):
+                some = pl.ds(pl.multiple_of(i * chunk + b * 16, 16), 16)
+                dhid = dbuf[pl.ds(pl.multiple_of(b * 16, 16), 16), pl.ds(0, n)]
+                gate = r[1, some, cols].astype(F32)
+                up = r[2, some, cols].astype(F32)
+                sig = jax.nn.sigmoid(gate)
+                r[1, some, cols] = (dhid * up * sig * (1.0 + gate * (1.0 - sig))).astype(BF)
+                r[2, some, cols] = (dhid * gate * sig).astype(BF)
+                return 0
+
+            lax.fori_loop(0, chunk // 16, by_rows, 0)
+
+    def split_store(pair, value, keep, send):
+        for side in (0, 1):
+            part = value[:, side * local : (side + 1) * local]
+
+            @pl.when(c == side)
+            def _(part=part):
+                keep[pair] = part
+
+            @pl.when(c != side)
+            def _(part=part):
+                send[pair] = part.astype(BF)
+
+    def stage_a(i):
+        slot = lax.rem(i, 2)
+        rows = rows_at(i)
+        for pair in (0, 1):
+            cols = pl.ds(pair * 2 * local, 2 * local)
+            value = nn(r[1, rows, :], wg[:, cols]) + nn(r[2, rows, :], wu[:, cols])
+            split_store(pair, value, ck, cs)
+        remote(cs, cr.at[slot], c_sem, c_dev, slot).start()
+        cot_load(i, slot, 0).start()
+
+    def stage_b(i):
+        slot = lax.rem(i, 2)
+        remote(cs, cr.at[slot], c_sem, c_dev, slot).wait()
+        ys[...] = (ck[...] + cr[slot].astype(F32)).astype(BF)
+        remote(ys, yr.at[slot], y_sem, y_dev, slot).start()
+
+    def stage_c(i):
+        slot = lax.rem(i, 2)
+        remote(ys, yr.at[slot], y_sem, y_dev, slot).wait()
+        da2f[slot, :, c] = (ys[...].astype(F32) + yr[slot].astype(F32)).astype(BF)
+        remote(da2f.at[slot, :, c], da2f.at[slot, :, c], f_sem, c_dev, slot).start()
+        h1_load(i).start()
+        bcv_load(i).start()
+
+    def stage_d(i):
+        slot = lax.rem(i, 2)
+        remote(da2f.at[slot, :, c], da2f.at[slot, :, c], f_sem, c_dev, slot).wait()
+        cot_load(i, slot, 0).wait()
+        h1_load(i).wait()
+        bcv_load(i).wait()
+        x_load(i).start()
+        at = pl.multiple_of(i * chunk, chunk)
+        own = pl.ds(pl.multiple_of(me * local, 128), local)
+
+        def by_rows(b, _):
+            some = pl.ds(pl.multiple_of(b * 16, 16), 16)
+            ssq = jnp.zeros((16, local), F32)
+            inner = jnp.zeros((16, local), F32)
+            for q in range(4):
+                cols = pl.ds(q * local, local)
+                h1 = h1c[some, cols].astype(F32)
+                ssq += h1 * h1
+                inner += da2f[slot, q // 2, q % 2, some, :].astype(F32) * gains_v[1:2, cols] * h1
+            r2 = lax.rsqrt(jnp.sum(ssq, -1, keepdims=True) / width + EPS)
+            scale = r2 * r2 * r2 * jnp.sum(inner, -1, keepdims=True) / width
+
+            def grad(cols, da2):
+                h1 = h1c[some, cols].astype(F32)
+                return cotc[slot, some, cols].astype(F32) + r2 * (da2 * gains_v[1:2, cols]) - h1 * scale
+
+            for q in range(4):
+                cols = pl.ds(q * local, local)
+                dhoc[some, cols] = grad(cols, da2f[slot, q // 2, q % 2, some, :].astype(F32)).astype(BF)
+            da2 = da2f[slot, y, c, some, :].astype(F32)
+            dh1s[i, some, :] = grad(own, da2)
+            terms = da2 * h1c[some, own].astype(F32) * r2
+            small_v[pl.ds(8, 8), :] += terms[:8] + terms[8:]
+            return 0
+
+        lax.fori_loop(0, chunk // 16, by_rows, 0)
+        for q in range(4):
+            cols = pl.ds(q * local, local)
+            lt[0, cols, pl.ds(at, chunk)] = dhoc[:, cols].T
+        dmixed = nt(dhoc[...], wo[...])
+        b_gate, c_gate, value = bcv[0], bcv[1], bcv[2]
+        bxp[pl.ds(0, 8), :] = before_v[i]
+        bxp[pl.ds(8, chunk), :] = (b_gate.astype(F32) * value.astype(F32)).astype(BF).astype(F32)
+        shifts = [bxp[pl.ds(6 + k, chunk), :] for k in range(3)]
+        conv = sum(taps_v[k : k + 1, :] * shifts[k] for k in range(3))
+        r[0, pl.ds(at, chunk), pl.ds(0, local)] = (c_gate.astype(F32) * conv).astype(BF)
+        r[0, pl.ds(at, chunk), pl.ds(2 * local, local)] = (dmixed * conv).astype(BF)
+        dconv = (dmixed * c_gate.astype(F32)).astype(BF).astype(F32)
+        dcp[slot, pl.ds(0, chunk), :] = dconv
+        halo_s[i] = dconv[:8]
+        for k in range(3):
+            small_v[1 + k : 2 + k, :] += jnp.sum(dconv * shifts[k], 0, keepdims=True)
+
+        @pl.when(z > 0)
+        def _():
+            halo_copy(i).start()
+
+    def halo_copy(i):
+        return remote(halo_s.at[i], halo_r.at[i], halo_sem, dn_dev, i)
+
+    def stage_e(i):
+        slot = lax.rem(i, 2)
+        x_load(i).wait()
+
+        @pl.when(z > 0)
+        def _():
+            halo_copy(i).wait_send()
+
+        @pl.when(z < last)
+        def _():
+            halo_copy(i).wait_recv()
+            dcp[slot, pl.ds(chunk, 8), :] = halo_r[i]
+
+        @pl.when(z == last)
+        def _():
+            dcp[slot, pl.ds(chunk, 8), :] = jnp.zeros((8, local), F32)
+
+        dbx = sum(taps_v[2 - k : 3 - k, :] * dcp[slot, pl.ds(k, chunk), :] for k in range(3))
+        rows = rows_at(i)
+        r[0, rows, pl.ds(local, local)] = (dbx * bcv[2].astype(F32)).astype(BF)
+        r[0, rows, pl.ds(3 * local, local)] = (dbx * bcv[0].astype(F32)).astype(BF)
+        inner = jnp.zeros((chunk, 1), F32)
+        ssq = jnp.zeros((chunk, 1), F32)
+        for pair in (0, 1):
+            cols = pl.ds(pair * 2 * local, 2 * local)
+            value = nt(r[0, rows, pl.ds(local, 3 * local)], w0[cols, pl.ds(0, 3 * local)])
+            x = xc[:, cols].astype(F32)
+            inner += jnp.sum(value * x * gains_v[0:1, cols], -1, keepdims=True)
+            ssq += jnp.sum(x * x, -1, keepdims=True)
+            split_store(pair, value, ck2, cs2)
+        xo[...] = xc[:, pl.ds(pl.multiple_of(me * local, 128), local)]
+        ins[...] = jnp.broadcast_to(inner, ins.shape)
+        r1s[slot] = jnp.broadcast_to(lax.rsqrt(ssq / width + EPS), r1s.shape[1:])
+        remote(cs2, cr2.at[slot], c2_sem, c_dev, slot).start()
+        remote(ins, inr.at[slot], i_sem, c_dev, slot).start()
+
+    def stage_f(i):
+        slot = lax.rem(i, 2)
+        remote(cs2, cr2.at[slot], c2_sem, c_dev, slot).wait()
+        remote(ins, inr.at[slot], i_sem, c_dev, slot).wait()
+        ys2[...] = (ck2[1 - y] + cr2[slot, 1 - y].astype(F32)).astype(BF)
+        qk2[...] = ck2[y] + cr2[slot, y].astype(F32)
+        iys[...] = ins[...] + inr[slot]
+        remote(ys2, yr2.at[slot], y2_sem, y_dev, slot).start()
+        remote(iys, iyr.at[slot], iy_sem, y_dev, slot).start()
+
+    def gx_copy(i):
+        return load(gxb, gx_h.at[rows_at(i), :], gx_sem)
+
+    def stage_g(i):
+        slot = lax.rem(i, 2)
+        remote(ys2, yr2.at[slot], y2_sem, y_dev, slot).wait()
+        remote(iys, iyr.at[slot], iy_sem, y_dev, slot).wait()
+        da1 = qk2[...] + yr2[slot].astype(F32)
+        inner = (iys[:, :1] + iyr[slot, :, :1])
+        r1 = r1s[slot, :, :1]
+        own = pl.ds(pl.multiple_of(me * local, 128), local)
+        x = xo[...].astype(F32)
+        gain = gains_v[0:1, own]
+        small_v[0:1, :] += jnp.sum(da1 * x * r1, 0, keepdims=True)
+
+        @pl.when(i > 0)
+        def _():
+            gx_copy(i - 1).wait()
+
+        gxb[...] = (dh1s[i] + r1 * gain * da1 - x * (r1 * r1 * r1 * inner / width)).astype(BF)
+        gx_copy(i).start()
+
+    def valid(i, f):
+        @pl.when(jnp.logical_and(i >= 0, i < chunks))
+        def _():
+            f(i)
+
+    def part_one(i, _):
+        tick(i, 0)
+
+        @pl.when(i == 0)
+        def _():
+            cot_load(0, 0, 0).start()
+            gate_load.wait()
+            up_load.wait()
+            wd_load.wait()
+
+        hidden_back(i)
+        return 0
+
+    lax.fori_loop(0, chunks, part_one, 0)
+    for one in wi_loads:
+        one.start()
+    wg_load.wait()
+    wu_load.wait()
+    wo_load.wait()
+    for one in wi_loads:
+        one.wait()
+
+    def a_transposed(src_h, i):
+        one = load(src_h.at[rows_at(i), :], dhoc, l_sem.at[4, 0])
+        one.start()
+        one.wait()
+        at = pl.multiple_of(i * chunk, chunk)
+        transpose_into(1, lambda q: dhoc[:, pl.ds(q * local, local)], at)
+
+    def part_two(j, kind):
+        t = chunks + 2 * j
+        tick(t, kind)
+        valid(j - 3, stage_g)
+        valid(j - 2, stage_e)
+        valid(j - 1, stage_c)
+        valid(j, stage_a)
+        tick(t + 1, kind)
+        valid(j, stage_b)
+        valid(j - 1, stage_d)
+        valid(j - 2, stage_f)
+
+    def a2_body(i, _):
+        a_transposed(a2_h, i)
+        return 0
+
+    lax.fori_loop(0, chunks, a2_body, 0)
+    part_two(0, 0)
+
+    def loop_rest(j, _):
+        part_two(j, 1)
+        return 0
+
+    lax.fori_loop(1, 1 + (2 * per) // 2, loop_rest, 0)
+
+    def a1_body(i, _):
+        a_transposed(a1_h, i)
+        return 0
+
+    lax.fori_loop(0, chunks, a1_body, 0)
+    gx_copy(chunks - 1).wait()
+
+    def part_three(k, _):
+        tick(3 * per + k, 3)
+        return 0
+
+    lax.fori_loop(0, per, part_three, 0)
+
+    def part_four(k, _):
+        tick(units + k)
+        return 0
+
+    lax.fori_loop(0, depth, part_four, 0)
+    out_do(units - 2, "wait")
+    out_do(units - 1, "wait")
+
+
+def backward(dims, hidden, gate, up, a1, a2, x_full, h1, cot, bcv, before, wd, wg, wu, wo, wi, gains, taps):
+    tokens, chunk, width, ff, local, nseq = dims
+    block = width // (2 * nseq)
+    chunks = tokens // chunk
+    last = nseq - 1
+    m = ROWS * nseq
+    DMA = pltpu.SemaphoreType.DMA
+    shape = jax.ShapeDtypeStruct
+    scratch = [
+        pltpu.VMEM((2, width, tokens), BF),
+        pltpu.VMEM((3, tokens, ff), BF),
+        pltpu.VMEM((ff, width), BF),
+        pltpu.VMEM((ff, width), BF),
+        pltpu.VMEM((ff, width), BF),
+        pltpu.VMEM((local, width), BF),
+        pltpu.VMEM((2, chunk, width), BF),
+        pltpu.VMEM((chunk, width), BF),
+        pltpu.VMEM((chunk, width), BF),
+        pltpu.VMEM((chunk, local), BF),
+        pltpu.VMEM((3, chunk, local), BF),
+        pltpu.VMEM((8 + chunk, local), F32),
+        pltpu.VMEM((chunk, (ff // 2 + 127) // 128 * 128), F32),
+        pltpu.VMEM((2, 8 + chunk, local), F32),
+        pltpu.VMEM((chunk, width), BF),
+        pltpu.VMEM((chunks, chunk, local), F32),
+        pltpu.VMEM((2, chunk, 128), F32),
+        pltpu.VMEM((2, m, ff), BF),
+        pltpu.VMEM((4, m, ff), BF),
+        pltpu.VMEM((6, m, ff), BF),
+        pltpu.VMEM((2, last * (last + 1) // 2, ROWS, ff), BF),
+        pltpu.VMEM((2, last, 3, ROWS, ff), BF),
+        pltpu.VMEM((2, ROWS, ff), F32),
+        pltpu.VMEM((2, chunk, local), F32),
+        pltpu.VMEM((2, chunk, local), BF),
+        pltpu.VMEM((2, 2, chunk, local), BF),
+        pltpu.VMEM((2, chunk, local), BF),
+        pltpu.VMEM((2, 2, chunk, local), BF),
+        pltpu.VMEM((2, 2, 2, chunk, local), BF),
+        pltpu.VMEM((2, chunk, local), F32),
+        pltpu.VMEM((2, chunk, local), BF),
+        pltpu.VMEM((2, 2, chunk, local), BF),
+        pltpu.VMEM((chunk, local), BF),
+        pltpu.VMEM((2, chunk, local), BF),
+        pltpu.VMEM((chunk, local), F32),
+        pltpu.VMEM((chunk, 128), F32),
+        pltpu.VMEM((2, chunk, 128), F32),
+        pltpu.VMEM((chunk, 128), F32),
+        pltpu.VMEM((2, chunk, 128), F32),
+        pltpu.VMEM((chunk, local), BF),
+        pltpu.VMEM((chunks, 8, local), F32),
+        pltpu.VMEM((chunks, 8, local), F32),
+        DMA((2,)), DMA((4,)), DMA((2, last, 3)), DMA((2, last, 3)), DMA((8,)),
+        DMA((2, 2)), DMA((2, 2)), DMA((2, 2)), DMA((2, 2)), DMA((2, 2)),
+        DMA((2, 2)), DMA((2, 2)), DMA((2, chunks)), DMA((12,)), DMA((5, 2)), DMA(()),
+    ]
+    return pl.pallas_call(
+        functools.partial(backward_kernel, dims),
+        out_shape=(
+            shape((block, ff), F32), shape((block, ff), F32), shape((block, ff), F32),
+            shape((block, local), F32), shape((3, block, local), F32),
+            shape((tokens, local), BF), shape((16, local), F32),
+        ),
+        in_specs=[ANY] * 9 + [VMEM] + [ANY] * 5 + [VMEM] * 2,
+        out_specs=(ANY,) * 6 + (VMEM,),
+        scratch_shapes=scratch,
+        compiler_params=pltpu.CompilerParams(
+            collective_id=0, has_side_effects=True, vmem_limit_bytes=63 * 2**20
+        ),
+    )(hidden, gate, up, a1, a2, x_full, h1, cot, bcv, before, wd, wg, wu, wo, wi, gains, taps)
 
 
 def shifted(array, axis, by):
@@ -12,6 +631,62 @@
     return lax.ppermute(array, axis, pairs)
 
 
+def fused_device(inputs, gain_mix, w_in, kernel, w_out, gain_ff, w_gate, w_up, w_down, cotangent):
+    groups, seq_rows, local = inputs.shape
+    width = local * lax.axis_size("mp")
+    ff = w_down.shape[0]
+    tokens = groups * seq_rows
+    nseq = lax.axis_size("seq")
+    dims = (tokens, seq_rows, width, ff, local, nseq)
+    x_own = inputs.reshape(tokens, local)
+    taps = kernel.astype(F32)
+    wi = w_in.transpose(1, 0, 2)
+    wg, wu = w_gate.T, w_up.T
+
+    def all_features(values):
+        return lax.all_gather(values, "mp", axis=1, tiled=True)
+
+    def share_sums(values):
+        return lax.psum_scatter(values.astype(BF), "mp", scatter_dimension=1, tiled=True)
+
+    gains = all_features(jnp.stack([gain_mix, gain_ff])).astype(F32)
+    x_full = all_features(x_own)
+    cot = all_features(cotangent.reshape(tokens, local))
+
+    def normed(values, gain):
+        values = values.astype(F32)
+        scale = lax.rsqrt(jnp.mean(values * values, -1, keepdims=True) + EPS)
+        return (values * scale * gain).astype(BF)
+
+    a1 = normed(x_full, gains[0])
+    proj = [jnp.dot(a1, wi[k], preferred_element_type=F32) for k in range(3)]
+    bcv = jnp.stack(proj).astype(BF)
+    bx = (bcv[0].astype(F32) * bcv[2].astype(F32)).astype(BF).reshape(groups, seq_rows, local)
+    before = shifted(bx[:, seq_rows - 8 :], "seq", 1)
+    padded = jnp.concatenate([before[:, 6:], bx], 1).astype(F32)
+    conv = taps[0] * padded[:, :-2] + taps[1] * padded[:, 1:-1] + taps[2] * padded[:, 2:]
+    mixed = (bcv[1].astype(F32) * conv.reshape(tokens, local)).astype(BF)
+    h1_own = x_own.astype(F32) + share_sums(jnp.dot(mixed, w_out, preferred_element_type=F32)).astype(F32)
+    h1 = all_features(h1_own.astype(BF))
+    a2 = normed(h1, gains[1])
+    gate = lax.dot_general(a2, wg, (((1,), (1,)), ((), ())), preferred_element_type=F32)
+    up = lax.dot_general(a2, wu, (((1,), (1,)), ((), ())), preferred_element_type=F32)
+    hidden = (gate * jax.nn.sigmoid(gate) * up).astype(BF)
+    ffn = share_sums(jnp.dot(hidden, w_down, preferred_element_type=F32))
+    block_out = (h1_own + ffn.astype(F32)).astype(BF)
+    gdown, ggate, gup, gout, gin, gx, small = backward(
+        dims, hidden, gate.astype(BF), up.astype(BF), a1, a2, x_full, h1, cot, bcv,
+        before.astype(F32), w_down, wg, wu, w_out, wi, gains, taps,
+    )
+    small = small.at[4].set(small[8:].sum(0))[:8]
+    small = lax.psum(small, ("dp", "seq"))
+    whole = (groups, seq_rows, local)
+    return (
+        block_out.reshape(whole), gx.reshape(whole), small[0], gin.transpose(1, 0, 2), small[1:4],
+        gout.T, small[4], ggate, gup, gdown.T,
+    )
+
+
 def contract_rows(left, right):
     return lax.dot_general(
         left, right, (((0,), (0,)), ((), ())), preferred_element_type=jnp.float32
@@ -24,7 +699,7 @@
     )
 
 
-def on_device(inputs, gain_mix, w_in, kernel, w_out, gain_ff, w_gate, w_up, w_down, cotangent):
+def plain_device(inputs, gain_mix, w_in, kernel, w_out, gain_ff, w_gate, w_up, w_down, cotangent):
     groups, seq_rows, local_width = inputs.shape
     full_width = local_width * lax.axis_size("mp")
     tokens = groups * seq_rows
@@ -159,8 +834,10 @@
         P("mp", None),
         P("dp", "seq", "mp"),
     )
+    sizes = mesh.shape
+    fused = sizes["dp"] == 2 and sizes["seq"] == 4 and sizes["mp"] == 4
     return jax.shard_map(
-        on_device,
+        fused_device if fused else plain_device,
         mesh=mesh,
         in_specs=placed,
         out_specs=(

time: 884 us -> 537 us (0.61)
  waiting for transfers between devices: 585 us -> 94 us
  Pallas kernels: 0 us -> 262 us
  matrix products: 133 us -> 39 us
  blocking collectives: 65.7 us -> 40.5 us
  local copies, waits for them, and re-layouts: 34.9 us -> 51.3 us
  other arithmetic: 38.6 us -> 24 us
    reduce_scatter x5 -> x0, waiting for transfers between devices: 398 us -> none  [scattered(): lax.psum_scatter(values.astype(jnp.bfloat16), ('dp', 'seq'), scatter_dime...]
    pallas_call x0 -> x1, Pallas kernels: none -> 262 us  [backward(): pl.pallas_call(functools.partial(backward_kernel, dims), out_shape=(shape...]
    dot_general x15 -> x7, matrix products: 133 us -> 39 us  [the longest x1 12 us: fused_device(): lax.dot_general(a2, wg, (((1,), (1,)), ((), ())), preferred_element_type=...]
    unnamed x17 -> x7, waiting for transfers between devices: 115 us -> 40.1 us
    psum x5 -> x1, blocking collectives: 65.7 us -> 34.4 us  [fused_device(): small = lax.psum(small, ('dp', 'seq'))]
    dot_general x0 -> x2, local copies, waits for them, and re-layouts: none -> 16.3 us  [the longest x1 8.17 us: fused_device(): lax.dot_general(a2, wu, (((1,), (1,)), ((), ())), preferred_element_type=...]
    all_gather x4 -> x3, waiting for transfers between devices: 66.4 us -> 52.5 us  [all_features(): return lax.all_gather(values, 'mp', axis=1, tiled=True)]
    unnamed x59 -> x56, local copies, waits for them, and re-layouts: 32.8 us -> 20.8 us
  transfers between devices with their start and end apart: 15 -> 6, of which waited for: 13 -> 4; matrix products, arithmetic and copies ran while one was open for 14% -> 15% of each run, Pallas kernels for 0% -> 50%
where the time goes in v2:
time: 537 us; the launch traced here: 529 us
  Pallas kernels  262 us (49%)
  waiting for transfers between devices  94 us (18%)
  local copies, waits for them, and re-layouts  51.3 us (10%)
  blocking collectives  40.5 us (8%)
  matrix products  39 us (7%)
  other arithmetic  24 us (4%)
  between operations  14.5 us (3%)
    pallas_call x1, Pallas kernels, backward(): pl.pallas_call(functools.partial(backward_kernel, dims), out_shape=(shape...  262 us
    all_gather x3, waiting for transfers between devices, all_features(): return lax.all_gather(values, 'mp', axis=1, tiled=True)  52.5 us
    unnamed x7, waiting for transfers between devices  40.1 us
    psum x1, blocking collectives, fused_device(): small = lax.psum(small, ('dp', 'seq'))  34.4 us
    unnamed x56, local copies, waits for them, and re-layouts  20.8 us
    dot_general x1, matrix products, fused_device(): lax.dot_general(a2, wg, (((1,), (1,)), ((), ())), preferred_element_type=...  12 us
    dot_general x1, matrix products, fused_device(): lax.dot_general(a2, wu, (((1,), (1,)), ((), ())), preferred_element_type=...  10.8 us
  transfers between devices with their start and end apart: 6, of which 4 were waited for; matrix products, arithmetic and copies ran while one was open for 15% of the time, Pallas kernels for 50%

profile of v2, /device:TPU:0, one launch (start us, length us, event | category | flops | bytes accessed | tf_op | source)
XLA Modules:
  0.0 529.4 jit_solution(2884881339578281090)
XLA Ops:
  9.3 6.1 %all_gather.13 = bf16[2,1536]{1,0:T(2,128)(2,1)S(1)} all-gather(bf16[2,384]{1,0:T(2,128)(2,1)S(1)} %pad_maximum_fusion.1), channel_id=1, replica_groups=mesh['dp'=2,'seq'=4,'mp'=4] {'mp'}, dimensions={1}, use_global_device_ids=true | all-gather | bytes 7680 | tf_op jit(solution)/shard_map/all_gather | solution.py:647
  16.2 24.6 %all-gather.4.cloned.1.call-done.x_h = bf16[1024,1536]{1,0:T(8,128)(2,1)} async-done(((bf16[1024,384]{1,0:T(8,128)(2,1)}), bf16[1024,1536]{1,0:T(8,128)(2,1)}) %all-gather.4.cloned.1.call-update) | async-done | bytes 3145744 | tf_op jit(solution)/shard_map/all_gather | solution.py:647
  40.8 2.7 fusion
  44.4 1.8 copy-done.8
  48.1 2.7 multiply_convert_fusion.1
  50.7 3.4 collective-permute-start
  56.9 2.7 fusion.8
  61.4 2.9 copy.37
  64.3 38.9 %reduce-scatter.7.cloned.1.call-done = bf16[384,1024]{1,0:T(8,128)(2,1)} async-done(((bf16[1536,1024]{1,0:T(8,128)(2,1)}), bf16[384,1024]{1,0:T(8,128)(2,1)}) %reduce-scatter.7.cloned.1.call-update) | async-done | bytes 786448
  106.7 27.8 %all-gather.6.cloned.1.call-done.h1_h = bf16[1024,1536]{1,0:T(8,128)(2,1)} async-done(((bf16[1024,384]{1,0:T(8,128)(2,1)}), bf16[1024,1536]{1,0:T(8,128)(2,1)}) %all-gather.6.cloned.1.call-update) | async-done | bytes 3145744 | tf_op jit(solution)/shard_map/all_gather | solution.py:647
  134.6 2.7 fusion.3
  138.2 12.0 %fusion.12 = (bf16[1024,1728]{0,1:T(8,128)(2,1)}, f32[1024,1728]{0,1:T(8,128)}) fusion(bf16[1024,1536]{1,0:T(8,128)(2,1)S(1)} %fusion.5.a2_h, bf16[1536,1728]{0,1:T(8,128)(2,1)} %param.18), kind=kOutput, calls=%fused_computation.45 | convolution fusion | flops 5437587456 | bytes 19070976 | tf_op jit(solution)/shard_map/dot_general | solution.py:672
  150.2 8.1 %copy.33 = f32[1024,1728]{1,0:T(8,128)} copy(f32[1024,1728]{0,1:T(8,128)} %get-tuple-element.48) | data formatting | bytes 14155776 | tf_op jit(solution)/shard_map/dot_general | solution.py:672
  158.3 10.8 %fusion.13 = (bf16[1024,1728]{0,1:T(8,128)(2,1)}, f32[1024,1728]{0,1:T(8,128)}) fusion(bf16[1024,1536]{1,0:T(8,128)(2,1)S(1)} %fusion.5.a2_h, bf16[1536,1728]{0,1:T(8,128)(2,1)} %param.19), kind=kOutput, calls=%fused_computation.46 | convolution fusion | flops 5437587456 | bytes 19070976 | tf_op jit(solution)/shard_map/dot_general | solution.py:673
  169.1 8.2 %copy.34 = f32[1024,1728]{1,0:T(8,128)} copy(f32[1024,1728]{0,1:T(8,128)} %get-tuple-element.50) | data formatting | bytes 14155776 | tf_op jit(solution)/shard_map/dot_general | solution.py:673
  177.3 6.4 %multiply_convert_fusion.hidden_h = bf16[1024,1728]{1,0:T(8,128)(2,1)S(1)} fusion(f32[1024,1728]{1,0:T(8,128)} %copy.34, f32[1024,1728]{1,0:T(8,128)} %copy.33), kind=kLoop, calls=%fused_computation.4 | loop fusion | flops 10616832 | bytes 17694720 | tf_op jit(solution)/shard_map/convert_element_type | solution.py:674
  185.6 7.2 %convolution_convert_fusion = bf16[1024,1536]{1,0:T(8,128)(2,1)} fusion(bf16[1024,1728]{1,0:T(8,128)(2,1)S(1)} %multiply_convert_fusion.hidden_h, bf16[1728,1536]{1,0:T(8,128)(2,1)S(1)} %bitcast.56), kind=kOutput, calls=%fused_computation.11 | convolution fusion | flops 5437390848 | bytes 11993088 | tf_op jit(solution)/shard_map/dot_general | solution.py:675
  192.8 4.7 copy.39
  199.0 3.3 pad_maximum_fusion.bcv_h
  202.4 3.7 copy.35.gate_h
  206.1 5.9 %copy.36.up_h = bf16[1024,1728]{1,0:T(8,128)(2,1)} copy(bf16[1024,1728]{0,1:T(8,128)(2,1)} %get-tuple-element.49) | data formatting | bytes 7077888 | tf_op jit(solution)/shard_map/convert_element_type | solution.py:678
  212.0 262.3 %shard_map.177 = (f32[192,1728]{1,0:T(8,128)}, f32[192,1728]{1,0:T(8,128)}, f32[192,1728]{1,0:T(8,128)}, f32[192,384]{1,0:T(8,128)}, f32[3,192,384]{2,1,0:T(8,12...) custom-call(bf16[1024,1728]{1,0:T(8,128)(2,1)} %copy-done.2, bf16[1024,1728]{1,0:T(8,128)(2,1)} %copy.35.gate_h, ...), custom_call_target="tpu_custom_call" | custom-call | tf_op jit(solution)/shard_map/pallas_call | solution.py:612
  477.1 34.4 %psum.7 = f32[8,384]{1,0:T(8,128)S(1)} all-reduce(f32[8,384]{1,0:T(8,128)S(1)} %slice.103), channel_id=1, replica_groups=mesh['dp'=2,'seq'=4,'mp'=4] {'dp','seq'}, use_global_device_ids=true, to_apply=%region_5.0 | all-reduce | flops 3072 | bytes 24576 | tf_op jit(solution)/shard_map/psum | solution.py:682
  514.2 2.5 add_convert_fusion
  (92 shorter events, 29.0 us)
Async XLA Ops:
  7.2 33.6 %all-gather.4.cloned.1.call-start = ((), (), s32[]{:S(2)}) async-start(), calls=%async_computation.2 | async-start | bytes 3932160 | tf_op jit(solution)/shard_map/all_gather | solution.py:647
  7.9 95.3 %reduce-scatter.7.cloned.1.call-start = ((), (), s32[]{:S(2)}) async-start(), calls=%async_computation.5 | async-start | bytes 3932160
  15.5 29.0 %copy-start.18 = (f32[2,1536]{1,0:T(2,128)}, f32[2,1536]{1,0:T(2,128)S(1)}, u32[]{:S(2)}) copy-start(f32[2,1536]{1,0:T(2,128)S(1)} %convert_element_type.83.gains_v) | copy-start | bytes 36868
  16.2 38.0 %copy-start.19 = (f32[3,384]{1,0:T(4,128)}, f32[3,384]{1,0:T(4,128)S(1)}, u32[]{:S(2)}) copy-start(f32[3,384]{1,0:T(4,128)S(1)} %convert_element_type.87.taps_v) | copy-start | bytes 13828
  40.8 2.8 copy-start
  44.4 12.4 %copy-start.3 = (bf16[1024,1536]{1,0:T(8,128)(2,1)}, bf16[1024,1536]{1,0:T(8,128)(2,1)S(1)}, u32[]{:S(2)}) copy-start(bf16[1024,1536]{1,0:T(8,128)(2,1)S(1)} %fusion.2.a1_h) | copy-start | bytes 9437188
  48.0 2.7 copy-start.15
  50.7 4.9 collective-permute-start
  64.3 40.4 %copy-start.5 = (bf16[4,256,384]{2,1,0:T(8,128)(2,1)S(1)}, bf16[4,256,384]{2,1,0:T(8,128)(2,1)}, u32[]{:S(2)}) copy-start(bf16[4,256,384]{2,1,0:T(8,128)(2,1)} %param.12) | copy-start | bytes 2359300
  64.3 70.3 %all-gather.6.cloned.1.call-start = ((), (), s32[]{:S(2)}) async-start(), calls=%async_computation.3 | async-start | bytes 3932160 | tf_op jit(solution)/shard_map/all_gather | solution.py:647
  104.7 32.6 %copy-start.7 = (bf16[1024,384]{1,0:T(8,128)(2,1)}, bf16[1024,384]{1,0:T(8,128)(2,1)S(1)}, u32[]{:S(2)}) copy-start(bf16[1024,384]{1,0:T(8,128)(2,1)S(1)} %copy.38) | copy-start | bytes 2359300
  105.9 106.1 %all-gather.8.cloned.1.call-start = ((), (), s32[]{:S(2)}) async-start(), calls=%async_computation.4 | async-start | bytes 3932160 | tf_op jit(solution)/shard_map/all_gather | solution.py:647
  106.5 406.2 %reduce-scatter.9.cloned.1.call-start = ((), (), s32[]{:S(2)}) async-start(), calls=%async_computation.6 | async-start | bytes 3932160
  134.6 2.8 copy-start.1
  138.2 20.1 %copy-start.4 = (bf16[1024,1536]{1,0:T(8,128)(2,1)}, bf16[1024,1536]{1,0:T(8,128)(2,1)S(1)}, u32[]{:S(2)}) copy-start(bf16[1024,1536]{1,0:T(8,128)(2,1)S(1)} %fusion.5.a2_h) | copy-start | bytes 9437188
  169.1 16.4 %slice-start = ((s8[5308416]{0:T(1024)(128)(4,1)}), s8[1114112]{0:T(1024)(128)(4,1)S(1)}, s32[]{:S(2)}) async-start(s8[5308416]{0:T(1024)(128)(4,1)} %bitcast.55), calls=%async_computation.7 | async-start | bytes 2228224
  177.3 8.3 %slice-start.1 = ((s8[5308416]{0:T(1024)(128)(4,1)}), s8[4194304]{0:T(1024)(128)(4,1)S(1)}, s32[]{:S(2)}) async-start(s8[5308416]{0:T(1024)(128)(4,1)} %bitcast.55), calls=%async_computation.8 | async-start | bytes 8388608
  197.5 4.9 copy-start.9
  212.0 302.2 %copy-start.6 = (bf16[4,256,384]{2,1,0:T(8,128)(2,1)S(1)}, bf16[4,256,384]{2,1,0:T(8,128)(2,1)}, u32[]{:S(2)}) copy-start(bf16[4,256,384]{2,1,0:T(8,128)(2,1)} %param.12) | copy-start | bytes 2359300
  514.2 3.4 copy-start.14
  514.2 4.3 copy-start.17
  514.2 5.0 copy-start.12
  516.7 3.6 copy-start.11
  518.5 2.9 copy-start.10
  (5 other events, 10.2 us)
Sparse Core Ops, SparseCore 0:
  9.6 31.1 all-gather.3
  64.4 38.7 reduce-scatter.6
  106.0 28.4 all-gather.5
  136.1 28.4 all-gather.7
  197.6 37.9 reduce-scatter.8

commit v3 on v2

--- a/solution.py
+++ b/solution.py
@@ -24,17 +24,18 @@
     return lax.dot_general(left, right, (((1,), (1,)), ((), ())), preferred_element_type=F32)
 
 
-def backward_kernel(
+def block_kernel(
     dims,
-    hidden_h, gate_h, up_h, a1_h, a2_h, x_h, h1_h, cot_h, bcv_h, before_v,
-    wd_h, wg_h, wu_h, wo_h, wi_h, gains_v, taps_v,
-    gdown_h, ggate_h, gup_h, gout_h, gin_h, gx_h, small_v,
-    lt, r, w0, wg, wu, wo, cotc, h1c, xc, xo, bcv, bxp, dbuf, dcp, dhoc, dh1s, r1s,
+    x_in, cot_in, own_v, wd_h, wg_h, wu_h, wo_h, wi_h,
+    gdown_h, ggate_h, gup_h, gout_h, gin_h, gx_h, out_h, small_v,
+    x_h, cot_h, h1_h, bcv_h,
+    lt, r, w0, wg, wu, wo, cotc, xc, xo, bcv, bxp, dbuf, dcp, dhoc, dh1s, r1s, gv,
     xs, xr, s_buf, zs, zr, ob,
-    ck, cs, cr, ys, yr, da2f, ck2, cs2, cr2, ys2, yr2, qk2,
-    ins, inr, iys, iyr, gxb, halo_s, halo_r,
+    kf, cs, cr, ys, yr4, da2f, cs2, ys2, yr2,
+    ins, inr, iys, iyr, gxb, halo_s, halo_r, before_s, before_r, small_r,
     xs_sem, xr_sem, zs_sem, zr_sem, ob_sem, c_sem, y_sem, f_sem, c2_sem, y2_sem,
-    i_sem, iy_sem, halo_sem, w_sem, l_sem, gx_sem,
+    i_sem, iy_sem, halo_sem, before_sem, gather_sem, own_sem, w_sem, l_sem, bcv_sem, h1_sem, gx_sem,
+    small_sem,
 ):
     tokens, chunk, width, ff, local, nseq = dims
     chunks = tokens // chunk
@@ -52,6 +53,9 @@
     y_dev = {"mp": (1 - y) * 2 + c}
     c_dev = {"mp": y * 2 + 1 - c}
     last = nseq - 1
+    ck, ck2, qk2 = kf.at[pl.ds(0, 2)], kf.at[pl.ds(2, 2)], kf.at[4]
+    third = ff // 3 // 128 * 128
+    cuts = ((0, third), (third, third), (2 * third, ff - 2 * third))
 
     def remote(src, dst, sems, where, at=None):
         s_sem, r_sem = (sems.at[0], sems.at[1]) if at is None else (sems.at[0, at], sems.at[1, at])
@@ -63,27 +67,17 @@
     def load(src, dst, sem):
         return pltpu.make_async_copy(src, dst, sem)
 
-    first_loads = [
-        load(cot_h, r.at[2, :, pl.ds(0, width)], w_sem.at[0]),
-        load(hidden_h, r.at[0], w_sem.at[1]),
-    ]
-    gate_load = load(gate_h, r.at[1], w_sem.at[2])
-    up_load = load(up_h, r.at[2], w_sem.at[3])
-    wd_load = load(wd_h, w0, w_sem.at[4])
-    wg_load = load(wg_h, wg, w_sem.at[5])
-    wu_load = load(wu_h, wu, w_sem.at[6])
-    wo_load = load(wo_h, wo, w_sem.at[7])
-    wi_loads = [
-        load(wi_h.at[k], w0.at[pl.ds(0, width), pl.ds(k * local, local)], w_sem.at[8 + k])
-        for k in range(3)
-    ]
-    for one in first_loads:
-        one.start()
-    gate_load.start()
-    wd_load.start()
-    wg_load.start()
-    wu_load.start()
+    def wi_load(k):
+        return load(wi_h.at[k], w0.at[pl.ds(0, width), pl.ds(k * local, local)], w_sem.at[k])
+
+    wd_load = load(wd_h, w0, w_sem.at[3])
+    wg_load = load(wg_h, wg, w_sem.at[4])
+    wu_load = load(wu_h, wu, w_sem.at[5])
+    wo_load = load(wo_h, wo, w_sem.at[6])
+    for k in range(3):
+        wi_load(k).start()
     wo_load.start()
+    gv[me] = own_v[...]
 
     barrier = pltpu.get_barrier_semaphore()
     for dev in (x_dev, y_dev, c_dev):
@@ -102,20 +96,57 @@
 
     small_v[...] = jnp.zeros_like(small_v)
 
-    def transpose_into(index, src, at):
-        for q in range(4):
-            lt[index, pl.ds(q * local, local), pl.ds(at, chunk)] = src(q).T
-
-    for one in first_loads:
-        one.wait()
-
-    def cot_t(i, _):
-        at = pl.multiple_of(i * chunk, chunk)
-        transpose_into(0, lambda q: r[2, pl.ds(at, chunk), pl.ds(q * local, local)], at)
-        return 0
-
-    lax.fori_loop(0, chunks, cot_t, 0)
-    up_load.start()
+    def rows_at(i):
+        return pl.ds(pl.multiple_of(i * chunk, chunk), chunk)
+
+    def gather(which, i, leg):
+        if which == 2:
+            src = mine = own_v
+            dst = gv
+            at = (2, 0)
+        else:
+            src, dst = (x_in, x_h) if which == 0 else (cot_in, cot_h)
+            mine = src.at[rows_at(i), :]
+            at = (which, i)
+        slot = (lambda q: dst.at[q]) if which == 2 else (lambda q: dst.at[q, rows_at(i), :])
+        sems = [gather_sem.at[leg, way, at[0], at[1]] for way in (0, 1)]
+        if leg == 0:
+            pair, where = (mine, slot(me)), y_dev
+        elif leg == 1:
+            pair, where = (mine, slot(me)), c_dev
+        else:
+            from_y = (1 - y) * 2 + c
+            pair, where = (slot(from_y), slot(from_y)), c_dev
+        return pltpu.make_async_remote_copy(
+            src_ref=pair[0], dst_ref=pair[1], send_sem=sems[0], recv_sem=sems[1],
+            device_id=where, device_id_type=MESH,
+        )
+
+    def gather_start(which, i):
+        gather(which, i, 0).start()
+        gather(which, i, 1).start()
+
+    def gather_pass(which, i):
+        gather(which, i, 0).wait_recv()
+        gather(which, i, 2).start()
+
+    def gather_end(which, i):
+        gather(which, i, 0).wait_send()
+        gather(which, i, 1).wait()
+        gather(which, i, 2).wait()
+
+    own_copies = [
+        load(x_in, x_h.at[me], own_sem.at[0]),
+        load(cot_in, cot_h.at[me], own_sem.at[1]),
+    ]
+    for i in range(chunks):
+        gather_start(0, i)
+        if i == 0:
+            gather_start(2, 0)
+    for one in own_copies:
+        one.start()
+    wg_load.start()
+    wu_load.start()
 
     def x_copy(u):
         return pltpu.make_async_remote_copy(
@@ -199,8 +230,7 @@
             else:
                 li, ri = 1, u // per
             left = jnp.concatenate(rows_of(li, 1 - p) + rows_of(li, p), 0)
-            cut = (ff // 2 + 127) // 128 * 128
-            for lo, n in ((0, cut), (cut, ff - cut)):
+            for lo, n in cuts:
                 out = nn(left, r[ri, :, pl.ds(lo, n)])
                 xs[lax.rem(u, 2), :, pl.ds(lo, n)] = out[:m].astype(BF)
                 s_buf[lax.rem(u, 6), :, pl.ds(lo, n)] = out[m:].astype(BF)
@@ -229,12 +259,20 @@
         def _():
             out_do(u - 2, "wait")
 
-        ob[lax.rem(u, 2)] = s_buf[sl, pl.ds(z * ROWS, ROWS), :].astype(F32)
         for way in (0, 1):
             @pl.when(receives(way, last - 1))
             def _(way=way):
                 z_copy(u, way, last - 1).wait_recv()
-                ob[lax.rem(u, 2)] += zr[way, last - 1, slot].astype(F32)
+
+        def end(ways):
+            total = s_buf[sl, pl.ds(z * ROWS, ROWS), :].astype(F32)
+            for way in ways:
+                total += zr[way, last - 1, slot].astype(F32)
+            ob[lax.rem(u, 2)] = total.astype(BF)
+
+        pl.when(z == 0)(lambda: end((1,)))
+        pl.when(z == last)(lambda: end((0,)))
+        pl.when(jnp.logical_and(z > 0, z < last))(lambda: end((0, 1)))
 
         for way in (0, 1):
             for step in range(last):
@@ -269,37 +307,188 @@
             compute(t, kind)
             x_copy(t).start()
 
-    def rows_at(i):
-        return pl.ds(pl.multiple_of(i * chunk, chunk), chunk)
-
-    def cot_load(i, slot, sem):
-        return load(cot_h.at[rows_at(i), :], cotc.at[slot], l_sem.at[sem, slot])
+    def in_slices(src, to, slot):
+        return [load(src(q), to(q), l_sem.at[slot, q]) for q in range(4)]
+
+    def cot_load(i, slot):
+        return in_slices(
+            lambda q: cot_h.at[q, rows_at(i), :],
+            lambda q: cotc.at[slot, :, pl.ds(q * local, local)],
+            slot,
+        )
+
+    def start(copies):
+        for one in copies:
+            one.start()
+
+    def wait(copies):
+        for one in copies:
+            one.wait()
 
     def h1_load(i):
-        return load(h1_h.at[rows_at(i), :], h1c, l_sem.at[1, 0])
+        return load(h1_h.at[:, rows_at(i), :], xc, l_sem.at[2, 0])
 
     def bcv_load(i):
-        return load(bcv_h.at[:, rows_at(i), :], bcv, l_sem.at[2, 0])
+        return load(bcv_h.at[:, rows_at(i), :], bcv, l_sem.at[2, 1])
 
     def x_load(i):
-        return load(x_h.at[rows_at(i), :], xc, l_sem.at[3, 0])
+        return load(x_h.at[:, rows_at(i), :], xc, l_sem.at[2, 2])
+
+    def gain(row, q):
+        return gv[q, row : row + 1, :]
+
+    def by_sixteen(f):
+        def body(b, _):
+            f(pl.ds(pl.multiple_of(b * 16, 16), 16))
+            return 0
+
+        lax.fori_loop(0, chunk // 16, body, 0)
+
+    def normed_to(src, row, after=None):
+        def f(some):
+            ssq = jnp.zeros((16, local), F32)
+            for q in range(4):
+                values = src(q, some).astype(F32)
+                ssq += values * values
+            scale = lax.rsqrt(jnp.sum(ssq, -1, keepdims=True) / width + EPS)
+            for q in range(4):
+                dhoc[some, pl.ds(q * local, local)] = (src(q, some).astype(F32) * scale * gain(row, q)).astype(BF)
+
+        by_sixteen(f)
+
+    def transposed_to(index, i):
+        at = pl.multiple_of(i * chunk, chunk)
+        for q in range(4):
+            cols = pl.ds(q * local, local)
+            lt[index, cols, pl.ds(at, chunk)] = dhoc[:, cols].T
+
+    def before_copy(i):
+        return remote(before_s.at[i], before_r.at[i], before_sem, up_dev, i)
+
+    def bcv_store(i):
+        return load(bcv, bcv_h.at[:, rows_at(i), :], bcv_sem)
+
+    def h1_store(i, slot, pair, core):
+        return load(da2f.at[slot, pair, core], h1_h.at[2 * pair + core, rows_at(i), :], h1_sem.at[pair, core])
+
+    def project(i):
+        gather_end(0, i)
+        x_load(i).start()
+        x_load(i).wait()
+        normed_to(lambda q, some: xc[q, some, :], 0)
+        value = nn(dhoc[...], w0[pl.ds(0, width), pl.ds(0, 3 * local)])
+
+        @pl.when(i > 0)
+        def _():
+            bcv_store(i - 1).wait()
+
+        for k in range(3):
+            bcv[k] = value[:, k * local : (k + 1) * local].astype(BF)
+        dcp[pl.ds(0, chunk), :] = value[:, local : 2 * local]
+        bx = (value[:, :local] * value[:, 2 * local :]).astype(BF)
+        bcv[3] = bx
+        bxp[pl.ds(8, chunk), :] = bx.astype(F32)
+        before_s[i] = bxp[pl.ds(chunk, 8), :]
+
+        @pl.when(z < last)
+        def _():
+            before_copy(i).start()
+
+        bcv_store(i).start()
+
+    def conv_of():
+        shifts = [bxp[pl.ds(6 + k, chunk), :] for k in range(3)]
+        return sum(own_v[2 + k : 3 + k, :] * shifts[k] for k in range(3)), shifts
+
+    def mix(i):
+        slot = lax.rem(i, 2)
+
+        @pl.when(z < last)
+        def _():
+            before_copy(i).wait_send()
+
+        @pl.when(z > 0)
+        def _():
+            before_copy(i).wait_recv()
+
+        @pl.when(z == 0)
+        def _():
+            before_r[i] = jnp.zeros((8, local), F32)
+
+        bxp[pl.ds(0, 8), :] = before_r[i]
+        mixed = (dcp[pl.ds(0, chunk), :] * conv_of()[0]).astype(BF)
+        for pair in (0, 1):
+            split_store(pair, nn(mixed, wo[:, pl.ds(pair * 2 * local, 2 * local)]), ck, cs)
+        remote(cs, cr.at[slot], c_sem, c_dev, slot).start()
+
+    def share(i):
+        slot = lax.rem(i, 2)
+        remote(cs, cr.at[slot], c_sem, c_dev, slot).wait()
+        for pair in (0, 1):
+            total = ck[pair] + cr[slot, pair].astype(F32)
+            kf[2 + 2 * slot + pair] = total + xc[2 * pair + c].astype(F32)
+            ys[slot, pair] = total.astype(BF)
+        remote(ys.at[slot], yr4.at[i], y_sem, y_dev, i).start()
+
+    def residual(i):
+        slot = lax.rem(i, 2)
+        remote(ys.at[slot], yr4.at[i], y_sem, y_dev, i).wait()
+
+        @pl.when(i >= 1)
+        def _():
+            for pair in (0, 1):
+                for core in (0, 1):
+                    h1_store(i - 1, 1 - slot, pair, core).wait()
+
+        for pair in (0, 1):
+            h1 = kf[2 + 2 * slot + pair] + yr4[i, pair].astype(F32)
+            da2f[slot, pair, c] = h1.astype(BF)
+
+            @pl.when(y == pair)
+            def _(h1=h1):
+                dh1s[i] = h1
+        remote(da2f.at[slot, :, c], da2f.at[slot, :, c], f_sem, c_dev, slot).start()
+
+    def feed(i):
+        slot = lax.rem(i, 2)
+        remote(da2f.at[slot, :, c], da2f.at[slot, :, c], f_sem, c_dev, slot).wait()
+        for pair in (0, 1):
+            for core in (0, 1):
+                h1_store(i, slot, pair, core).start()
+        normed_to(lambda q, some: da2f[slot, q // 2, q % 2, some, :], 1)
+        transposed_to(1, i)
+        for lo, n in cuts:
+            dbuf[0, :, pl.ds(0, n)] = nt(dhoc[...], wg[pl.ds(lo, n), :])
+            dbuf[1, :, pl.ds(0, n)] = nt(dhoc[...], wu[pl.ds(lo, n), :])
+
+            def by_rows(b, _, lo=lo, n=n):
+                cols = pl.ds(lo, n)
+                here = pl.ds(pl.multiple_of(b * 16, 16), 16)
+                some = pl.ds(pl.multiple_of(i * chunk + b * 16, 16), 16)
+                gate = dbuf[0, here, pl.ds(0, n)]
+                up = dbuf[1, here, pl.ds(0, n)]
+                r[0, some, cols] = (gate * jax.nn.sigmoid(gate) * up).astype(BF)
+                r[1, some, cols] = gate.astype(BF)
+                r[2, some, cols] = up.astype(BF)
+                return 0
+
+            lax.fori_loop(0, chunk // 16, by_rows, 0)
 
     def hidden_back(i):
         slot = lax.rem(i, 2)
-        cot_load(i, slot, 0).wait()
+        wait(cot_load(i, slot))
 
         @pl.when(i + 1 < chunks)
         def _():
-            cot_load(i + 1, 1 - slot, 0).start()
-
-        cut = (ff // 2 + 127) // 128 * 128
-        for lo, n in ((0, cut), (cut, ff - cut)):
+            start(cot_load(i + 1, 1 - slot))
+
+        for lo, n in cuts:
             cols = pl.ds(lo, n)
-            dbuf[:, pl.ds(0, n)] = nt(cotc[slot], w0[pl.ds(lo, n), :])
+            dbuf[0, :, pl.ds(0, n)] = nt(cotc[slot], w0[pl.ds(lo, n), :])
 
             def by_rows(b, _, cols=cols, n=n):
                 some = pl.ds(pl.multiple_of(i * chunk + b * 16, 16), 16)
-                dhid = dbuf[pl.ds(pl.multiple_of(b * 16, 16), 16), pl.ds(0, n)]
+                dhid = dbuf[0, pl.ds(pl.multiple_of(b * 16, 16), 16), pl.ds(0, n)]
                 gate = r[1, some, cols].astype(F32)
                 up = r[2, some, cols].astype(F32)
                 sig = jax.nn.sigmoid(gate)
@@ -329,18 +518,18 @@
             value = nn(r[1, rows, :], wg[:, cols]) + nn(r[2, rows, :], wu[:, cols])
             split_store(pair, value, ck, cs)
         remote(cs, cr.at[slot], c_sem, c_dev, slot).start()
-        cot_load(i, slot, 0).start()
+        start(cot_load(i, slot))
 
     def stage_b(i):
         slot = lax.rem(i, 2)
         remote(cs, cr.at[slot], c_sem, c_dev, slot).wait()
-        ys[...] = (ck[...] + cr[slot].astype(F32)).astype(BF)
-        remote(ys, yr.at[slot], y_sem, y_dev, slot).start()
+        ys[slot] = (ck[...] + cr[slot].astype(F32)).astype(BF)
+        remote(ys.at[slot], yr4.at[slot], y_sem, y_dev, slot).start()
 
     def stage_c(i):
         slot = lax.rem(i, 2)
-        remote(ys, yr.at[slot], y_sem, y_dev, slot).wait()
-        da2f[slot, :, c] = (ys[...].astype(F32) + yr[slot].astype(F32)).astype(BF)
+        remote(ys.at[slot], yr4.at[slot], y_sem, y_dev, slot).wait()
+        da2f[slot, :, c] = (ys[slot].astype(F32) + yr4[slot].astype(F32)).astype(BF)
         remote(da2f.at[slot, :, c], da2f.at[slot, :, c], f_sem, c_dev, slot).start()
         h1_load(i).start()
         bcv_load(i).start()
@@ -348,10 +537,9 @@
     def stage_d(i):
         slot = lax.rem(i, 2)
         remote(da2f.at[slot, :, c], da2f.at[slot, :, c], f_sem, c_dev, slot).wait()
-        cot_load(i, slot, 0).wait()
+        wait(cot_load(i, slot))
         h1_load(i).wait()
         bcv_load(i).wait()
-        x_load(i).start()
         at = pl.multiple_of(i * chunk, chunk)
         own = pl.ds(pl.multiple_of(me * local, 128), local)
 
@@ -361,39 +549,37 @@
             inner = jnp.zeros((16, local), F32)
             for q in range(4):
                 cols = pl.ds(q * local, local)
-                h1 = h1c[some, cols].astype(F32)
+                h1 = xc[q, some, :].astype(F32)
                 ssq += h1 * h1
-                inner += da2f[slot, q // 2, q % 2, some, :].astype(F32) * gains_v[1:2, cols] * h1
+                inner += da2f[slot, q // 2, q % 2, some, :].astype(F32) * gain(1, q) * h1
             r2 = lax.rsqrt(jnp.sum(ssq, -1, keepdims=True) / width + EPS)
             scale = r2 * r2 * r2 * jnp.sum(inner, -1, keepdims=True) / width
 
-            def grad(cols, da2):
-                h1 = h1c[some, cols].astype(F32)
-                return cotc[slot, some, cols].astype(F32) + r2 * (da2 * gains_v[1:2, cols]) - h1 * scale
+            def grad(q, cols, da2):
+                h1 = xc[q, some, :].astype(F32)
+                return cotc[slot, some, cols].astype(F32) + r2 * (da2 * gain(1, q)) - h1 * scale
 
             for q in range(4):
                 cols = pl.ds(q * local, local)
-                dhoc[some, cols] = grad(cols, da2f[slot, q // 2, q % 2, some, :].astype(F32)).astype(BF)
+                dhoc[some, cols] = grad(q, cols, da2f[slot, q // 2, q % 2, some, :].astype(F32)).astype(BF)
             da2 = da2f[slot, y, c, some, :].astype(F32)
-            dh1s[i, some, :] = grad(own, da2)
-            terms = da2 * h1c[some, own].astype(F32) * r2
+            dh1s[i, some, :] = grad(me, own, da2)
+            terms = da2 * xc[me, some, :].astype(F32) * r2
             small_v[pl.ds(8, 8), :] += terms[:8] + terms[8:]
             return 0
 
         lax.fori_loop(0, chunk // 16, by_rows, 0)
-        for q in range(4):
-            cols = pl.ds(q * local, local)
-            lt[0, cols, pl.ds(at, chunk)] = dhoc[:, cols].T
+        x_load(i).start()
+        transposed_to(0, i)
         dmixed = nt(dhoc[...], wo[...])
-        b_gate, c_gate, value = bcv[0], bcv[1], bcv[2]
-        bxp[pl.ds(0, 8), :] = before_v[i]
-        bxp[pl.ds(8, chunk), :] = (b_gate.astype(F32) * value.astype(F32)).astype(BF).astype(F32)
-        shifts = [bxp[pl.ds(6 + k, chunk), :] for k in range(3)]
-        conv = sum(taps_v[k : k + 1, :] * shifts[k] for k in range(3))
+        c_gate = bcv[1]
+        bxp[pl.ds(0, 8), :] = before_r[i]
+        bxp[pl.ds(8, chunk), :] = bcv[3].astype(F32)
+        conv, shifts = conv_of()
         r[0, pl.ds(at, chunk), pl.ds(0, local)] = (c_gate.astype(F32) * conv).astype(BF)
         r[0, pl.ds(at, chunk), pl.ds(2 * local, local)] = (dmixed * conv).astype(BF)
         dconv = (dmixed * c_gate.astype(F32)).astype(BF).astype(F32)
-        dcp[slot, pl.ds(0, chunk), :] = dconv
+        dcp[pl.ds(0, chunk), :] = dconv
         halo_s[i] = dconv[:8]
         for k in range(3):
             small_v[1 + k : 2 + k, :] += jnp.sum(dconv * shifts[k], 0, keepdims=True)
@@ -416,13 +602,13 @@
         @pl.when(z < last)
         def _():
             halo_copy(i).wait_recv()
-            dcp[slot, pl.ds(chunk, 8), :] = halo_r[i]
+            dcp[pl.ds(chunk, 8), :] = halo_r[i]
 
         @pl.when(z == last)
         def _():
-            dcp[slot, pl.ds(chunk, 8), :] = jnp.zeros((8, local), F32)
-
-        dbx = sum(taps_v[2 - k : 3 - k, :] * dcp[slot, pl.ds(k, chunk), :] for k in range(3))
+            dcp[pl.ds(chunk, 8), :] = jnp.zeros((8, local), F32)
+
+        dbx = sum(own_v[4 - k : 5 - k, :] * dcp[pl.ds(k, chunk), :] for k in range(3))
         rows = rows_at(i)
         r[0, rows, pl.ds(local, local)] = (dbx * bcv[2].astype(F32)).astype(BF)
         r[0, rows, pl.ds(3 * local, local)] = (dbx * bcv[0].astype(F32)).astype(BF)
@@ -431,22 +617,25 @@
         for pair in (0, 1):
             cols = pl.ds(pair * 2 * local, 2 * local)
             value = nt(r[0, rows, pl.ds(local, 3 * local)], w0[cols, pl.ds(0, 3 * local)])
-            x = xc[:, cols].astype(F32)
-            inner += jnp.sum(value * x * gains_v[0:1, cols], -1, keepdims=True)
-            ssq += jnp.sum(x * x, -1, keepdims=True)
+            for side in (0, 1):
+                q = 2 * pair + side
+                x = xc[q].astype(F32)
+                part = value[:, side * local : (side + 1) * local]
+                inner += jnp.sum(part * x * gain(0, q), -1, keepdims=True)
+                ssq += jnp.sum(x * x, -1, keepdims=True)
             split_store(pair, value, ck2, cs2)
-        xo[...] = xc[:, pl.ds(pl.multiple_of(me * local, 128), local)]
+        xo[...] = xc[me]
         ins[...] = jnp.broadcast_to(inner, ins.shape)
         r1s[slot] = jnp.broadcast_to(lax.rsqrt(ssq / width + EPS), r1s.shape[1:])
-        remote(cs2, cr2.at[slot], c2_sem, c_dev, slot).start()
+        remote(cs2, yr4.at[2 + slot], c2_sem, c_dev, slot).start()
         remote(ins, inr.at[slot], i_sem, c_dev, slot).start()
 
     def stage_f(i):
         slot = lax.rem(i, 2)
-        remote(cs2, cr2.at[slot], c2_sem, c_dev, slot).wait()
+        remote(cs2, yr4.at[2 + slot], c2_sem, c_dev, slot).wait()
         remote(ins, inr.at[slot], i_sem, c_dev, slot).wait()
-        ys2[...] = (ck2[1 - y] + cr2[slot, 1 - y].astype(F32)).astype(BF)
-        qk2[...] = ck2[y] + cr2[slot, y].astype(F32)
+        ys2[...] = (ck2[1 - y] + yr4[2 + slot, 1 - y].astype(F32)).astype(BF)
+        qk2[...] = ck2[y] + yr4[2 + slot, y].astype(F32)
         iys[...] = ins[...] + inr[slot]
         remote(ys2, yr2.at[slot], y2_sem, y_dev, slot).start()
         remote(iys, iyr.at[slot], iy_sem, y_dev, slot).start()
@@ -461,70 +650,168 @@
         da1 = qk2[...] + yr2[slot].astype(F32)
         inner = (iys[:, :1] + iyr[slot, :, :1])
         r1 = r1s[slot, :, :1]
-        own = pl.ds(pl.multiple_of(me * local, 128), local)
         x = xo[...].astype(F32)
-        gain = gains_v[0:1, own]
+        scaled = gain(0, me)
         small_v[0:1, :] += jnp.sum(da1 * x * r1, 0, keepdims=True)
 
         @pl.when(i > 0)
         def _():
             gx_copy(i - 1).wait()
 
-        gxb[...] = (dh1s[i] + r1 * gain * da1 - x * (r1 * r1 * r1 * inner / width)).astype(BF)
+        gxb[...] = (dh1s[i] + r1 * scaled * da1 - x * (r1 * r1 * r1 * inner / width)).astype(BF)
         gx_copy(i).start()
+
+    def out_start(i):
+        rows = rows_at(i)
+        for pair in (0, 1):
+            cols = pl.ds(pair * 2 * local, 2 * local)
+            split_store(pair, nn(r[0, rows, :], w0[:, cols]), ck2, cs2)
+        remote(cs2, yr4.at[2 + lax.rem(i, 2)], c2_sem, c_dev, lax.rem(i, 2)).start()
+
+    def out_share(i):
+        slot = lax.rem(i, 2)
+        remote(cs2, yr4.at[2 + slot], c2_sem, c_dev, slot).wait()
+        ys2[...] = (ck2[1 - y] + yr4[2 + slot, 1 - y].astype(F32)).astype(BF)
+        qk2[...] = ck2[y] + yr4[2 + slot, y].astype(F32)
+        remote(ys2, yr2.at[slot], y2_sem, y_dev, slot).start()
+
+    def out_copy(i):
+        return load(gxb, out_h.at[rows_at(i), :], gx_sem)
+
+    def out_end(i):
+        slot = lax.rem(i, 2)
+        remote(ys2, yr2.at[slot], y2_sem, y_dev, slot).wait()
+
+        @pl.when(i > 0)
+        def _():
+            out_copy(i - 1).wait()
+
+        gxb[...] = (dh1s[i] + (qk2[...] + yr2[slot].astype(F32))).astype(BF)
+        out_copy(i).start()
 
     def valid(i, f):
         @pl.when(jnp.logical_and(i >= 0, i < chunks))
         def _():
             f(i)
 
+    gather_pass(0, 0)
+    gather_pass(2, 0)
+    for k in range(3):
+        wi_load(k).wait()
+    wo_load.wait()
+    gather_end(2, 0)
+    for one in own_copies:
+        one.wait()
+
+    def forward(j, _):
+        @pl.when(j < chunks)
+        def _():
+            project(j)
+
+            @pl.when(j + 1 < chunks)
+            def _():
+                gather_pass(0, j + 1)
+
+            mix(j)
+
+        @pl.when(j == chunks - 1)
+        def _():
+            wd_load.start()
+
+        @pl.when(j >= 2)
+        def _():
+            residual(j - 2)
+
+        @pl.when(j < chunks)
+        def _():
+            share(j)
+
+        @pl.when(j == chunks - 1)
+        def _():
+            for i in range(chunks):
+                gather_start(1, i)
+
+        @pl.when(j == 2)
+        def _():
+            wg_load.wait()
+            wu_load.wait()
+
+        @pl.when(j >= 2)
+        def _():
+            feed(j - 2)
+
+        return 0
+
+    lax.fori_loop(0, chunks + 2, forward, 0)
+    bcv_store(chunks - 1).wait()
+    for pair in (0, 1):
+        for core in (0, 1):
+            h1_store(chunks - 1, (chunks - 1) % 2, pair, core).wait()
+
+    def cot_pass(i, _):
+        gather_pass(1, i)
+        return 0
+
+    lax.fori_loop(0, chunks, cot_pass, 0)
+
+    def cot_turn(i, _):
+        gather_end(1, i)
+        slot = lax.rem(i, 2)
+        start(cot_load(i, slot))
+        wait(cot_load(i, slot))
+        at = pl.multiple_of(i * chunk, chunk)
+        for q in range(4):
+            cols = pl.ds(q * local, local)
+            lt[0, cols, pl.ds(at, chunk)] = cotc[slot, :, cols].T
+        return 0
+
+    lax.fori_loop(0, chunks, cot_turn, 0)
+    start(cot_load(0, 0))
+
     def part_one(i, _):
         tick(i, 0)
 
         @pl.when(i == 0)
         def _():
-            cot_load(0, 0, 0).start()
-            gate_load.wait()
-            up_load.wait()
             wd_load.wait()
 
+        valid(i - 2, out_end)
+        valid(i - 1, out_share)
+        out_start(i)
         hidden_back(i)
         return 0
 
     lax.fori_loop(0, chunks, part_one, 0)
-    for one in wi_loads:
-        one.start()
-    wg_load.wait()
-    wu_load.wait()
-    wo_load.wait()
-    for one in wi_loads:
-        one.wait()
-
-    def a_transposed(src_h, i):
-        one = load(src_h.at[rows_at(i), :], dhoc, l_sem.at[4, 0])
-        one.start()
-        one.wait()
-        at = pl.multiple_of(i * chunk, chunk)
-        transpose_into(1, lambda q: dhoc[:, pl.ds(q * local, local)], at)
+    for k in range(3):
+        wi_load(k).start()
 
     def part_two(j, kind):
         t = chunks + 2 * j
         tick(t, kind)
+
+        @pl.when(j == 0)
+        def _():
+            out_end(chunks - 2)
+            out_share(chunks - 1)
+
         valid(j - 3, stage_g)
         valid(j - 2, stage_e)
         valid(j - 1, stage_c)
         valid(j, stage_a)
         tick(t + 1, kind)
+
+        @pl.when(j == 0)
+        def _():
+            out_end(chunks - 1)
+            out_copy(chunks - 1).wait()
+
         valid(j, stage_b)
         valid(j - 1, stage_d)
         valid(j - 2, stage_f)
 
-    def a2_body(i, _):
-        a_transposed(a2_h, i)
-        return 0
-
-    lax.fori_loop(0, chunks, a2_body, 0)
     part_two(0, 0)
+    for k in range(3):
+        wi_load(k).wait()
 
     def loop_rest(j, _):
         part_two(j, 1)
@@ -532,15 +819,71 @@
 
     lax.fori_loop(1, 1 + (2 * per) // 2, loop_rest, 0)
 
-    def a1_body(i, _):
-        a_transposed(a1_h, i)
+    def a1_turn(i, _):
+        x_load(i).start()
+        x_load(i).wait()
+        normed_to(lambda q, some: xc[q, some, :], 0)
+        transposed_to(1, i)
         return 0
 
-    lax.fori_loop(0, chunks, a1_body, 0)
+    lax.fori_loop(0, chunks, a1_turn, 0)
     gx_copy(chunks - 1).wait()
+    small_v[4:5, :] = jnp.sum(small_v[8:16, :], 0, keepdims=True)
+
+    def small_x():
+        return pltpu.make_async_remote_copy(
+            src_ref=small_v.at[pl.ds(0, 8)], dst_ref=small_r.at[0], send_sem=small_sem.at[0, 0],
+            recv_sem=small_sem.at[0, 1], device_id=x_dev, device_id_type=MESH,
+        )
+
+    def small_z(way):
+        return pltpu.make_async_remote_copy(
+            src_ref=small_r.at[1 + way], dst_ref=small_r.at[3 + way], send_sem=small_sem.at[1 + way, 0],
+            recv_sem=small_sem.at[1 + way, 1], device_id=dn_dev if way else up_dev, device_id_type=MESH,
+        )
+
+    small_x().start()
+
+    def small_step(k):
+        @pl.when(k == 0)
+        def _():
+            small_x().wait()
+            total = small_v[pl.ds(0, 8), :] + small_r[0]
+            small_v[pl.ds(0, 8), :] = total
+            small_r[1] = total
+            small_r[2] = total
+
+        for way in (0, 1):
+            turn = last - z if way else z
+
+            @pl.when(jnp.logical_and(turn < last, k == turn))
+            def _(way=way, turn=turn):
+                @pl.when(turn > 0)
+                def _():
+                    small_z(way).wait_recv()
+                    small_r[1 + way] = small_v[pl.ds(0, 8), :] + small_r[3 + way]
+
+                small_z(way).start()
+
+    def small_end():
+        for way in (0, 1):
+            turn = last - z if way else z
+
+            @pl.when(turn < last)
+            def _(way=way):
+                small_z(way).wait_send()
+
+            @pl.when(turn == last)
+            def _(way=way):
+                small_z(way).wait_recv()
+
+            @pl.when(turn > 0)
+            def _(way=way):
+                small_v[pl.ds(0, 8), :] += small_r[3 + way]
 
     def part_three(k, _):
         tick(3 * per + k, 3)
+        small_step(k)
         return 0
 
     lax.fori_loop(0, per, part_three, 0)
@@ -550,18 +893,20 @@
         return 0
 
     lax.fori_loop(0, depth, part_four, 0)
+    small_end()
     out_do(units - 2, "wait")
     out_do(units - 1, "wait")
 
 
-def backward(dims, hidden, gate, up, a1, a2, x_full, h1, cot, bcv, before, wd, wg, wu, wo, wi, gains, taps):
+def block(dims, x_own, cot_own, own, wd, wg, wu, wo, wi):
     tokens, chunk, width, ff, local, nseq = dims
-    block = width // (2 * nseq)
+    rows = width // (2 * nseq)
     chunks = tokens // chunk
     last = nseq - 1
     m = ROWS * nseq
     DMA = pltpu.SemaphoreType.DMA
     shape = jax.ShapeDtypeStruct
+    third = ff // 3 // 128 * 128
     scratch = [
         pltpu.VMEM((2, width, tokens), BF),
         pltpu.VMEM((3, tokens, ff), BF),
@@ -570,34 +915,31 @@
         pltpu.VMEM((ff, width), BF),
         pltpu.VMEM((local, width), BF),
         pltpu.VMEM((2, chunk, width), BF),
-        pltpu.VMEM((chunk, width), BF),
-        pltpu.VMEM((chunk, width), BF),
+        pltpu.VMEM((4, chunk, local), BF),
         pltpu.VMEM((chunk, local), BF),
-        pltpu.VMEM((3, chunk, local), BF),
+        pltpu.VMEM((4, chunk, local), BF),
         pltpu.VMEM((8 + chunk, local), F32),
-        pltpu.VMEM((chunk, (ff // 2 + 127) // 128 * 128), F32),
-        pltpu.VMEM((2, 8 + chunk, local), F32),
+        pltpu.VMEM((2, chunk, ff - 2 * third), F32),
+        pltpu.VMEM((8 + chunk, local), F32),
         pltpu.VMEM((chunk, width), BF),
         pltpu.VMEM((chunks, chunk, local), F32),
         pltpu.VMEM((2, chunk, 128), F32),
+        pltpu.VMEM((4, 8, local), F32),
         pltpu.VMEM((2, m, ff), BF),
         pltpu.VMEM((4, m, ff), BF),
         pltpu.VMEM((6, m, ff), BF),
         pltpu.VMEM((2, last * (last + 1) // 2, ROWS, ff), BF),
         pltpu.VMEM((2, last, 3, ROWS, ff), BF),
-        pltpu.VMEM((2, ROWS, ff), F32),
-        pltpu.VMEM((2, chunk, local), F32),
+        pltpu.VMEM((2, ROWS, ff), BF),
+        pltpu.VMEM((6, chunk, local), F32),
         pltpu.VMEM((2, chunk, local), BF),
         pltpu.VMEM((2, 2, chunk, local), BF),
+        pltpu.VMEM((2, 2, chunk, local), BF),
+        pltpu.VMEM((4, 2, chunk, local), BF),
+        pltpu.VMEM((2, 2, 2, chunk, local), BF),
         pltpu.VMEM((2, chunk, local), BF),
-        pltpu.VMEM((2, 2, chunk, local), BF),
-        pltpu.VMEM((2, 2, 2, chunk, local), BF),
-        pltpu.VMEM((2, chunk, local), F32),
-        pltpu.VMEM((2, chunk, local), BF),
-        pltpu.VMEM((2, 2, chunk, local), BF),
         pltpu.VMEM((chunk, local), BF),
         pltpu.VMEM((2, chunk, local), BF),
-        pltpu.VMEM((chunk, local), F32),
         pltpu.VMEM((chunk, 128), F32),
         pltpu.VMEM((2, chunk, 128), F32),
         pltpu.VMEM((chunk, 128), F32),
@@ -605,24 +947,30 @@
         pltpu.VMEM((chunk, local), BF),
         pltpu.VMEM((chunks, 8, local), F32),
         pltpu.VMEM((chunks, 8, local), F32),
+        pltpu.VMEM((chunks, 8, local), F32),
+        pltpu.VMEM((chunks, 8, local), F32),
+        pltpu.VMEM((5, 8, local), F32),
         DMA((2,)), DMA((4,)), DMA((2, last, 3)), DMA((2, last, 3)), DMA((8,)),
-        DMA((2, 2)), DMA((2, 2)), DMA((2, 2)), DMA((2, 2)), DMA((2, 2)),
-        DMA((2, 2)), DMA((2, 2)), DMA((2, chunks)), DMA((12,)), DMA((5, 2)), DMA(()),
+        DMA((2, 2)), DMA((2, chunks)), DMA((2, 2)), DMA((2, 2)), DMA((2, 2)),
+        DMA((2, 2)), DMA((2, 2)), DMA((2, chunks)), DMA((2, chunks)), DMA((3, 2, 3, chunks)),
+        DMA((2,)), DMA((7,)), DMA((3, 4)), DMA(()), DMA((2, 2)), DMA(()), DMA((3, 2)),
     ]
     return pl.pallas_call(
-        functools.partial(backward_kernel, dims),
+        functools.partial(block_kernel, dims),
         out_shape=(
-            shape((block, ff), F32), shape((block, ff), F32), shape((block, ff), F32),
-            shape((block, local), F32), shape((3, block, local), F32),
-            shape((tokens, local), BF), shape((16, local), F32),
+            shape((rows, ff), BF), shape((rows, ff), BF), shape((rows, ff), BF),
+            shape((rows, local), BF), shape((3, rows, local), BF),
+            shape((tokens, local), BF), shape((tokens, local), BF), shape((16, local), F32),
+            shape((4, tokens, local), BF), shape((4, tokens, local), BF),
+            shape((4, tokens, local), BF), shape((4, tokens, local), BF),
         ),
-        in_specs=[ANY] * 9 + [VMEM] + [ANY] * 5 + [VMEM] * 2,
-        out_specs=(ANY,) * 6 + (VMEM,),
+        in_specs=[ANY, ANY, VMEM] + [ANY] * 5,
+        out_specs=(ANY,) * 7 + (VMEM,) + (ANY,) * 4,
         scratch_shapes=scratch,
         compiler_params=pltpu.CompilerParams(
             collective_id=0, has_side_effects=True, vmem_limit_bytes=63 * 2**20
         ),
-    )(hidden, gate, up, a1, a2, x_full, h1, cot, bcv, before, wd, wg, wu, wo, wi, gains, taps)
+    )(x_own, cot_own, own, wd, wg, wu, wo, wi)
 
 
 def shifted(array, axis, by):
@@ -636,54 +984,18 @@
     width = local * lax.axis_size("mp")
     ff = w_down.shape[0]
     tokens = groups * seq_rows
-    nseq = lax.axis_size("seq")
-    dims = (tokens, seq_rows, width, ff, local, nseq)
-    x_own = inputs.reshape(tokens, local)
-    taps = kernel.astype(F32)
-    wi = w_in.transpose(1, 0, 2)
-    wg, wu = w_gate.T, w_up.T
-
-    def all_features(values):
-        return lax.all_gather(values, "mp", axis=1, tiled=True)
-
-    def share_sums(values):
-        return lax.psum_scatter(values.astype(BF), "mp", scatter_dimension=1, tiled=True)
-
-    gains = all_features(jnp.stack([gain_mix, gain_ff])).astype(F32)
-    x_full = all_features(x_own)
-    cot = all_features(cotangent.reshape(tokens, local))
-
-    def normed(values, gain):
-        values = values.astype(F32)
-        scale = lax.rsqrt(jnp.mean(values * values, -1, keepdims=True) + EPS)
-        return (values * scale * gain).astype(BF)
-
-    a1 = normed(x_full, gains[0])
-    proj = [jnp.dot(a1, wi[k], preferred_element_type=F32) for k in range(3)]
-    bcv = jnp.stack(proj).astype(BF)
-    bx = (bcv[0].astype(F32) * bcv[2].astype(F32)).astype(BF).reshape(groups, seq_rows, local)
-    before = shifted(bx[:, seq_rows - 8 :], "seq", 1)
-    padded = jnp.concatenate([before[:, 6:], bx], 1).astype(F32)
-    conv = taps[0] * padded[:, :-2] + taps[1] * padded[:, 1:-1] + taps[2] * padded[:, 2:]
-    mixed = (bcv[1].astype(F32) * conv.reshape(tokens, local)).astype(BF)
-    h1_own = x_own.astype(F32) + share_sums(jnp.dot(mixed, w_out, preferred_element_type=F32)).astype(F32)
-    h1 = all_features(h1_own.astype(BF))
-    a2 = normed(h1, gains[1])
-    gate = lax.dot_general(a2, wg, (((1,), (1,)), ((), ())), preferred_element_type=F32)
-    up = lax.dot_general(a2, wu, (((1,), (1,)), ((), ())), preferred_element_type=F32)
-    hidden = (gate * jax.nn.sigmoid(gate) * up).astype(BF)
-    ffn = share_sums(jnp.dot(hidden, w_down, preferred_element_type=F32))
-    block_out = (h1_own + ffn.astype(F32)).astype(BF)
-    gdown, ggate, gup, gout, gin, gx, small = backward(
-        dims, hidden, gate.astype(BF), up.astype(BF), a1, a2, x_full, h1, cot, bcv,
-        before.astype(F32), w_down, wg, wu, w_out, wi, gains, taps,
-    )
-    small = small.at[4].set(small[8:].sum(0))[:8]
-    small = lax.psum(small, ("dp", "seq"))
+    dims = (tokens, seq_rows, width, ff, local, lax.axis_size("seq"))
+    own = jnp.concatenate(
+        [gain_mix[None], gain_ff[None], kernel, jnp.zeros((3, local), BF)], 0
+    ).astype(F32)
+    gdown, ggate, gup, gout, gin, gx, out, small = block(
+        dims, inputs.reshape(tokens, local), cotangent.reshape(tokens, local), own,
+        w_down, w_gate.T, w_up.T, w_out, w_in.transpose(1, 0, 2),
+    )[:8]
     whole = (groups, seq_rows, local)
     return (
-        block_out.reshape(whole), gx.reshape(whole), small[0], gin.transpose(1, 0, 2), small[1:4],
-        gout.T, small[4], ggate, gup, gdown.T,
+        out.reshape(whole), gx.reshape(whole), small[0], gin.transpose(1, 0, 2).astype(F32), small[1:4],
+        gout.T.astype(F32), small[4], ggate.astype(F32), gup.astype(F32), gdown.T.astype(F32),
     )
 
 

time: 537 us -> 403 us (0.75); the launches traced: 529 us -> 402 us
  Pallas kernels: 262 us -> 385 us
  waiting for transfers between devices: 94 us -> 0 us
  local copies, waits for them, and re-layouts: 51.3 us -> 5.95 us
  blocking collectives: 40.5 us -> 0 us
  matrix products: 39 us -> 0 us
  other arithmetic: 24 us -> 9.65 us
  between operations: 14.5 us -> 0.68 us
    pallas_call x1, Pallas kernels: 262 us -> 385 us  [block(): pl.pallas_call(functools.partial(block_kernel, dims), out_shape=(shape((r...]
    all_gather x3 -> x0, waiting for transfers between devices: 52.5 us -> none  [all_features(): return lax.all_gather(values, 'mp', axis=1, tiled=True)]
    unnamed x7 -> x0, waiting for transfers between devices: 40.1 us -> none
    dot_general x7 -> x0, matrix products: 39 us -> none  [the longest x1 12 us: fused_device(): lax.dot_general(a2, wg, (((1,), (1,)), ((), ())), preferred_element_type=...]
    psum x1 -> x0, blocking collectives: 34.4 us -> none  [fused_device(): small = lax.psum(small, ('dp', 'seq'))]
    unnamed x56 -> x10, local copies, waits for them, and re-layouts: 20.8 us -> 1.77 us
    dot_general x2 -> x0, local copies, waits for them, and re-layouts: 16.3 us -> none  [the longest x1 8.17 us: fused_device(): lax.dot_general(a2, wu, (((1,), (1,)), ((), ())), preferred_element_type=...]
    convert_element_type x2 -> x0, local copies, waits for them, and re-layouts: 9.62 us -> none  [the longest x1 5.9 us: fused_device(): up.astype(BF)]
  transfers between devices with their start and end apart: 6 -> 0, of which waited for: 4 -> 0; matrix products, arithmetic and copies ran while one was open for 15% -> 0% of each run, Pallas kernels for 50% -> 0%
where the time goes in v3:
time: 403 us; the launch traced here: 402 us
  Pallas kernels  385 us (96%)
  other arithmetic  9.65 us (2%)
  local copies, waits for them, and re-layouts  5.95 us (1%)
    pallas_call x1, Pallas kernels, block(): pl.pallas_call(functools.partial(block_kernel, dims), out_shape=(shape((r...  385 us

profile of v3, /device:TPU:0, one launch (start us, length us, event | category | flops | bytes accessed | tf_op | source)
XLA Modules:
  0.0 401.8 jit_solution(8671316030737043029)
XLA Ops:
  0.7 0.1 pad.3.clone
  0.7 0.7 broadcast_in_dim.9
  1.4 0.7 broadcast_in_dim.10
  2.1 1.4 maximum_convert_fusion.own_v
  3.4 385.5 %shard_map.177 = (bf16[192,1728]{1,0:T(8,128)(2,1)}, bf16[192,1728]{1,0:T(8,128)(2,1)}, bf16[192,1728]{1,0:T(8,128)(2,1)}, bf16[192,384]{1,0:T(8,128)(2,1)}, bf1...) custom-call(bf16[1024,384]{1,0:T(8,128)(2,1)} %bitcast.16, ...), custom_call_target="tpu_custom_call" | custom-call | tf_op jit(solution)/shard_map/pallas_call | solution.py:958
  388.9 0.0 copy-start.3
  388.9 0.0 copy-start.2
  389.0 1.4 slice_reduce_fusion
  390.4 1.3 slice.10
  391.7 1.6 convert_bitcast_fusion.2
  393.3 2.0 convert_bitcast_fusion.1
  395.3 0.0 copy-start.1
  395.3 2.3 convert_element_type.32
  397.7 0.0 copy-done.3
  397.7 0.0 copy-start
  397.7 1.2 convert_element_type.33
  398.8 0.0 copy-done.2
  398.8 1.2 convert_bitcast_fusion
  400.0 0.0 copy-done.1
  400.0 0.9 copy.22
  400.9 0.0 copy-done
  400.9 0.9 copy.23
  (1 shorter events, 0.0 us)
Async XLA Ops:
  388.9 8.7 %copy-start.3 = (bf16[192,1728]{1,0:T(8,128)(2,1)S(1)}, bf16[192,1728]{1,0:T(8,128)(2,1)}, u32[]{:S(2)}) copy-start(bf16[192,1728]{1,0:T(8,128)(2,1)} %get-tuple-element.24) | copy-start | bytes 1990660
  388.9 9.9 %copy-start.2 = (bf16[192,1728]{1,0:T(8,128)(2,1)S(1)}, bf16[192,1728]{1,0:T(8,128)(2,1)}, u32[]{:S(2)}) copy-start(bf16[192,1728]{1,0:T(8,128)(2,1)} %get-tuple-element.25) | copy-start | bytes 1990660
  395.3 4.7 %copy-start.1 = (bf16[1024,384]{1,0:T(8,128)(2,1)S(1)}, bf16[1024,384]{1,0:T(8,128)(2,1)}, u32[]{:S(2)}) copy-start(bf16[1024,384]{1,0:T(8,128)(2,1)} %get-tuple-element.18) | copy-start | bytes 2359300
  397.7 3.2 copy-start

commit v4 on v3

--- a/solution.py
+++ b/solution.py
@@ -12,6 +12,23 @@
 BF = jnp.bfloat16
 F32 = jnp.float32
 ROWS = 32
+SECOND = 3
+LAG = 3
+WAIT = 3
+PLACES = {
+    "out_start": (2, (1, 4, 7, 8)),
+    "out_share": (2, (2, 5, 8, 10)),
+    "out_end": (1, (4, 7, 9, 12)),
+    "a": (2, (3, 8, 10, 14)),
+    "b": (2, (4, 9, 12, 15)),
+    "c": (1, (8, 11, 14, 18)),
+    "d": (2, (9, 13, 17, 19)),
+    "e": (2, (12, 15, 18, 20)),
+    "f": (2, (14, 16, 19, 21)),
+    "g": (2, (15, 18, 20, 22)),
+    "a1": (2, (15, 16, 17, 19)),
+}
+HIDDEN = (1, {2: 3, 3: 4, 4: 5, 5: 7, 6: 12})
 ANY = pl.BlockSpec(memory_space=pl.ANY)
 VMEM = pl.BlockSpec(memory_space=pltpu.VMEM)
 
@@ -30,19 +47,19 @@
     gdown_h, ggate_h, gup_h, gout_h, gin_h, gx_h, out_h, small_v,
     x_h, cot_h, h1_h, bcv_h,
     lt, r, w0, wg, wu, wo, cotc, xc, xo, bcv, bxp, dbuf, dcp, dhoc, dh1s, r1s, gv,
-    xs, xr, s_buf, zs, zr, ob,
+    xs, xr, s_buf, zs, zr, ob, vs, vr, vk,
     kf, cs, cr, ys, yr4, da2f, cs2, ys2, yr2,
     ins, inr, iys, iyr, gxb, halo_s, halo_r, before_s, before_r, small_r,
     xs_sem, xr_sem, zs_sem, zr_sem, ob_sem, c_sem, y_sem, f_sem, c2_sem, y2_sem,
-    i_sem, iy_sem, halo_sem, before_sem, gather_sem, own_sem, w_sem, l_sem, bcv_sem, h1_sem, gx_sem,
-    small_sem,
+    i_sem, iy_sem, halo_sem, before_sem, gather_sem, w_sem, l_sem, bcv_sem, h1_sem, gx_sem,
+    small_sem, v_sem,
 ):
     tokens, chunk, width, ff, local, nseq = dims
     chunks = tokens // chunk
     block = width // (2 * nseq)
     per = block // ROWS
-    units = 4 * per
-    depth = nseq + 1
+    beat = per + 1
+    ticks = 4 * beat
     p = lax.axis_index("dp")
     z = lax.axis_index("seq")
     me = lax.axis_index("mp")
@@ -135,39 +152,76 @@
         gather(which, i, 1).wait()
         gather(which, i, 2).wait()
 
-    own_copies = [
-        load(x_in, x_h.at[me], own_sem.at[0]),
-        load(cot_in, cot_h.at[me], own_sem.at[1]),
-    ]
     for i in range(chunks):
         gather_start(0, i)
         if i == 0:
             gather_start(2, 0)
-    for one in own_copies:
-        one.start()
     wg_load.start()
     wu_load.start()
 
-    def x_copy(u):
-        return pltpu.make_async_remote_copy(
-            src_ref=xs.at[lax.rem(u, 2)], dst_ref=xr.at[lax.rem(u, 4)],
-            send_sem=xs_sem.at[lax.rem(u, 2)], recv_sem=xr_sem.at[lax.rem(u, 4)],
-            device_id=x_dev, device_id_type=MESH,
-        )
-
-    def zs_at(u, step):
-        first = sum(last - one for one in range(step))
-        return first + lax.rem(u, last - step)
-
-    def z_copy(u, way, step):
-        return pltpu.make_async_remote_copy(
-            src_ref=zs.at[way, zs_at(u, step)], dst_ref=zr.at[way, step, lax.rem(u, 3)],
-            send_sem=zs_sem.at[way, step, lax.rem(u, 3)], recv_sem=zr_sem.at[way, step, lax.rem(u, 3)],
-            device_id=dn_dev if way else up_dev, device_id_type=MESH,
-        )
-
-    def sends(way, step):
-        return z >= last - step if way else jnp.logical_and(z <= step, z < last)
+    def on_size(t, f):
+        pl.when(t // beat < 3)(lambda: f(pl.ds(0, ff)))
+        pl.when(t // beat == 3)(lambda: f(pl.ds(0, 4 * local)))
+
+    def place(t):
+        return lax.rem(t, beat)
+
+    def is_first(t):
+        return place(t) == 0
+
+    def is_second(t):
+        return place(t) == SECOND
+
+    def is_plain(t):
+        return jnp.logical_and(place(t) != 0, place(t) != SECOND)
+
+    def row_block(t):
+        plain = place(t) - jnp.where(place(t) > SECOND, 2, 1)
+        return jnp.where(is_plain(t), plain, per - 1)
+
+    def x_number(t):
+        return t // beat * (per - 1) + row_block(t)
+
+    def x_do(t, what):
+        n = x_number(t)
+
+        def f(cols):
+            copy = pltpu.make_async_remote_copy(
+                src_ref=xs.at[lax.rem(n, 3), :, cols], dst_ref=xr.at[lax.rem(n, 5), :, cols],
+                send_sem=xs_sem.at[lax.rem(n, 3)], recv_sem=xr_sem.at[lax.rem(n, 5)],
+                device_id=x_dev, device_id_type=MESH,
+            )
+            getattr(copy, what)()
+
+        on_size(t, f)
+
+    def v_do(t, what):
+        def f(cols):
+            copy = pltpu.make_async_remote_copy(
+                src_ref=vs.at[:, cols], dst_ref=vr.at[:, cols], send_sem=v_sem.at[0], recv_sem=v_sem.at[1],
+                device_id=x_dev, device_id_type=MESH,
+            )
+            getattr(copy, what)()
+
+        on_size(t, f)
+
+    def zs_at(t, step):
+        return 2 * step + lax.rem(t, 2)
+
+    def zr_at(t, step):
+        count = 3 if 0 < step < last - 1 else 4
+        return 3 * step + min(step, 1) + lax.rem(t, count)
+
+    def z_do(t, way, step, what):
+        def f(cols):
+            copy = pltpu.make_async_remote_copy(
+                src_ref=zs.at[way, zs_at(t, step), :, cols], dst_ref=zr.at[way, zr_at(t, step), :, cols],
+                send_sem=zs_sem.at[way, zs_at(t, step)], recv_sem=zr_sem.at[way, zr_at(t, step)],
+                device_id=dn_dev if way else up_dev, device_id_type=MESH,
+            )
+            getattr(copy, what)()
+
+        on_size(t, f)
 
     def receives(way, step):
         if way:
@@ -179,143 +233,202 @@
             return jnp.logical_and(z > 0, z >= last - step)
         return jnp.logical_and(z < last, z <= step)
 
-    def z_step(u, step):
-        sl, slot = lax.rem(u, 6), lax.rem(u, 3)
+    def z_arrived(t, step):
+        for way in (0, 1):
+            @pl.when(receives(way, step))
+            def _(way=way):
+                z_do(t, way, step, "wait_recv")
+
+            @pl.when(can_send(way, step))
+            def _(way=way):
+                z_do(t, way, step, "wait_send")
+
+    def z_step(t, step):
+        sl = lax.rem(t, LAG + 4)
+        if step > 0:
+            z_arrived(t, step - 1)
         for way in (0, 1):
             quarter = z - last + step if way else last - step + z
+            fresh = can_send(way, step)
             if step > 0:
                 @pl.when(jnp.logical_and(receives(way, step - 1), can_send(way, step)))
                 def _(way=way, quarter=quarter):
-                    z_copy(u, way, step - 1).wait_recv()
                     value = s_buf[sl, pl.ds(quarter * ROWS, ROWS), :].astype(F32) + zr[
-                        way, step - 1, slot
+                        way, zr_at(t, step - 1)
                     ].astype(F32)
-                    zs[way, zs_at(u, step)] = value.astype(BF)
-
-                fresh = jnp.logical_and(can_send(way, step), jnp.logical_not(receives(way, step - 1)))
-            else:
-                fresh = can_send(way, step)
+                    zs[way, zs_at(t, step)] = value.astype(BF)
+
+                fresh = jnp.logical_and(fresh, jnp.logical_not(receives(way, step - 1)))
 
             @pl.when(fresh)
             def _(way=way, quarter=quarter):
-                zs[way, zs_at(u, step)] = s_buf[sl, pl.ds(quarter * ROWS, ROWS), :]
-
+                zs[way, zs_at(t, step)] = s_buf[sl, pl.ds(quarter * ROWS, ROWS), :]
+
+        for way in (0, 1):
             @pl.when(can_send(way, step))
             def _(way=way):
-                z_copy(u, way, step).start()
-
-    def compute(u, kind):
-        k = lax.rem(u, per)
-        at = k * ROWS
+                z_do(t, way, step, "start")
+
+    def compute(t, kind):
+        sl = lax.rem(t, LAG + 4)
+        at = row_block(t) * ROWS
+        m = ROWS * nseq
 
         def rows_of(index, half):
-            return [
-                lt[index, pl.ds(pl.multiple_of((half * nseq + s) * block + at, ROWS), ROWS), :]
-                for s in range(nseq)
-            ]
-
-        m = ROWS * nseq
+            rows = [pl.ds(pl.multiple_of((half * nseq + s) * block + at, ROWS), ROWS) for s in range(nseq)]
+            if kind == 3 and index == 1:
+                return [wg[some, pl.ds(0, tokens)] for some in rows]
+            return [lt[index, some, :] for some in rows]
+
         if kind == 3:
-            left = jnp.concatenate(rows_of(0, 1 - p) + rows_of(0, p), 0)
-            out = nn(left, r[0, :, pl.ds(0, local)])
-            xs[lax.rem(u, 2), :, pl.ds(0, local)] = out[:m].astype(BF)
-            s_buf[lax.rem(u, 6), :, pl.ds(0, local)] = out[m:].astype(BF)
-            left = jnp.concatenate(rows_of(1, 1 - p) + rows_of(1, p), 0)
-            out = nn(left, r[0, :, pl.ds(local, 3 * local)])
-            xs[lax.rem(u, 2), :, pl.ds(local, 3 * local)] = out[:m].astype(BF)
-            s_buf[lax.rem(u, 6), :, pl.ds(local, 3 * local)] = out[m:].astype(BF)
+            parts = [(0, 0, 0, local)] + [(1, 0, k * local, local) for k in (1, 2, 3)]
+        elif kind == 0:
+            parts = [(0, 0, lo, n) for lo, n in cuts]
         else:
-            if kind == 0:
-                li, ri = 0, 0
-            else:
-                li, ri = 1, u // per
-            left = jnp.concatenate(rows_of(li, 1 - p) + rows_of(li, p), 0)
-            for lo, n in cuts:
-                out = nn(left, r[ri, :, pl.ds(lo, n)])
-                xs[lax.rem(u, 2), :, pl.ds(lo, n)] = out[:m].astype(BF)
-                s_buf[lax.rem(u, 6), :, pl.ds(lo, n)] = out[m:].astype(BF)
-
-    def out_do(u, what):
-        slot = lax.rem(u, 2)
-        rows = pl.ds(pl.multiple_of(lax.rem(u, per) * ROWS, ROWS), ROWS)
+            parts = [(1, t // beat, lo, n) for lo, n in cuts]
+
+        @pl.when(is_plain(t))
+        def _():
+            slot = lax.rem(x_number(t), 3)
+            left = [jnp.concatenate(rows_of(i, 1 - p) + rows_of(i, p), 0) for i in sorted({q[0] for q in parts})]
+            for i, ri, lo, n in parts:
+                cols = pl.ds(lo, n)
+                out = nn(left[i if len(left) == 2 else 0], r[ri, :, cols])
+                xs[slot, :, cols] = out[:m].astype(BF)
+                s_buf[sl, :, cols] = out[m:].astype(BF)
+            x_do(t, "start")
+
+        @pl.when(jnp.logical_not(is_plain(t)))
+        def _():
+            half = jnp.where(is_first(t), p, 1 - p)
+            left = [jnp.concatenate(rows_of(i, half), 0) for i in sorted({q[0] for q in parts})]
+            for i, ri, lo, n in parts:
+                cols = pl.ds(lo, n)
+                s_buf[sl, :, cols] = nn(left[i if len(left) == 2 else 0], r[ri, :, cols]).astype(BF)
+
+    def out_do(src, t, sems, what):
+        rows = pl.ds(pl.multiple_of(row_block(t) * ROWS, ROWS), ROWS)
         for g, target in enumerate((gdown_h, ggate_h, gup_h)):
-            @pl.when(u // per == g)
+            @pl.when(t // beat == g)
             def _(target=target):
-                getattr(load(ob.at[slot], target.at[rows, :], ob_sem.at[slot]), what)()
-
-        @pl.when(u // per == 3)
-        def _():
-            out = load(ob.at[slot, :, pl.ds(0, local)], gout_h.at[rows, :], ob_sem.at[slot])
-            getattr(out, what)()
+                getattr(load(src, target.at[rows, :], ob_sem.at[sems, 0]), what)()
+
+        @pl.when(t // beat == 3)
+        def _():
+            getattr(load(src.at[:, pl.ds(0, local)], gout_h.at[rows, :], ob_sem.at[sems, 0]), what)()
             for k in range(3):
-                part = ob.at[slot, :, pl.ds((k + 1) * local, local)]
-                one = load(part, gin_h.at[k, rows, :], ob_sem.at[slot + 2 + 2 * k])
-                getattr(one, what)()
-
-    def finish(u):
-        sl, slot = lax.rem(u, 6), lax.rem(u, 3)
-
-        @pl.when(u >= 2)
-        def _():
-            out_do(u - 2, "wait")
-
-        for way in (0, 1):
-            @pl.when(receives(way, last - 1))
-            def _(way=way):
-                z_copy(u, way, last - 1).wait_recv()
-
-        def end(ways):
-            total = s_buf[sl, pl.ds(z * ROWS, ROWS), :].astype(F32)
-            for way in ways:
-                total += zr[way, last - 1, slot].astype(F32)
-            ob[lax.rem(u, 2)] = total.astype(BF)
-
-        pl.when(z == 0)(lambda: end((1,)))
-        pl.when(z == last)(lambda: end((0,)))
-        pl.when(jnp.logical_and(z > 0, z < last))(lambda: end((0, 1)))
-
-        for way in (0, 1):
-            for step in range(last):
-                @pl.when(can_send(way, step))
-                def _(way=way, step=step):
-                    z_copy(u, way, step).wait_send()
-
-        out_do(u, "start")
-
-    def tick(t, kind=None, guard=True):
-        def within(u, f):
-            if guard:
-                @pl.when(jnp.logical_and(u >= 0, u < units))
-                def _():
-                    f()
-            else:
-                f()
-
-        within(t - depth, lambda: finish(t - depth))
-        for step in range(last - 1, 0, -1):
-            within(t - 2 - step, lambda step=step: z_step(t - 2 - step, step))
-
-        def x_in():
-            u = t - 2
-            x_copy(u).wait()
-            sl = lax.rem(u, 6)
-            s_buf[sl] = (s_buf[sl].astype(F32) + xr[lax.rem(u, 4)].astype(F32)).astype(BF)
+                part = src.at[:, pl.ds((k + 1) * local, local)]
+                getattr(load(part, gin_h.at[k, rows, :], ob_sem.at[sems, 1 + k]), what)()
+
+    def plain_out(t, what):
+        slot = lax.rem(x_number(t), 2)
+        out_do(ob.at[slot], t, slot, what)
+
+    def finish(t):
+        sl = lax.rem(t, LAG + 4)
+        z_arrived(t, last - 1)
+
+        def total(then):
+            def end(ways):
+                value = s_buf[sl, pl.ds(z * ROWS, ROWS), :].astype(F32)
+                for way in ways:
+                    value += zr[way, zr_at(t, last - 1)].astype(F32)
+                then(value)
+
+            pl.when(z == 0)(lambda: end((1,)))
+            pl.when(z == last)(lambda: end((0,)))
+            pl.when(jnp.logical_and(z > 0, z < last))(lambda: end((0, 1)))
+
+        @pl.when(is_plain(t))
+        def _():
+            n = x_number(t)
+            before = t - jnp.where(place(t) == per, 2, 3)
+
+            @pl.when(n >= 2)
+            def _():
+                plain_out(before, "wait")
+
+            def put(value):
+                ob[lax.rem(n, 2)] = value.astype(BF)
+
+            total(put)
+            plain_out(t, "start")
+
+        @pl.when(is_first(t))
+        def _():
+            def put(value):
+                vk[...] = value
+
+            total(put)
+
+        @pl.when(is_second(t))
+        def _():
+            def put(value):
+                vs[...] = value.astype(BF)
+
+            total(put)
+            v_do(t, "start")
+
+    def v_end(t):
+        @pl.when(is_second(t))
+        def _():
+            v_do(t, "wait")
+
+            @pl.when(t >= beat)
+            def _():
+                out_do(ob.at[2], t - beat, 2, "wait")
+
+            ob[2] = (vk[...] + vr[...].astype(F32)).astype(BF)
+            out_do(ob.at[2], t, 2, "start")
+
+    def within(t, f):
+        @pl.when(jnp.logical_and(t >= 0, t < ticks))
+        def _():
+            f(t)
+
+    def tick_a(t, full=False):
+        within(t - LAG - 4 - WAIT, v_end)
+        within(t - LAG - 4, finish)
+
+        def x_in(u):
+            @pl.when(is_plain(u))
+            def _():
+                x_do(u, "wait")
+                sl = lax.rem(u, LAG + 4)
+                arrived = xr[lax.rem(x_number(u), 5)].astype(F32)
+                s_buf[sl] = (s_buf[sl].astype(F32) + arrived).astype(BF)
+
             z_step(u, 0)
 
-        within(t - 2, x_in)
-        if kind is not None:
-            compute(t, kind)
-            x_copy(t).start()
-
-    def in_slices(src, to, slot):
-        return [load(src(q), to(q), l_sem.at[slot, q]) for q in range(4)]
-
-    def cot_load(i, slot):
+        within(t - LAG, x_in)
+        if full:
+            pl.when(t // beat == 0)(lambda: compute(t, 0))
+            pl.when(jnp.logical_and(t // beat > 0, t // beat < 3))(lambda: compute(t, 1))
+            pl.when(t // beat == 3)(lambda: compute(t, 3))
+
+    def tick_b(t):
+        within(t - LAG - 1, lambda u: z_step(u, 1))
+
+    def tick_c(t):
+        within(t - LAG - 2, lambda u: z_step(u, 2))
+
+    def in_slices(own, others, to, slot):
+        copies = [load(own, to(me), l_sem.at[slot, 0])]
+        for step in range(1, 4):
+            q = lax.rem(me + step, 4)
+            copies.append(load(others(q), to(q), l_sem.at[slot, step]))
+        return copies
+
+    def cot_load(i):
         return in_slices(
+            cot_in.at[rows_at(i), :],
             lambda q: cot_h.at[q, rows_at(i), :],
-            lambda q: cotc.at[slot, :, pl.ds(q * local, local)],
-            slot,
+            lambda q: cotc.at[:, pl.ds(pl.multiple_of(q * local, 128), local)],
+            0,
         )
+
+    def x_load(i):
+        return in_slices(x_in.at[rows_at(i), :], lambda q: x_h.at[q, rows_at(i), :], lambda q: xc.at[q], 1)
 
     def start(copies):
         for one in copies:
@@ -330,9 +443,6 @@
 
     def bcv_load(i):
         return load(bcv_h.at[:, rows_at(i), :], bcv, l_sem.at[2, 1])
-
-    def x_load(i):
-        return load(x_h.at[:, rows_at(i), :], xc, l_sem.at[2, 2])
 
     def gain(row, q):
         return gv[q, row : row + 1, :]
@@ -373,8 +483,8 @@
 
     def project(i):
         gather_end(0, i)
-        x_load(i).start()
-        x_load(i).wait()
+        start(x_load(i))
+        wait(x_load(i))
         normed_to(lambda q, some: xc[q, some, :], 0)
         value = nn(dhoc[...], w0[pl.ds(0, width), pl.ds(0, 3 * local)])
 
@@ -449,6 +559,15 @@
                 dh1s[i] = h1
         remote(da2f.at[slot, :, c], da2f.at[slot, :, c], f_sem, c_dev, slot).start()
 
+    def cot_turn(i):
+        gather_end(1, i)
+        start(cot_load(i))
+        wait(cot_load(i))
+        at = pl.multiple_of(i * chunk, chunk)
+        for q in range(4):
+            cols = pl.ds(q * local, local)
+            lt[0, cols, pl.ds(at, chunk)] = cotc[:, cols].T
+
     def feed(i):
         slot = lax.rem(i, 2)
         remote(da2f.at[slot, :, c], da2f.at[slot, :, c], f_sem, c_dev, slot).wait()
@@ -457,38 +576,45 @@
                 h1_store(i, slot, pair, core).start()
         normed_to(lambda q, some: da2f[slot, q // 2, q % 2, some, :], 1)
         transposed_to(1, i)
+        rows = rows_at(i)
         for lo, n in cuts:
-            dbuf[0, :, pl.ds(0, n)] = nt(dhoc[...], wg[pl.ds(lo, n), :])
-            dbuf[1, :, pl.ds(0, n)] = nt(dhoc[...], wu[pl.ds(lo, n), :])
+            dbuf[:, pl.ds(0, n)] = nt(dhoc[...], wg[pl.ds(lo, n), :])
+            r[2, rows, pl.ds(lo, n)] = nt(dhoc[...], wu[pl.ds(lo, n), :]).astype(BF)
 
             def by_rows(b, _, lo=lo, n=n):
                 cols = pl.ds(lo, n)
                 here = pl.ds(pl.multiple_of(b * 16, 16), 16)
                 some = pl.ds(pl.multiple_of(i * chunk + b * 16, 16), 16)
-                gate = dbuf[0, here, pl.ds(0, n)]
-                up = dbuf[1, here, pl.ds(0, n)]
+                gate = dbuf[here, pl.ds(0, n)]
+                up = r[2, some, cols].astype(F32)
                 r[0, some, cols] = (gate * jax.nn.sigmoid(gate) * up).astype(BF)
                 r[1, some, cols] = gate.astype(BF)
-                r[2, some, cols] = up.astype(BF)
                 return 0
 
             lax.fori_loop(0, chunk // 16, by_rows, 0)
 
-    def hidden_back(i):
-        slot = lax.rem(i, 2)
-        wait(cot_load(i, slot))
-
-        @pl.when(i + 1 < chunks)
-        def _():
-            start(cot_load(i + 1, 1 - slot))
-
-        for lo, n in cuts:
+    def hidden_back(piece):
+        i = piece // 3
+
+        @pl.when(lax.rem(piece, 3) == 0)
+        def _():
+            wait(cot_load(i))
+
+        for k, cut in enumerate(cuts):
+            pl.when(lax.rem(piece, 3) == k)(functools.partial(hidden_cut, i, *cut))
+
+        @pl.when(jnp.logical_and(lax.rem(piece, 3) == 2, i + 1 < chunks))
+        def _():
+            start(cot_load(i + 1))
+
+    def hidden_cut(i, lo, n):
+        if True:
             cols = pl.ds(lo, n)
-            dbuf[0, :, pl.ds(0, n)] = nt(cotc[slot], w0[pl.ds(lo, n), :])
+            dbuf[:, pl.ds(0, n)] = nt(cotc[...], w0[pl.ds(lo, n), :])
 
             def by_rows(b, _, cols=cols, n=n):
                 some = pl.ds(pl.multiple_of(i * chunk + b * 16, 16), 16)
-                dhid = dbuf[0, pl.ds(pl.multiple_of(b * 16, 16), 16), pl.ds(0, n)]
+                dhid = dbuf[pl.ds(pl.multiple_of(b * 16, 16), 16), pl.ds(0, n)]
                 gate = r[1, some, cols].astype(F32)
                 up = r[2, some, cols].astype(F32)
                 sig = jax.nn.sigmoid(gate)
@@ -518,7 +644,34 @@
             value = nn(r[1, rows, :], wg[:, cols]) + nn(r[2, rows, :], wu[:, cols])
             split_store(pair, value, ck, cs)
         remote(cs, cr.at[slot], c_sem, c_dev, slot).start()
-        start(cot_load(i, slot))
+
+        @pl.when(i == chunks - 1)
+        def _():
+            start(x_whole())
+
+    def x_whole():
+        copies = [load(x_in, wu.at[pl.ds(0, tokens), pl.ds(pl.multiple_of(me * local, 128), local)], l_sem.at[3, 0])]
+        for step in range(1, 4):
+            q = lax.rem(me + step, 4)
+            cols = pl.ds(pl.multiple_of(q * local, 128), local)
+            copies.append(load(x_h.at[q], wu.at[pl.ds(0, tokens), cols], l_sem.at[3, step]))
+        return copies
+
+    def stage_a1(i):
+        @pl.when(i == 0)
+        def _():
+            wait(x_whole())
+
+        at = pl.multiple_of(i * chunk, chunk)
+        normed_to(lambda q, some: wu[pl.ds(at + some.start, 16), pl.ds(q * local, local)], 0)
+        for q in range(4):
+            cols = pl.ds(q * local, local)
+            wg[cols, pl.ds(at, chunk)] = dhoc[:, cols].T
+
+    def stage_loads(i):
+        start(cot_load(i))
+        h1_load(i).start()
+        bcv_load(i).start()
 
     def stage_b(i):
         slot = lax.rem(i, 2)
@@ -531,13 +684,11 @@
         remote(ys.at[slot], yr4.at[slot], y_sem, y_dev, slot).wait()
         da2f[slot, :, c] = (ys[slot].astype(F32) + yr4[slot].astype(F32)).astype(BF)
         remote(da2f.at[slot, :, c], da2f.at[slot, :, c], f_sem, c_dev, slot).start()
-        h1_load(i).start()
-        bcv_load(i).start()
 
     def stage_d(i):
         slot = lax.rem(i, 2)
         remote(da2f.at[slot, :, c], da2f.at[slot, :, c], f_sem, c_dev, slot).wait()
-        wait(cot_load(i, slot))
+        wait(cot_load(i))
         h1_load(i).wait()
         bcv_load(i).wait()
         at = pl.multiple_of(i * chunk, chunk)
@@ -557,7 +708,7 @@
 
             def grad(q, cols, da2):
                 h1 = xc[q, some, :].astype(F32)
-                return cotc[slot, some, cols].astype(F32) + r2 * (da2 * gain(1, q)) - h1 * scale
+                return cotc[some, cols].astype(F32) + r2 * (da2 * gain(1, q)) - h1 * scale
 
             for q in range(4):
                 cols = pl.ds(q * local, local)
@@ -569,7 +720,7 @@
             return 0
 
         lax.fori_loop(0, chunk // 16, by_rows, 0)
-        x_load(i).start()
+        start(x_load(i))
         transposed_to(0, i)
         dmixed = nt(dhoc[...], wo[...])
         c_gate = bcv[1]
@@ -593,7 +744,14 @@
 
     def stage_e(i):
         slot = lax.rem(i, 2)
-        x_load(i).wait()
+
+        @pl.when(i == 0)
+        def _():
+            for k in range(3):
+                wi_load(k).wait()
+            out_copy(chunks - 1).wait()
+
+        wait(x_load(i))
 
         @pl.when(z > 0)
         def _():
@@ -625,10 +783,14 @@
                 ssq += jnp.sum(x * x, -1, keepdims=True)
             split_store(pair, value, ck2, cs2)
         xo[...] = xc[me]
-        ins[...] = jnp.broadcast_to(inner, ins.shape)
-        r1s[slot] = jnp.broadcast_to(lax.rsqrt(ssq / width + EPS), r1s.shape[1:])
+        ins[...] = jnp.broadcast_to(inner, (chunk, 128)).T[:8]
+        r1s[...] = jnp.broadcast_to(lax.rsqrt(ssq / width + EPS), r1s.shape)
         remote(cs2, yr4.at[2 + slot], c2_sem, c_dev, slot).start()
         remote(ins, inr.at[slot], i_sem, c_dev, slot).start()
+
+        @pl.when(i + 1 < chunks)
+        def _():
+            stage_loads(i + 1)
 
     def stage_f(i):
         slot = lax.rem(i, 2)
@@ -648,8 +810,8 @@
         remote(ys2, yr2.at[slot], y2_sem, y_dev, slot).wait()
         remote(iys, iyr.at[slot], iy_sem, y_dev, slot).wait()
         da1 = qk2[...] + yr2[slot].astype(F32)
-        inner = (iys[:, :1] + iyr[slot, :, :1])
-        r1 = r1s[slot, :, :1]
+        inner = jnp.broadcast_to(iys[:1] + iyr[slot, :1], (128, chunk)).T[:, :1]
+        r1 = r1s[:, :1]
         x = xo[...].astype(F32)
         scaled = gain(0, me)
         small_v[0:1, :] += jnp.sum(da1 * x * r1, 0, keepdims=True)
@@ -668,6 +830,11 @@
             split_store(pair, nn(r[0, rows, :], w0[:, cols]), ck2, cs2)
         remote(cs2, yr4.at[2 + lax.rem(i, 2)], c2_sem, c_dev, lax.rem(i, 2)).start()
 
+        @pl.when(i == chunks - 1)
+        def _():
+            for k in range(3):
+                wi_load(k).start()
+
     def out_share(i):
         slot = lax.rem(i, 2)
         remote(cs2, yr4.at[2 + slot], c2_sem, c_dev, slot).wait()
@@ -700,8 +867,6 @@
         wi_load(k).wait()
     wo_load.wait()
     gather_end(2, 0)
-    for one in own_copies:
-        one.wait()
 
     def forward(j, _):
         @pl.when(j < chunks)
@@ -726,10 +891,14 @@
         def _():
             share(j)
 
+        @pl.when(j < chunks - 2)
+        def _():
+            gather_start(1, j)
+
         @pl.when(j == chunks - 1)
         def _():
-            for i in range(chunks):
-                gather_start(1, i)
+            gather_start(1, chunks - 2)
+            gather_start(1, chunks - 1)
 
         @pl.when(j == 2)
         def _():
@@ -738,7 +907,12 @@
 
         @pl.when(j >= 2)
         def _():
+            gather_pass(1, j - 2)
             feed(j - 2)
+
+        @pl.when(j >= 3)
+        def _():
+            cot_turn(j - 3)
 
         return 0
 
@@ -748,87 +922,8 @@
         for core in (0, 1):
             h1_store(chunks - 1, (chunks - 1) % 2, pair, core).wait()
 
-    def cot_pass(i, _):
-        gather_pass(1, i)
-        return 0
-
-    lax.fori_loop(0, chunks, cot_pass, 0)
-
-    def cot_turn(i, _):
-        gather_end(1, i)
-        slot = lax.rem(i, 2)
-        start(cot_load(i, slot))
-        wait(cot_load(i, slot))
-        at = pl.multiple_of(i * chunk, chunk)
-        for q in range(4):
-            cols = pl.ds(q * local, local)
-            lt[0, cols, pl.ds(at, chunk)] = cotc[slot, :, cols].T
-        return 0
-
-    lax.fori_loop(0, chunks, cot_turn, 0)
-    start(cot_load(0, 0))
-
-    def part_one(i, _):
-        tick(i, 0)
-
-        @pl.when(i == 0)
-        def _():
-            wd_load.wait()
-
-        valid(i - 2, out_end)
-        valid(i - 1, out_share)
-        out_start(i)
-        hidden_back(i)
-        return 0
-
-    lax.fori_loop(0, chunks, part_one, 0)
-    for k in range(3):
-        wi_load(k).start()
-
-    def part_two(j, kind):
-        t = chunks + 2 * j
-        tick(t, kind)
-
-        @pl.when(j == 0)
-        def _():
-            out_end(chunks - 2)
-            out_share(chunks - 1)
-
-        valid(j - 3, stage_g)
-        valid(j - 2, stage_e)
-        valid(j - 1, stage_c)
-        valid(j, stage_a)
-        tick(t + 1, kind)
-
-        @pl.when(j == 0)
-        def _():
-            out_end(chunks - 1)
-            out_copy(chunks - 1).wait()
-
-        valid(j, stage_b)
-        valid(j - 1, stage_d)
-        valid(j - 2, stage_f)
-
-    part_two(0, 0)
-    for k in range(3):
-        wi_load(k).wait()
-
-    def loop_rest(j, _):
-        part_two(j, 1)
-        return 0
-
-    lax.fori_loop(1, 1 + (2 * per) // 2, loop_rest, 0)
-
-    def a1_turn(i, _):
-        x_load(i).start()
-        x_load(i).wait()
-        normed_to(lambda q, some: xc[q, some, :], 0)
-        transposed_to(1, i)
-        return 0
-
-    lax.fori_loop(0, chunks, a1_turn, 0)
-    gx_copy(chunks - 1).wait()
-    small_v[4:5, :] = jnp.sum(small_v[8:16, :], 0, keepdims=True)
+    cot_turn(chunks - 1)
+    start(cot_load(0))
 
     def small_x():
         return pltpu.make_async_remote_copy(
@@ -841,8 +936,6 @@
             src_ref=small_r.at[1 + way], dst_ref=small_r.at[3 + way], send_sem=small_sem.at[1 + way, 0],
             recv_sem=small_sem.at[1 + way, 1], device_id=dn_dev if way else up_dev, device_id_type=MESH,
         )
-
-    small_x().start()
 
     def small_step(k):
         @pl.when(k == 0)
@@ -881,21 +974,80 @@
             def _(way=way):
                 small_v[pl.ds(0, 8), :] += small_r[3 + way]
 
-    def part_three(k, _):
-        tick(3 * per + k, 3)
-        small_step(k)
+    def stage_last(i):
+        stage_g(i)
+
+        @pl.when(i == chunks - 1)
+        def _():
+            small_v[4:5, :] = jnp.sum(small_v[8:16, :], 0, keepdims=True)
+            small_x().start()
+
+    order = (
+        ("g", stage_last), ("out_end", out_end), ("out_share", out_share), ("b", stage_b), ("f", stage_f),
+        ("c", stage_c), ("e", stage_e), ("d", stage_d), ("out_start", out_start), ("a", stage_a),
+        ("hidden", None), ("a1", stage_a1),
+    )
+
+    def stages(t, third):
+        for name, f in order:
+            if name == "hidden":
+                if HIDDEN[0] != third:
+                    continue
+                done = 0
+                low = high = 0
+                for at, upto in HIDDEN[1].items():
+                    low = jnp.where(t == at, done, low)
+                    high = jnp.where(t == at, upto, high)
+                    done = upto
+
+                def piece(k, _):
+                    hidden_back(k)
+                    return 0
+
+                lax.fori_loop(low, high, piece, 0)
+            elif PLACES[name][0] == third:
+                where = PLACES[name][1]
+                i = sum(jnp.where(t >= at, 1, 0) for at in where[1:])
+                now = functools.reduce(jnp.logical_or, [t == at for at in where])
+                pl.when(now)(functools.partial(f, i))
+
+    def each_tick(t, _):
+        tick_a(t, True)
+
+        @pl.when(t == 0)
+        def _():
+            wd_load.wait()
+
+        @pl.when(t == beat)
+        def _():
+            stage_loads(0)
+
+        stages(t, 0)
+        tick_b(t)
+        stages(t, 1)
+        tick_c(t)
+        stages(t, 2)
+
+        @pl.when(t > PLACES["g"][1][-1])
+        def _():
+            small_step(t - PLACES["g"][1][-1] - 1)
+
         return 0
 
-    lax.fori_loop(0, per, part_three, 0)
+    lax.fori_loop(0, ticks, each_tick, 0)
+    gx_copy(chunks - 1).wait()
 
     def part_four(k, _):
-        tick(units + k)
+        tick_a(ticks + k)
+        tick_b(ticks + k)
+        tick_c(ticks + k)
         return 0
 
-    lax.fori_loop(0, depth, part_four, 0)
+    lax.fori_loop(0, LAG + 4, part_four, 0)
     small_end()
-    out_do(units - 2, "wait")
-    out_do(units - 1, "wait")
+    plain_out(ticks - 2, "wait")
+    plain_out(ticks - 1, "wait")
+    out_do(ob.at[2], 3 * beat + SECOND, 2, "wait")
 
 
 def block(dims, x_own, cot_own, own, wd, wg, wu, wo, wi):
@@ -914,23 +1066,26 @@
         pltpu.VMEM((ff, width), BF),
         pltpu.VMEM((ff, width), BF),
         pltpu.VMEM((local, width), BF),
-        pltpu.VMEM((2, chunk, width), BF),
+        pltpu.VMEM((chunk, width), BF),
         pltpu.VMEM((4, chunk, local), BF),
         pltpu.VMEM((chunk, local), BF),
         pltpu.VMEM((4, chunk, local), BF),
         pltpu.VMEM((8 + chunk, local), F32),
-        pltpu.VMEM((2, chunk, ff - 2 * third), F32),
+        pltpu.VMEM((chunk, ff - 2 * third), F32),
         pltpu.VMEM((8 + chunk, local), F32),
         pltpu.VMEM((chunk, width), BF),
         pltpu.VMEM((chunks, chunk, local), F32),
-        pltpu.VMEM((2, chunk, 128), F32),
+        pltpu.VMEM((chunk, 128), F32),
         pltpu.VMEM((4, 8, local), F32),
-        pltpu.VMEM((2, m, ff), BF),
-        pltpu.VMEM((4, m, ff), BF),
-        pltpu.VMEM((6, m, ff), BF),
-        pltpu.VMEM((2, last * (last + 1) // 2, ROWS, ff), BF),
-        pltpu.VMEM((2, last, 3, ROWS, ff), BF),
-        pltpu.VMEM((2, ROWS, ff), BF),
+        pltpu.VMEM((3, m, ff), BF),
+        pltpu.VMEM((5, m, ff), BF),
+        pltpu.VMEM((LAG + 4, m, ff), BF),
+        pltpu.VMEM((2, 2 * last, ROWS, ff), BF),
+        pltpu.VMEM((2, 3 * last + 2, ROWS, ff), BF),
+        pltpu.VMEM((3, ROWS, ff), BF),
+        pltpu.VMEM((ROWS, ff), BF),
+        pltpu.VMEM((ROWS, ff), BF),
+        pltpu.VMEM((ROWS, ff), F32),
         pltpu.VMEM((6, chunk, local), F32),
         pltpu.VMEM((2, chunk, local), BF),
         pltpu.VMEM((2, 2, chunk, local), BF),
@@ -940,20 +1095,20 @@
         pltpu.VMEM((2, chunk, local), BF),
         pltpu.VMEM((chunk, local), BF),
         pltpu.VMEM((2, chunk, local), BF),
-        pltpu.VMEM((chunk, 128), F32),
-        pltpu.VMEM((2, chunk, 128), F32),
-        pltpu.VMEM((chunk, 128), F32),
-        pltpu.VMEM((2, chunk, 128), F32),
+        pltpu.VMEM((8, chunk), F32),
+        pltpu.VMEM((2, 8, chunk), F32),
+        pltpu.VMEM((8, chunk), F32),
+        pltpu.VMEM((2, 8, chunk), F32),
         pltpu.VMEM((chunk, local), BF),
         pltpu.VMEM((chunks, 8, local), F32),
         pltpu.VMEM((chunks, 8, local), F32),
         pltpu.VMEM((chunks, 8, local), F32),
         pltpu.VMEM((chunks, 8, local), F32),
         pltpu.VMEM((5, 8, local), F32),
-        DMA((2,)), DMA((4,)), DMA((2, last, 3)), DMA((2, last, 3)), DMA((8,)),
+        DMA((3,)), DMA((5,)), DMA((2, 2 * last)), DMA((2, 3 * last + 2)), DMA((3, 4)),
         DMA((2, 2)), DMA((2, chunks)), DMA((2, 2)), DMA((2, 2)), DMA((2, 2)),
         DMA((2, 2)), DMA((2, 2)), DMA((2, chunks)), DMA((2, chunks)), DMA((3, 2, 3, chunks)),
-        DMA((2,)), DMA((7,)), DMA((3, 4)), DMA(()), DMA((2, 2)), DMA(()), DMA((3, 2)),
+        DMA((7,)), DMA((4, 4)), DMA(()), DMA((2, 2)), DMA(()), DMA((3, 2)), DMA((2,)),
     ]
     return pl.pallas_call(
         functools.partial(block_kernel, dims),

time: 403 us -> 329 us (0.82)
  Pallas kernels: 385 us -> 312 us
    pallas_call x1, Pallas kernels: 385 us -> 312 us  [block(): pl.pallas_call(functools.partial(block_kernel, dims), out_shape=(shape((r...]
where the time goes in v4:
time: 329 us; the launch traced here: 328 us
  Pallas kernels  312 us (95%)
  other arithmetic  9.65 us (3%)
  local copies, waits for them, and re-layouts  5.95 us (2%)
    pallas_call x1, Pallas kernels, block(): pl.pallas_call(functools.partial(block_kernel, dims), out_shape=(shape((r...  312 us

profile of v4, /device:TPU:0, one launch (start us, length us, event | category | flops | bytes accessed | tf_op | source)
XLA Modules:
  0.0 327.9 jit_solution(17380998893443797194)
XLA Ops:
  0.7 0.1 pad.3.clone
  0.7 0.7 broadcast_in_dim.9
  1.4 0.7 broadcast_in_dim.10
  2.1 1.4 maximum_convert_fusion.own_v
  3.4 311.6 %shard_map.177 = (bf16[192,1728]{1,0:T(8,128)(2,1)}, bf16[192,1728]{1,0:T(8,128)(2,1)}, bf16[192,1728]{1,0:T(8,128)(2,1)}, bf16[192,384]{1,0:T(8,128)(2,1)}, bf1...) custom-call(bf16[1024,384]{1,0:T(8,128)(2,1)} %bitcast.16, ...), custom_call_target="tpu_custom_call" | custom-call | tf_op jit(solution)/shard_map/pallas_call | solution.py:1113
  315.1 0.0 copy-start.3
  315.1 0.0 copy-start.2
  315.1 1.4 slice_reduce_fusion
  316.5 1.3 slice.10
  317.8 1.6 convert_bitcast_fusion.2
  319.5 2.0 convert_bitcast_fusion.1
  321.5 0.0 copy-start.1
  321.5 2.3 convert_element_type.32
  323.8 0.0 copy-done.3
  323.8 0.0 copy-start
  323.8 1.2 convert_element_type.33
  325.0 0.0 copy-done.2
  325.0 1.2 convert_bitcast_fusion
  326.1 0.0 copy-done.1
  326.1 0.9 copy.22
  327.0 0.0 copy-done
  327.0 0.9 copy.23
  (1 shorter events, 0.0 us)
Async XLA Ops:
  315.1 8.7 %copy-start.3 = (bf16[192,1728]{1,0:T(8,128)(2,1)S(1)}, bf16[192,1728]{1,0:T(8,128)(2,1)}, u32[]{:S(2)}) copy-start(bf16[192,1728]{1,0:T(8,128)(2,1)} %get-tuple-element.24) | copy-start | bytes 1990660
  315.1 9.9 %copy-start.2 = (bf16[192,1728]{1,0:T(8,128)(2,1)S(1)}, bf16[192,1728]{1,0:T(8,128)(2,1)}, u32[]{:S(2)}) copy-start(bf16[192,1728]{1,0:T(8,128)(2,1)} %get-tuple-element.25) | copy-start | bytes 1990660
  321.5 4.7 %copy-start.1 = (bf16[1024,384]{1,0:T(8,128)(2,1)S(1)}, bf16[1024,384]{1,0:T(8,128)(2,1)}, u32[]{:S(2)}) copy-start(bf16[1024,384]{1,0:T(8,128)(2,1)} %get-tuple-element.18) | copy-start | bytes 2359300
  323.8 3.2 copy-start

commit v5 on v4

--- a/solution.py
+++ b/solution.py
@@ -43,10 +43,10 @@
 
 def block_kernel(
     dims,
-    x_in, cot_in, own_v, wd_h, wg_h, wu_h, wo_h, wi_h,
+    x_in, cot_in, gain_mix_v, gain_ff_v, taps_v, wd_h, wg_h, wu_h, wo_h, wi_h,
     gdown_h, ggate_h, gup_h, gout_h, gin_h, gx_h, out_h, small_v,
     x_h, cot_h, h1_h, bcv_h,
-    lt, r, w0, wg, wu, wo, cotc, xc, xo, bcv, bxp, dbuf, dcp, dhoc, dh1s, r1s, gv,
+    lt, r, w0, wg, wu, wo, cotc, xc, xo, bcv, bxp, dbuf, dcp, dhoc, dh1s, r1s, gv, own_v,
     xs, xr, s_buf, zs, zr, ob, vs, vr, vk,
     kf, cs, cr, ys, yr4, da2f, cs2, ys2, yr2,
     ins, inr, iys, iyr, gxb, halo_s, halo_r, before_s, before_r, small_r,
@@ -94,6 +94,10 @@
     for k in range(3):
         wi_load(k).start()
     wo_load.start()
+    own_v[0:1, :] = gain_mix_v[...].astype(F32).reshape(1, local)
+    own_v[1:2, :] = gain_ff_v[...].astype(F32).reshape(1, local)
+    own_v[2:5, :] = taps_v[...].astype(F32)
+    own_v[5:8, :] = jnp.zeros((3, local), F32)
     gv[me] = own_v[...]
 
     barrier = pltpu.get_barrier_semaphore()
@@ -1050,7 +1054,7 @@
     out_do(ob.at[2], 3 * beat + SECOND, 2, "wait")
 
 
-def block(dims, x_own, cot_own, own, wd, wg, wu, wo, wi):
+def block(dims, x_own, cot_own, gain_mix, gain_ff, taps, wd, wg, wu, wo, wi):
     tokens, chunk, width, ff, local, nseq = dims
     rows = width // (2 * nseq)
     chunks = tokens // chunk
@@ -1077,6 +1081,7 @@
         pltpu.VMEM((chunks, chunk, local), F32),
         pltpu.VMEM((chunk, 128), F32),
         pltpu.VMEM((4, 8, local), F32),
+        pltpu.VMEM((8, local), F32),
         pltpu.VMEM((3, m, ff), BF),
         pltpu.VMEM((5, m, ff), BF),
         pltpu.VMEM((LAG + 4, m, ff), BF),
@@ -1119,13 +1124,13 @@
             shape((4, tokens, local), BF), shape((4, tokens, local), BF),
             shape((4, tokens, local), BF), shape((4, tokens, local), BF),
         ),
-        in_specs=[ANY, ANY, VMEM] + [ANY] * 5,
+        in_specs=[ANY] * 2 + [VMEM] * 3 + [ANY] * 5,
         out_specs=(ANY,) * 7 + (VMEM,) + (ANY,) * 4,
         scratch_shapes=scratch,
         compiler_params=pltpu.CompilerParams(
             collective_id=0, has_side_effects=True, vmem_limit_bytes=63 * 2**20
         ),
-    )(x_own, cot_own, own, wd, wg, wu, wo, wi)
+    )(x_own, cot_own, gain_mix, gain_ff, taps, wd, wg, wu, wo, wi)
 
 
 def shifted(array, axis, by):
@@ -1140,18 +1145,62 @@
     ff = w_down.shape[0]
     tokens = groups * seq_rows
     dims = (tokens, seq_rows, width, ff, local, lax.axis_size("seq"))
-    own = jnp.concatenate(
-        [gain_mix[None], gain_ff[None], kernel, jnp.zeros((3, local), BF)], 0
-    ).astype(F32)
     gdown, ggate, gup, gout, gin, gx, out, small = block(
-        dims, inputs.reshape(tokens, local), cotangent.reshape(tokens, local), own,
+        dims, inputs.reshape(tokens, local), cotangent.reshape(tokens, local), gain_mix, gain_ff, kernel,
         w_down, w_gate.T, w_up.T, w_out, w_in.transpose(1, 0, 2),
     )[:8]
+    gdown, ggate, gup, gout, gin, gx, out, gmix, gtaps, gff = widen(
+        gdown, ggate, gup, gout, gin, gx, out, small
+    )
     whole = (groups, seq_rows, local)
     return (
-        out.reshape(whole), gx.reshape(whole), small[0], gin.transpose(1, 0, 2).astype(F32), small[1:4],
-        gout.T.astype(F32), small[4], ggate.astype(F32), gup.astype(F32), gdown.T.astype(F32),
-    )
+        out.reshape(whole), gx.reshape(whole), gmix, gin.transpose(1, 0, 2), gtaps,
+        gout.T, gff, ggate, gup, gdown.T,
+    )
+
+
+def widen_kernel(*refs):
+    count = 7
+    src, small, dst = refs[:count], refs[count], refs[count + 1 : 2 * count + 1]
+    gmix, gtaps, gff = refs[2 * count + 1 : 2 * count + 4]
+    narrow = refs[2 * count + 4 : 3 * count + 4]
+    wide = refs[3 * count + 4 : 4 * count + 2]
+    in_sem, out_sem = refs[4 * count + 2 :]
+    loads = [pltpu.make_async_copy(src[k], narrow[k], in_sem.at[k]) for k in range(count)]
+    stores = [
+        pltpu.make_async_copy(wide[k] if k < count - 2 else narrow[k], dst[k], out_sem.at[k])
+        for k in range(count)
+    ]
+    for one in loads:
+        one.start()
+    gmix[...] = small[0:1, :].reshape(gmix.shape)
+    gtaps[...] = small[1:4, :]
+    gff[...] = small[4:5, :].reshape(gff.shape)
+    for k in range(count):
+        loads[k].wait()
+        if k < count - 2:
+            wide[k][...] = narrow[k][...].astype(F32)
+        stores[k].start()
+    for one in stores:
+        one.wait()
+
+
+def widen(*arrays):
+    big, small = arrays[:7], arrays[7]
+    local = small.shape[1]
+    shape = jax.ShapeDtypeStruct
+    outs = [shape(a.shape, F32 if k < 5 else BF) for k, a in enumerate(big)]
+    outs += [shape((local,), F32), shape((3, local), F32), shape((local,), F32)]
+    return pl.pallas_call(
+        widen_kernel,
+        out_shape=outs,
+        in_specs=[ANY] * 7 + [VMEM],
+        out_specs=[ANY] * 7 + [VMEM] * 3,
+        scratch_shapes=[pltpu.VMEM(a.shape, BF) for a in big]
+        + [pltpu.VMEM(a.shape, F32) for a in big[:5]]
+        + [pltpu.SemaphoreType.DMA((7,))] * 2,
+        compiler_params=pltpu.CompilerParams(vmem_limit_bytes=63 * 2**20),
+    )(*big, small)
 
 
 def contract_rows(left, right):

time: 329 us -> 318 us (0.967)
  other arithmetic: 9.65 us -> 0 us
  local copies, waits for them, and re-layouts: 5.95 us -> 0 us
  Pallas kernels: 312 us -> 317 us
    convert_element_type x6 -> x0, other arithmetic: 9.65 us -> none  [the longest x1 2.34 us: fused_device(): ggate.astype(F32)]
    pallas_call x0 -> x1, Pallas kernels: none -> 5.49 us  [widen(): pl.pallas_call(widen_kernel, out_shape=outs, in_specs=[ANY] * 7 + [VMEM],...]
where the time goes in v5:
time: 318 us
  Pallas kernels  317 us (100%)
    pallas_call x1, Pallas kernels, block(): pl.pallas_call(functools.partial(block_kernel, dims), out_shape=(shape((r...  312 us

profile of v5, /device:TPU:0, one launch (start us, length us, event | category | flops | bytes accessed | tf_op | source)
XLA Modules:
  0.0 318.0 jit_solution(3623338679254164223)
XLA Ops:
  0.6 311.7 %shard_map.177 = (bf16[192,1728]{1,0:T(8,128)(2,1)}, bf16[192,1728]{1,0:T(8,128)(2,1)}, bf16[192,1728]{1,0:T(8,128)(2,1)}, bf16[192,384]{1,0:T(8,128)(2,1)}, bf1...) custom-call(bf16[1024,384]{1,0:T(8,128)(2,1)} %bitcast.13, ...), custom_call_target="tpu_custom_call" | custom-call | tf_op jit(solution)/shard_map/pallas_call | solution.py:1118
  312.3 5.5 %shard_map.178 = (f32[192,1728]{1,0:T(8,128)}, f32[192,1728]{1,0:T(8,128)}, f32[192,1728]{1,0:T(8,128)}, f32[192,384]{1,0:T(8,128)}, f32[3,192,384]{2,1,0:T(8,12...) custom-call(bf16[192,1728]{1,0:T(8,128)(2,1)} %get-tuple-element.28., ...), custom_call_target="tpu_custom_call" | custom-call | tf_op jit(solution)/shard_map/pallas_call | solution.py:1194

commit v6 on v5

--- a/solution.py
+++ b/solution.py
@@ -45,14 +45,14 @@
     dims,
     x_in, cot_in, gain_mix_v, gain_ff_v, taps_v, wd_h, wg_h, wu_h, wo_h, wi_h,
     gdown_h, ggate_h, gup_h, gout_h, gin_h, gx_h, out_h, small_v,
-    x_h, cot_h, h1_h, bcv_h,
-    lt, r, w0, wg, wu, wo, cotc, xc, xo, bcv, bxp, dbuf, dcp, dhoc, dh1s, r1s, gv, own_v,
+    x_h, cot_h, h1_h, bcv_h, woy_h,
+    lt, r, w0, wg, wu, wof, cotc, xc, xo, bcv, bxp, dbuf, dcp, dhoc, dh1s, r1s, gv, own_v,
     xs, xr, s_buf, zs, zr, ob, vs, vr, vk,
     kf, cs, cr, ys, yr4, da2f, cs2, ys2, yr2,
     ins, inr, iys, iyr, gxb, halo_s, halo_r, before_s, before_r, small_r,
     xs_sem, xr_sem, zs_sem, zr_sem, ob_sem, c_sem, y_sem, f_sem, c2_sem, y2_sem,
     i_sem, iy_sem, halo_sem, before_sem, gather_sem, w_sem, l_sem, bcv_sem, h1_sem, gx_sem,
-    small_sem, v_sem,
+    small_sem, v_sem, wy_sem, wx_sem, wz_sem, wc_sem, wl_sem,
 ):
     tokens, chunk, width, ff, local, nseq = dims
     chunks = tokens // chunk
@@ -90,10 +90,11 @@
     wd_load = load(wd_h, w0, w_sem.at[3])
     wg_load = load(wg_h, wg, w_sem.at[4])
     wu_load = load(wu_h, wu, w_sem.at[5])
-    wo_load = load(wo_h, wo, w_sem.at[6])
+    def wo_load(q):
+        return load(wo_h.at[:, pl.ds(q * local, local)], wof.at[0, pl.ds(q * local, local), :], wl_sem.at[q])
+
     for k in range(3):
         wi_load(k).start()
-    wo_load.start()
     own_v[0:1, :] = gain_mix_v[...].astype(F32).reshape(1, local)
     own_v[1:2, :] = gain_ff_v[...].astype(F32).reshape(1, local)
     own_v[2:5, :] = taps_v[...].astype(F32)
@@ -120,16 +121,88 @@
     def rows_at(i):
         return pl.ds(pl.multiple_of(i * chunk, chunk), chunk)
 
+    def mixed_at(q, i):
+        return r.at[0, rows_at(i), pl.ds(pl.multiple_of(q * local, 128), local)]
+
+    share = local // (2 * nseq)
+
+    def piece(zz):
+        return woy_h.at[pl.ds(pl.multiple_of((p * nseq + zz) * share, 16), share), :]
+
+    def wy():
+        mine = wo_h.at[pl.ds(pl.multiple_of((p * nseq + z) * share, 16), share), :]
+        return pltpu.make_async_remote_copy(
+            src_ref=mine, dst_ref=piece(z), send_sem=wy_sem.at[0], recv_sem=wy_sem.at[1],
+            device_id=y_dev, device_id_type=MESH,
+        )
+
+    def wx(zz):
+        return remote(piece(zz), piece(zz), wx_sem, x_dev, zz)
+
+    def wz(way, step):
+        part = piece(z + step if way else z - step)
+        return pltpu.make_async_remote_copy(
+            src_ref=part, dst_ref=part, send_sem=wz_sem.at[0, way, step], recv_sem=wz_sem.at[1, way, step],
+            device_id=dn_dev if way else up_dev, device_id_type=MESH,
+        )
+
+    def wz_sends(way, step):
+        return jnp.logical_and(z > 0, z + step <= last) if way else jnp.logical_and(z < last, z >= step)
+
+    def wz_receives(way, step):
+        return z + 1 + step <= last if way else z >= step + 1
+
+    def wo_step(step):
+        if step == 0:
+            wy().wait_recv()
+            wx(z).start()
+        for way in (0, 1):
+            if step > 0:
+                @pl.when(wz_receives(way, step - 1))
+                def _(way=way):
+                    wz(way, step - 1).wait_recv()
+                    wx(z + step if way else z - step).start()
+            if step < last:
+                @pl.when(wz_sends(way, step))
+                def _(way=way):
+                    wz(way, step).start()
+
+    def wo_columns(src, q, kind):
+        rows = pl.ds(pl.multiple_of(q * local, 128), local)
+        for pair in (0, 1):
+            cols = pl.ds(pl.multiple_of((2 * pair + c) * local, 128), local)
+            yield load(src.at[:, cols], wof.at[pair, rows, :], wl_sem.at[2 * kind + pair])
+            cols = pl.ds(pl.multiple_of((2 * pair + 1 - c) * local, 128), local)
+            yield remote(src.at[:, cols], wof.at[pair, rows, :], wc_sem, c_dev, 2 * kind + pair)
+
+    def wo_end():
+        wy().wait_send()
+        for zz in range(nseq):
+            wx(zz).wait()
+        for way in (0, 1):
+            for step in range(last):
+                @pl.when(wz_sends(way, step))
+                def _(way=way, step=step):
+                    wz(way, step).wait_send()
+        for one in wo_columns(woy_h, (1 - y) * 2 + c, 1):
+            one.start()
+
     def gather(which, i, leg):
         if which == 2:
             src = mine = own_v
             dst = gv
             at = (2, 0)
+        elif which == 3:
+            mine = mixed_at(me, i)
+            at = (3, i)
         else:
             src, dst = (x_in, x_h) if which == 0 else (cot_in, cot_h)
             mine = src.at[rows_at(i), :]
             at = (which, i)
-        slot = (lambda q: dst.at[q]) if which == 2 else (lambda q: dst.at[q, rows_at(i), :])
+        if which == 3:
+            slot = lambda q: mixed_at(q, i)
+        else:
+            slot = (lambda q: dst.at[q]) if which == 2 else (lambda q: dst.at[q, rows_at(i), :])
         sems = [gather_sem.at[leg, way, at[0], at[1]] for way in (0, 1)]
         if leg == 0:
             pair, where = (mine, slot(me)), y_dev
@@ -156,10 +229,12 @@
         gather(which, i, 1).wait()
         gather(which, i, 2).wait()
 
+    gather(0, 0, 0).start()
+    gather_start(2, 0)
     for i in range(chunks):
-        gather_start(0, i)
-        if i == 0:
-            gather_start(2, 0)
+        gather(0, i, 1).start()
+    for one in wo_columns(wo_h, me, 0):
+        one.start()
     wg_load.start()
     wu_load.start()
 
@@ -451,16 +526,16 @@
     def gain(row, q):
         return gv[q, row : row + 1, :]
 
-    def by_sixteen(f):
+    def by_rows_of(count, f):
         def body(b, _):
-            f(pl.ds(pl.multiple_of(b * 16, 16), 16))
+            f(pl.ds(pl.multiple_of(b * count, count), count))
             return 0
 
-        lax.fori_loop(0, chunk // 16, body, 0)
+        lax.fori_loop(0, chunk // count, body, 0)
 
     def normed_to(src, row, after=None):
         def f(some):
-            ssq = jnp.zeros((16, local), F32)
+            ssq = jnp.zeros((64, local), F32)
             for q in range(4):
                 values = src(q, some).astype(F32)
                 ssq += values * values
@@ -468,7 +543,7 @@
             for q in range(4):
                 dhoc[some, pl.ds(q * local, local)] = (src(q, some).astype(F32) * scale * gain(row, q)).astype(BF)
 
-        by_sixteen(f)
+        by_rows_of(64, f)
 
     def transposed_to(index, i):
         at = pl.multiple_of(i * chunk, chunk)
@@ -486,8 +561,6 @@
         return load(da2f.at[slot, pair, core], h1_h.at[2 * pair + core, rows_at(i), :], h1_sem.at[pair, core])
 
     def project(i):
-        gather_end(0, i)
-        start(x_load(i))
         wait(x_load(i))
         normed_to(lambda q, some: xc[q, some, :], 0)
         value = nn(dhoc[...], w0[pl.ds(0, width), pl.ds(0, 3 * local)])
@@ -515,8 +588,6 @@
         return sum(own_v[2 + k : 3 + k, :] * shifts[k] for k in range(3)), shifts
 
     def mix(i):
-        slot = lax.rem(i, 2)
-
         @pl.when(z < last)
         def _():
             before_copy(i).wait_send()
@@ -531,22 +602,19 @@
 
         bxp[pl.ds(0, 8), :] = before_r[i]
         mixed = (dcp[pl.ds(0, chunk), :] * conv_of()[0]).astype(BF)
-        for pair in (0, 1):
-            split_store(pair, nn(mixed, wo[:, pl.ds(pair * 2 * local, 2 * local)]), ck, cs)
-        remote(cs, cr.at[slot], c_sem, c_dev, slot).start()
-
-    def share(i):
-        slot = lax.rem(i, 2)
-        remote(cs, cr.at[slot], c_sem, c_dev, slot).wait()
-        for pair in (0, 1):
-            total = ck[pair] + cr[slot, pair].astype(F32)
-            kf[2 + 2 * slot + pair] = total + xc[2 * pair + c].astype(F32)
-            ys[slot, pair] = total.astype(BF)
-        remote(ys.at[slot], yr4.at[i], y_sem, y_dev, i).start()
+        r[0, rows_at(i), pl.ds(pl.multiple_of(me * local, 128), local)] = mixed
+        gather_start(3, i)
+
+    def x_two(i):
+        return [
+            load(x_in.at[rows_at(i), :], cs2.at[y], l_sem.at[2, 2]),
+            load(x_h.at[(1 - y) * 2 + c, rows_at(i), :], cs2.at[1 - y], l_sem.at[2, 3]),
+        ]
 
     def residual(i):
         slot = lax.rem(i, 2)
-        remote(ys.at[slot], yr4.at[i], y_sem, y_dev, i).wait()
+        gather_end(3, i)
+        wait(x_two(i))
 
         @pl.when(i >= 1)
         def _():
@@ -555,13 +623,17 @@
                     h1_store(i - 1, 1 - slot, pair, core).wait()
 
         for pair in (0, 1):
-            h1 = kf[2 + 2 * slot + pair] + yr4[i, pair].astype(F32)
+            h1 = nn(r[0, rows_at(i), pl.ds(0, width)], wof[pair]) + cs2[pair].astype(F32)
             da2f[slot, pair, c] = h1.astype(BF)
 
             @pl.when(y == pair)
             def _(h1=h1):
                 dh1s[i] = h1
         remote(da2f.at[slot, :, c], da2f.at[slot, :, c], f_sem, c_dev, slot).start()
+
+        @pl.when(i + 1 < chunks)
+        def _():
+            start(x_two(i + 1))
 
     def cot_turn(i):
         gather_end(1, i)
@@ -587,15 +659,15 @@
 
             def by_rows(b, _, lo=lo, n=n):
                 cols = pl.ds(lo, n)
-                here = pl.ds(pl.multiple_of(b * 16, 16), 16)
-                some = pl.ds(pl.multiple_of(i * chunk + b * 16, 16), 16)
+                here = pl.ds(pl.multiple_of(b * 64, 64), 64)
+                some = pl.ds(pl.multiple_of(i * chunk + b * 64, 64), 64)
                 gate = dbuf[here, pl.ds(0, n)]
                 up = r[2, some, cols].astype(F32)
                 r[0, some, cols] = (gate * jax.nn.sigmoid(gate) * up).astype(BF)
                 r[1, some, cols] = gate.astype(BF)
                 return 0
 
-            lax.fori_loop(0, chunk // 16, by_rows, 0)
+            lax.fori_loop(0, chunk // 64, by_rows, 0)
 
     def hidden_back(piece):
         i = piece // 3
@@ -617,8 +689,8 @@
             dbuf[:, pl.ds(0, n)] = nt(cotc[...], w0[pl.ds(lo, n), :])
 
             def by_rows(b, _, cols=cols, n=n):
-                some = pl.ds(pl.multiple_of(i * chunk + b * 16, 16), 16)
-                dhid = dbuf[pl.ds(pl.multiple_of(b * 16, 16), 16), pl.ds(0, n)]
+                some = pl.ds(pl.multiple_of(i * chunk + b * 32, 32), 32)
+                dhid = dbuf[pl.ds(pl.multiple_of(b * 32, 32), 32), pl.ds(0, n)]
                 gate = r[1, some, cols].astype(F32)
                 up = r[2, some, cols].astype(F32)
                 sig = jax.nn.sigmoid(gate)
@@ -626,7 +698,7 @@
                 r[2, some, cols] = (dhid * gate * sig).astype(BF)
                 return 0
 
-            lax.fori_loop(0, chunk // 16, by_rows, 0)
+            lax.fori_loop(0, chunk // 32, by_rows, 0)
 
     def split_store(pair, value, keep, send):
         for side in (0, 1):
@@ -667,7 +739,7 @@
             wait(x_whole())
 
         at = pl.multiple_of(i * chunk, chunk)
-        normed_to(lambda q, some: wu[pl.ds(at + some.start, 16), pl.ds(q * local, local)], 0)
+        normed_to(lambda q, some: wu[pl.ds(at + some.start, some.size), pl.ds(q * local, local)], 0)
         for q in range(4):
             cols = pl.ds(q * local, local)
             wg[cols, pl.ds(at, chunk)] = dhoc[:, cols].T
@@ -680,13 +752,13 @@
     def stage_b(i):
         slot = lax.rem(i, 2)
         remote(cs, cr.at[slot], c_sem, c_dev, slot).wait()
-        ys[slot] = (ck[...] + cr[slot].astype(F32)).astype(BF)
-        remote(ys.at[slot], yr4.at[slot], y_sem, y_dev, slot).start()
+        ys[...] = (ck[...] + cr[slot].astype(F32)).astype(BF)
+        remote(ys, yr4.at[slot], y_sem, y_dev, slot).start()
 
     def stage_c(i):
         slot = lax.rem(i, 2)
-        remote(ys.at[slot], yr4.at[slot], y_sem, y_dev, slot).wait()
-        da2f[slot, :, c] = (ys[slot].astype(F32) + yr4[slot].astype(F32)).astype(BF)
+        remote(ys, yr4.at[slot], y_sem, y_dev, slot).wait()
+        da2f[slot, :, c] = (ys[...].astype(F32) + yr4[slot].astype(F32)).astype(BF)
         remote(da2f.at[slot, :, c], da2f.at[slot, :, c], f_sem, c_dev, slot).start()
 
     def stage_d(i):
@@ -699,9 +771,9 @@
         own = pl.ds(pl.multiple_of(me * local, 128), local)
 
         def by_rows(b, _):
-            some = pl.ds(pl.multiple_of(b * 16, 16), 16)
-            ssq = jnp.zeros((16, local), F32)
-            inner = jnp.zeros((16, local), F32)
+            some = pl.ds(pl.multiple_of(b * 64, 64), 64)
+            ssq = jnp.zeros((64, local), F32)
+            inner = jnp.zeros((64, local), F32)
             for q in range(4):
                 cols = pl.ds(q * local, local)
                 h1 = xc[q, some, :].astype(F32)
@@ -720,13 +792,21 @@
             da2 = da2f[slot, y, c, some, :].astype(F32)
             dh1s[i, some, :] = grad(me, own, da2)
             terms = da2 * xc[me, some, :].astype(F32) * r2
-            small_v[pl.ds(8, 8), :] += terms[:8] + terms[8:]
+            small_v[pl.ds(8, 8), :] += sum(terms[8 * k : 8 * k + 8] for k in range(8))
             return 0
 
-        lax.fori_loop(0, chunk // 16, by_rows, 0)
+        lax.fori_loop(0, chunk // 64, by_rows, 0)
         start(x_load(i))
         transposed_to(0, i)
-        dmixed = nt(dhoc[...], wo[...])
+        @pl.when(i == 0)
+        def _():
+            for q in range(4):
+                wo_load(q).wait()
+
+        dmixed = jnp.zeros((chunk, local), F32)
+        for q in range(4):
+            cols = pl.ds(q * local, local)
+            dmixed += nt(dhoc[:, cols], wof[0, cols, :])
         c_gate = bcv[1]
         bxp[pl.ds(0, 8), :] = before_r[i]
         bxp[pl.ds(8, chunk), :] = bcv[3].astype(F32)
@@ -866,61 +946,107 @@
             f(i)
 
     gather_pass(0, 0)
+    gather(0, 1, 0).start()
+    wy().start()
     gather_pass(2, 0)
     for k in range(3):
         wi_load(k).wait()
-    wo_load.wait()
     gather_end(2, 0)
+
+    gather_end(0, 0)
+    start(x_load(0))
 
     def forward(j, _):
         @pl.when(j < chunks)
         def _():
             project(j)
 
-            @pl.when(j + 1 < chunks)
-            def _():
-                gather_pass(0, j + 1)
-
-            mix(j)
-
-        @pl.when(j == chunks - 1)
-        def _():
-            wd_load.start()
-
-        @pl.when(j >= 2)
-        def _():
-            residual(j - 2)
-
-        @pl.when(j < chunks)
-        def _():
-            share(j)
-
-        @pl.when(j < chunks - 2)
-        def _():
-            gather_start(1, j)
-
-        @pl.when(j == chunks - 1)
-        def _():
-            gather_start(1, chunks - 2)
-            gather_start(1, chunks - 1)
-
-        @pl.when(j == 2)
+        @pl.when(j + 1 < chunks)
+        def _():
+            gather_pass(0, j + 1)
+
+        @pl.when(j + 2 < chunks)
+        def _():
+            gather(0, j + 2, 0).start()
+
+        pl.when(j == 0)(lambda: wo_step(0))
+        pl.when(j == 1)(lambda: wo_step(2))
+
+        @pl.when(j == chunks)
+        def _():
+            cot_turn(0)
+
+        @pl.when(j == chunks + 1)
+        def _():
+            cot_turn(1)
+
+        @pl.when(j == chunks + 2)
+        def _():
+            cot_turn(2)
+
+        @pl.when(j == 3)
         def _():
             wg_load.wait()
             wu_load.wait()
 
-        @pl.when(j >= 2)
-        def _():
-            gather_pass(1, j - 2)
-            feed(j - 2)
-
         @pl.when(j >= 3)
         def _():
-            cot_turn(j - 3)
+            feed(j - 3)
+
+        @pl.when(j < chunks)
+        def _():
+            mix(j)
+
+        @pl.when(j + 1 < chunks)
+        def _():
+            gather_end(0, j + 1)
+            start(x_load(j + 1))
+
+        pl.when(j == 0)(lambda: wo_step(1))
+        pl.when(j == 1)(lambda: wo_step(3))
+
+        @pl.when(jnp.logical_and(j > 0, j < chunks))
+        def _():
+            gather_pass(3, j - 1)
+
+        @pl.when(j == 2)
+        def _():
+            wo_end()
+            start(x_two(0))
+            for i in range(chunks):
+                gather(1, i, 1).start()
+            for i in range(2):
+                gather(1, i, 0).start()
+            for kind, src in ((0, wo_h), (1, woy_h)):
+                for one in wo_columns(src, me if kind == 0 else (1 - y) * 2 + c, kind):
+                    one.wait()
+
+        @pl.when(j == chunks - 1)
+        def _():
+            wd_load.start()
+
+        @pl.when(jnp.logical_and(j >= 2, j < chunks + 2))
+        def _():
+            residual(j - 2)
+
+        @pl.when(j == 3)
+        def _():
+            for k in range(2):
+                gather_pass(1, k)
+            for k in range(2, chunks):
+                gather(1, k, 0).start()
+
+        @pl.when(j == chunks)
+        def _():
+            gather_pass(3, chunks - 1)
+            for k in range(2, chunks):
+                gather_pass(1, k)
 
         return 0
 
-    lax.fori_loop(0, chunks + 2, forward, 0)
+    lax.fori_loop(0, chunks + 3, forward, 0)
+    for q in range(4):
+        wo_load(q).start()
     bcv_store(chunks - 1).wait()
     for pair in (0, 1):
         for core in (0, 1):
@@ -1069,7 +1195,7 @@
         pltpu.VMEM((ff, width), BF),
         pltpu.VMEM((ff, width), BF),
         pltpu.VMEM((ff, width), BF),
-        pltpu.VMEM((local, width), BF),
+        pltpu.VMEM((2, width, local), BF),
         pltpu.VMEM((chunk, width), BF),
         pltpu.VMEM((4, chunk, local), BF),
         pltpu.VMEM((chunk, local), BF),
@@ -1091,10 +1217,10 @@
         pltpu.VMEM((ROWS, ff), BF),
         pltpu.VMEM((ROWS, ff), BF),
         pltpu.VMEM((ROWS, ff), F32),
-        pltpu.VMEM((6, chunk, local), F32),
+        pltpu.VMEM((5, chunk, local), F32),
         pltpu.VMEM((2, chunk, local), BF),
         pltpu.VMEM((2, 2, chunk, local), BF),
-        pltpu.VMEM((2, 2, chunk, local), BF),
+        pltpu.VMEM((2, chunk, local), BF),
         pltpu.VMEM((4, 2, chunk, local), BF),
         pltpu.VMEM((2, 2, 2, chunk, local), BF),
         pltpu.VMEM((2, chunk, local), BF),
@@ -1112,8 +1238,8 @@
         pltpu.VMEM((5, 8, local), F32),
         DMA((3,)), DMA((5,)), DMA((2, 2 * last)), DMA((2, 3 * last + 2)), DMA((3, 4)),
         DMA((2, 2)), DMA((2, chunks)), DMA((2, 2)), DMA((2, 2)), DMA((2, 2)),
-        DMA((2, 2)), DMA((2, 2)), DMA((2, chunks)), DMA((2, chunks)), DMA((3, 2, 3, chunks)),
-        DMA((7,)), DMA((4, 4)), DMA(()), DMA((2, 2)), DMA(()), DMA((3, 2)), DMA((2,)),
+        DMA((2, 2)), DMA((2, 2)), DMA((2, chunks)), DMA((2, chunks)), DMA((3, 2, 4, chunks)),
+        DMA((7,)), DMA((4, 4)), DMA(()), DMA((2, 2)), DMA(()), DMA((3, 2)), DMA((2,)), DMA((2,)), DMA((2, nseq)), DMA((2, 2, last)), DMA((2, 4)), DMA((4,)),
     ]
     return pl.pallas_call(
         functools.partial(block_kernel, dims),
@@ -1122,10 +1248,10 @@
             shape((rows, local), BF), shape((3, rows, local), BF),
             shape((tokens, local), BF), shape((tokens, local), BF), shape((16, local), F32),
             shape((4, tokens, local), BF), shape((4, tokens, local), BF),
-            shape((4, tokens, local), BF), shape((4, tokens, local), BF),
+            shape((4, tokens, local), BF), shape((4, tokens, local), BF), shape((local, width), BF),
         ),
         in_specs=[ANY] * 2 + [VMEM] * 3 + [ANY] * 5,
-        out_specs=(ANY,) * 7 + (VMEM,) + (ANY,) * 4,
+        out_specs=(ANY,) * 7 + (VMEM,) + (ANY,) * 5,
         scratch_shapes=scratch,
         compiler_params=pltpu.CompilerParams(
             collective_id=0, has_side_effects=True, vmem_limit_bytes=63 * 2**20

time: 318 us -> 311 us (0.978)
  Pallas kernels: 317 us -> 310 us
    pallas_call x1, Pallas kernels: 312 us -> 305 us  [block(): pl.pallas_call(functools.partial(block_kernel, dims), out_shape=(shape((r...]
where the time goes in v6:
time: 311 us
  Pallas kernels  310 us (100%)
    pallas_call x1, Pallas kernels, block(): pl.pallas_call(functools.partial(block_kernel, dims), out_shape=(shape((r...  305 us

profile of v6, /device:TPU:0, one launch (start us, length us, event | category | flops | bytes accessed | tf_op | source)
XLA Modules:
  0.0 310.9 jit_solution(780336286859763374)
XLA Ops:
  0.6 304.6 %shard_map.177 = (bf16[192,1728]{1,0:T(8,128)(2,1)}, bf16[192,1728]{1,0:T(8,128)(2,1)}, bf16[192,1728]{1,0:T(8,128)(2,1)}, bf16[192,384]{1,0:T(8,128)(2,1)}, bf1...) custom-call(bf16[1024,384]{1,0:T(8,128)(2,1)} %bitcast.13, ...), custom_call_target="tpu_custom_call" | custom-call | tf_op jit(solution)/shard_map/pallas_call | solution.py:1244
  305.2 5.5 %shard_map.178 = (f32[192,1728]{1,0:T(8,128)}, f32[192,1728]{1,0:T(8,128)}, f32[192,1728]{1,0:T(8,128)}, f32[192,384]{1,0:T(8,128)}, f32[3,192,384]{2,1,0:T(8,12...) custom-call(bf16[192,1728]{1,0:T(8,128)(2,1)} %get-tuple-element.28., ...), custom_call_target="tpu_custom_call" | custom-call | tf_op jit(solution)/shard_map/pallas_call | solution.py:1320

commit v7 on v6

--- a/solution.py
+++ b/solution.py
@@ -635,9 +635,11 @@
         def _():
             start(x_two(i + 1))
 
-    def cot_turn(i):
+    def cot_fetch(i):
         gather_end(1, i)
         start(cot_load(i))
+
+    def cot_turn(i):
         wait(cot_load(i))
         at = pl.multiple_of(i * chunk, chunk)
         for q in range(4):
@@ -956,94 +958,49 @@
     gather_end(0, 0)
     start(x_load(0))
 
+    def when(now, *calls):
+        @pl.when(now)
+        def _():
+            for f in calls:
+                f()
+
+    def weights_there():
+        wg_load.wait()
+        wu_load.wait()
+
+    def wo_there():
+        wo_end()
+        for kind, src in ((0, wo_h), (1, woy_h)):
+            for one in wo_columns(src, me if kind == 0 else (1 - y) * 2 + c, kind):
+                one.wait()
+
     def forward(j, _):
-        @pl.when(j < chunks)
-        def _():
-            project(j)
-
-        @pl.when(j + 1 < chunks)
-        def _():
-            gather_pass(0, j + 1)
-
-        @pl.when(j + 2 < chunks)
-        def _():
-            gather(0, j + 2, 0).start()
-
-        pl.when(j == 0)(lambda: wo_step(0))
-        pl.when(j == 1)(lambda: wo_step(2))
-
-        @pl.when(j == chunks)
-        def _():
-            cot_turn(0)
-
-        @pl.when(j == chunks + 1)
-        def _():
-            cot_turn(1)
-
-        @pl.when(j == chunks + 2)
-        def _():
-            cot_turn(2)
-
-        @pl.when(j == 3)
-        def _():
-            wg_load.wait()
-            wu_load.wait()
-
-        @pl.when(j >= 3)
-        def _():
-            feed(j - 3)
-
-        @pl.when(j < chunks)
-        def _():
-            mix(j)
-
-        @pl.when(j + 1 < chunks)
-        def _():
-            gather_end(0, j + 1)
-            start(x_load(j + 1))
-
-        pl.when(j == 0)(lambda: wo_step(1))
-        pl.when(j == 1)(lambda: wo_step(3))
-
-        @pl.when(jnp.logical_and(j > 0, j < chunks))
-        def _():
-            gather_pass(3, j - 1)
-
-        @pl.when(j == 2)
-        def _():
-            wo_end()
-            start(x_two(0))
-            for i in range(chunks):
-                gather(1, i, 1).start()
-            for i in range(2):
-                gather(1, i, 0).start()
-            for kind, src in ((0, wo_h), (1, woy_h)):
-                for one in wo_columns(src, me if kind == 0 else (1 - y) * 2 + c, kind):
-                    one.wait()
-
-        @pl.when(j == chunks - 1)
-        def _():
-            wd_load.start()
-
-        @pl.when(jnp.logical_and(j >= 2, j < chunks + 2))
-        def _():
-            residual(j - 2)
-
-        @pl.when(j == 3)
-        def _():
-            for k in range(2):
-                gather_pass(1, k)
-            for k in range(2, chunks):
-                gather(1, k, 0).start()
-
-        @pl.when(j == chunks)
-        def _():
-            gather_pass(3, chunks - 1)
-            for k in range(2, chunks):
-                gather_pass(1, k)
-
+        when(j < chunks, lambda: project(j))
+        when(j + 1 < chunks, lambda: gather_pass(0, j + 1))
+        when(j + 2 < chunks, lambda: gather(0, j + 2, 0).start())
+        when(j == 0, lambda: wo_step(0))
+        when(j == 1, lambda: wo_step(1))
+        when(j == 2, lambda: wo_step(3))
+        when(j == 3, wo_there, weights_there)
+        when(j >= 3, lambda: residual(j - 3))
+        when(j < chunks, lambda: mix(j))
+        when(j + 1 < chunks, lambda: gather_end(0, j + 1), lambda: start(x_load(j + 1)))
+        when(j == 1, lambda: wo_step(2))
+        when(j == 2, lambda: start(x_two(0)), lambda: gather(1, 0, 0).start(), lambda: gather(1, 1, 0).start())
+        when(jnp.logical_and(j > 0, j < chunks), lambda: gather_pass(3, j - 1))
+        when(j > 3, lambda: cot_turn(j - 4))
+        when(j == 5, *[functools.partial(gather_pass, 1, k) for k in range(2, chunks)])
+        when(j > 3, lambda: cot_fetch(j - 3))
+        when(j >= 3, lambda: feed(j - 3))
+        when(
+            j == 3, wd_load.start, *[functools.partial(gather_pass, 1, k) for k in range(2)],
+            *[gather(1, k, 0).start for k in range(2, chunks)], lambda: cot_fetch(0),
+        )
+        when(j == 4, lambda: gather_pass(3, chunks - 1))
         return 0
 
+    for i in range(chunks):
+        gather(1, i, 1).start()
     lax.fori_loop(0, chunks + 3, forward, 0)
     for q in range(4):
         wo_load(q).start()

time: 311 us -> 303 us (0.974)
  Pallas kernels: 310 us -> 302 us
    pallas_call x1, Pallas kernels: 305 us -> 297 us  [block(): pl.pallas_call(functools.partial(block_kernel, dims), out_shape=(shape((r...]
where the time goes in v7:
time: 303 us
  Pallas kernels  302 us (100%)
    pallas_call x1, Pallas kernels, block(): pl.pallas_call(functools.partial(block_kernel, dims), out_shape=(shape((r...  297 us

profile of v7, /device:TPU:0, one launch (start us, length us, event | category | flops | bytes accessed | tf_op | source)
XLA Modules:
  0.0 303.0 jit_solution(5773266061792211231)
XLA Ops:
  0.6 296.7 %shard_map.177 = (bf16[192,1728]{1,0:T(8,128)(2,1)}, bf16[192,1728]{1,0:T(8,128)(2,1)}, bf16[192,1728]{1,0:T(8,128)(2,1)}, bf16[192,384]{1,0:T(8,128)(2,1)}, bf1...) custom-call(bf16[1024,384]{1,0:T(8,128)(2,1)} %bitcast.13, ...), custom_call_target="tpu_custom_call" | custom-call | tf_op jit(solution)/shard_map/pallas_call | solution.py:1201
  297.4 5.5 %shard_map.178 = (f32[192,1728]{1,0:T(8,128)}, f32[192,1728]{1,0:T(8,128)}, f32[192,1728]{1,0:T(8,128)}, f32[192,384]{1,0:T(8,128)}, f32[3,192,384]{2,1,0:T(8,12...) custom-call(bf16[192,1728]{1,0:T(8,128)(2,1)} %get-tuple-element.28., ...), custom_call_target="tpu_custom_call" | custom-call | tf_op jit(solution)/shard_map/pallas_call | solution.py:1277

commit v8 on v7

--- a/solution.py
+++ b/solution.py
@@ -285,11 +285,10 @@
         on_size(t, f)
 
     def zs_at(t, step):
-        return 2 * step + lax.rem(t, 2)
+        return sum(k + 2 for k in range(step)) + lax.rem(t, step + 2)
 
     def zr_at(t, step):
-        count = 3 if 0 < step < last - 1 else 4
-        return 3 * step + min(step, 1) + lax.rem(t, count)
+        return 4 * step + lax.rem(t, 6 if step == last - 1 else 4)
 
     def z_do(t, way, step, what):
         def f(cols):
@@ -324,27 +323,30 @@
 
     def z_step(t, step):
         sl = lax.rem(t, LAG + 4)
-        if step > 0:
-            z_arrived(t, step - 1)
+
+        def quarter(way, k):
+            at = z - last + k if way else last - k + z
+            return s_buf[sl, pl.ds(at * ROWS, ROWS), :]
+
+        if step == 0:
+            for way, end in ((0, 0), (1, last)):
+                @pl.when(z == end)
+                def _(way=way):
+                    for k in range(last):
+                        zs[way, zs_at(t, k)] = quarter(way, k)
+                        z_do(t, way, k, "start")
+
+            return
+        z_arrived(t, step - 1)
+        onward = [jnp.logical_and(receives(way, step - 1), can_send(way, step)) for way in (0, 1)]
         for way in (0, 1):
-            quarter = z - last + step if way else last - step + z
-            fresh = can_send(way, step)
-            if step > 0:
-                @pl.when(jnp.logical_and(receives(way, step - 1), can_send(way, step)))
-                def _(way=way, quarter=quarter):
-                    value = s_buf[sl, pl.ds(quarter * ROWS, ROWS), :].astype(F32) + zr[
-                        way, zr_at(t, step - 1)
-                    ].astype(F32)
-                    zs[way, zs_at(t, step)] = value.astype(BF)
-
-                fresh = jnp.logical_and(fresh, jnp.logical_not(receives(way, step - 1)))
-
-            @pl.when(fresh)
-            def _(way=way, quarter=quarter):
-                zs[way, zs_at(t, step)] = s_buf[sl, pl.ds(quarter * ROWS, ROWS), :]
+            @pl.when(onward[way])
+            def _(way=way):
+                value = quarter(way, step).astype(F32) + zr[way, zr_at(t, step - 1)].astype(F32)
+                zs[way, zs_at(t, step)] = value.astype(BF)
 
         for way in (0, 1):
-            @pl.when(can_send(way, step))
+            @pl.when(onward[way])
             def _(way=way):
                 z_do(t, way, step, "start")
 
@@ -1168,8 +1170,8 @@
         pltpu.VMEM((3, m, ff), BF),
         pltpu.VMEM((5, m, ff), BF),
         pltpu.VMEM((LAG + 4, m, ff), BF),
-        pltpu.VMEM((2, 2 * last, ROWS, ff), BF),
-        pltpu.VMEM((2, 3 * last + 2, ROWS, ff), BF),
+        pltpu.VMEM((2, last * (last + 3) // 2, ROWS, ff), BF),
+        pltpu.VMEM((2, 4 * last + 2, ROWS, ff), BF),
         pltpu.VMEM((3, ROWS, ff), BF),
         pltpu.VMEM((ROWS, ff), BF),
         pltpu.VMEM((ROWS, ff), BF),
@@ -1193,7 +1195,7 @@
         pltpu.VMEM((chunks, 8, local), F32),
         pltpu.VMEM((chunks, 8, local), F32),
         pltpu.VMEM((5, 8, local), F32),
-        DMA((3,)), DMA((5,)), DMA((2, 2 * last)), DMA((2, 3 * last + 2)), DMA((3, 4)),
+        DMA((3,)), DMA((5,)), DMA((2, last * (last + 3) // 2)), DMA((2, 4 * last + 2)), DMA((3, 4)),
         DMA((2, 2)), DMA((2, chunks)), DMA((2, 2)), DMA((2, 2)), DMA((2, 2)),
         DMA((2, 2)), DMA((2, 2)), DMA((2, chunks)), DMA((2, chunks)), DMA((3, 2, 4, chunks)),
         DMA((7,)), DMA((4, 4)), DMA(()), DMA((2, 2)), DMA(()), DMA((3, 2)), DMA((2,)), DMA((2,)), DMA((2, nseq)), DMA((2, 2, last)), DMA((2, 4)), DMA((4,)),
@@ -1254,12 +1256,13 @@
         pltpu.make_async_copy(wide[k] if k < count - 2 else narrow[k], dst[k], out_sem.at[k])
         for k in range(count)
     ]
-    for one in loads:
-        one.start()
+    order = (*range(count - 2, count), *range(count - 2))
+    for k in order:
+        loads[k].start()
     gmix[...] = small[0:1, :].reshape(gmix.shape)
     gtaps[...] = small[1:4, :]
     gff[...] = small[4:5, :].reshape(gff.shape)
-    for k in range(count):
+    for k in order:
         loads[k].wait()
         if k < count - 2:
             wide[k][...] = narrow[k][...].astype(F32)

time: 303 us -> 301 us (level)
  no operation moved by 1% of the time
where the time goes in v8:
time: 301 us
  Pallas kernels  300 us (100%)
    pallas_call x1, Pallas kernels, block(): pl.pallas_call(functools.partial(block_kernel, dims), out_shape=(shape((r...  295 us

profile of v8, /device:TPU:0, one launch (start us, length us, event | category | flops | bytes accessed | tf_op | source)
XLA Modules:
  0.0 300.9 jit_solution(17322293283922640028)
XLA Ops:
  0.6 294.6 %shard_map.177 = (bf16[192,1728]{1,0:T(8,128)(2,1)}, bf16[192,1728]{1,0:T(8,128)(2,1)}, bf16[192,1728]{1,0:T(8,128)(2,1)}, bf16[192,384]{1,0:T(8,128)(2,1)}, bf1...) custom-call(bf16[1024,384]{1,0:T(8,128)(2,1)} %bitcast.13, ...), custom_call_target="tpu_custom_call" | custom-call | tf_op jit(solution)/shard_map/pallas_call | solution.py:1203
  295.3 5.4 %shard_map.178 = (f32[192,1728]{1,0:T(8,128)}, f32[192,1728]{1,0:T(8,128)}, f32[192,1728]{1,0:T(8,128)}, f32[192,384]{1,0:T(8,128)}, f32[3,192,384]{2,1,0:T(8,12...) custom-call(bf16[192,1728]{1,0:T(8,128)(2,1)} %get-tuple-element.28., ...), custom_call_target="tpu_custom_call" | custom-call | tf_op jit(solution)/shard_map/pallas_call | solution.py:1280

commit v9 on v8

--- a/solution.py
+++ b/solution.py
@@ -91,7 +91,7 @@
     wg_load = load(wg_h, wg, w_sem.at[4])
     wu_load = load(wu_h, wu, w_sem.at[5])
     def wo_load(q):
-        return load(wo_h.at[:, pl.ds(q * local, local)], wof.at[0, pl.ds(q * local, local), :], wl_sem.at[q])
+        return load(wo_h.at[:, pl.ds(q * local, local)], wof.at[pl.ds(q * local, local), pl.ds(0, local)], wl_sem.at[q])
 
     for k in range(3):
         wi_load(k).start()
@@ -171,9 +171,9 @@
         rows = pl.ds(pl.multiple_of(q * local, 128), local)
         for pair in (0, 1):
             cols = pl.ds(pl.multiple_of((2 * pair + c) * local, 128), local)
-            yield load(src.at[:, cols], wof.at[pair, rows, :], wl_sem.at[2 * kind + pair])
+            yield load(src.at[:, cols], wof.at[rows, pl.ds(pair * local, local)], wl_sem.at[2 * kind + pair])
             cols = pl.ds(pl.multiple_of((2 * pair + 1 - c) * local, 128), local)
-            yield remote(src.at[:, cols], wof.at[pair, rows, :], wc_sem, c_dev, 2 * kind + pair)
+            yield remote(src.at[:, cols], wof.at[rows, pl.ds(pair * local, local)], wc_sem, c_dev, 2 * kind + pair)
 
     def wo_end():
         wy().wait_send()
@@ -233,10 +233,6 @@
     gather_start(2, 0)
     for i in range(chunks):
         gather(0, i, 1).start()
-    for one in wo_columns(wo_h, me, 0):
-        one.start()
-    wg_load.start()
-    wu_load.start()
 
     def on_size(t, f):
         pl.when(t // beat < 3)(lambda: f(pl.ds(0, ff)))
@@ -624,8 +620,9 @@
                 for core in (0, 1):
                     h1_store(i - 1, 1 - slot, pair, core).wait()
 
+        product = nn(r[0, rows_at(i), pl.ds(0, width)], wof[...])
         for pair in (0, 1):
-            h1 = nn(r[0, rows_at(i), pl.ds(0, width)], wof[pair]) + cs2[pair].astype(F32)
+            h1 = product[:, pair * local : (pair + 1) * local] + cs2[pair].astype(F32)
             da2f[slot, pair, c] = h1.astype(BF)
 
             @pl.when(y == pair)
@@ -810,7 +807,7 @@
         dmixed = jnp.zeros((chunk, local), F32)
         for q in range(4):
             cols = pl.ds(q * local, local)
-            dmixed += nt(dhoc[:, cols], wof[0, cols, :])
+            dmixed += nt(dhoc[:, cols], wof[cols, pl.ds(0, local)])
         c_gate = bcv[1]
         bxp[pl.ds(0, 8), :] = before_r[i]
         bxp[pl.ds(8, chunk), :] = bcv[3].astype(F32)
@@ -980,7 +977,7 @@
         when(j < chunks, lambda: project(j))
         when(j + 1 < chunks, lambda: gather_pass(0, j + 1))
         when(j + 2 < chunks, lambda: gather(0, j + 2, 0).start())
-        when(j == 0, lambda: wo_step(0))
+        when(j == 0, lambda: wo_step(0), wg_load.start, wu_load.start, *[one.start for one in wo_columns(wo_h, me, 0)])
         when(j == 1, lambda: wo_step(1))
         when(j == 2, lambda: wo_step(3))
         when(j == 3, wo_there, weights_there)
@@ -1154,7 +1151,7 @@
         pltpu.VMEM((ff, width), BF),
         pltpu.VMEM((ff, width), BF),
         pltpu.VMEM((ff, width), BF),
-        pltpu.VMEM((2, width, local), BF),
+        pltpu.VMEM((width, 2 * local), BF),
         pltpu.VMEM((chunk, width), BF),
         pltpu.VMEM((4, chunk, local), BF),
         pltpu.VMEM((chunk, local), BF),

time: 301 us -> 301 us (level)
  no operation moved by 1% of the time
where the time goes in v9:
time: 301 us
  Pallas kernels  300 us (100%)
    pallas_call x1, Pallas kernels, block(): pl.pallas_call(functools.partial(block_kernel, dims), out_shape=(shape((r...  294 us

profile of v9, /device:TPU:0, one launch (start us, length us, event | category | flops | bytes accessed | tf_op | source)
XLA Modules:
  0.0 300.7 jit_solution(5248909387487498773)
XLA Ops:
  0.6 294.4 %shard_map.177 = (bf16[192,1728]{1,0:T(8,128)(2,1)}, bf16[192,1728]{1,0:T(8,128)(2,1)}, bf16[192,1728]{1,0:T(8,128)(2,1)}, bf16[192,384]{1,0:T(8,128)(2,1)}, bf1...) custom-call(bf16[1024,384]{1,0:T(8,128)(2,1)} %bitcast.13, ...), custom_call_target="tpu_custom_call" | custom-call | tf_op jit(solution)/shard_map/pallas_call | solution.py:1200
  295.1 5.4 %shard_map.178 = (f32[192,1728]{1,0:T(8,128)}, f32[192,1728]{1,0:T(8,128)}, f32[192,1728]{1,0:T(8,128)}, f32[192,384]{1,0:T(8,128)}, f32[3,192,384]{2,1,0:T(8,12...) custom-call(bf16[192,1728]{1,0:T(8,128)(2,1)} %get-tuple-element.28., ...), custom_call_target="tpu_custom_call" | custom-call | tf_op jit(solution)/shard_map/pallas_call | solution.py:1277
